TPU v7x, 32 devices: a whole 2x2x4 slice. The times are simulated.
32 devices in a mesh: dp: 8 (over y, x, core), tensor: 4 (over z).
Axes of the slice: x: 2, y: 2, z: 4, core: 2. Of those that a mesh axis runs over, the one named last changes fastest.
Arguments:
- tokens: bfloat16 [16384, 1024], P(('dp', 'tensor')), may hold values from -6 to 6
- qkv_weight: bfloat16 [1024, 3, 1024], P('dp', None, 'tensor'), may hold values from -0.1875 to 0.1875
- out_weight: bfloat16 [1024, 1024], P('tensor', 'dp'), may hold values from -3.5 to 3.5
- up_weight: bfloat16 [1024, 4096], P('dp', 'tensor'), may hold values from -0.1875 to 0.1875
- down_weight: bfloat16 [4096, 1024], P('tensor', 'dp'), may hold values from -0.09375 to 0.09375
- mid_gain: float32 [1024], P(('dp', 'tensor')), may hold values from 0.5 to 1.5
- mid_shift: float32 [1024], P(('dp', 'tensor')), may hold values from -3 to 3
- query_bias: float32 [1024], P(('dp', 'tensor')), may hold values from -6 to 6
- value_bias: float32 [1024], P(('dp', 'tensor')), may hold values from -0.75 to 0.75
- out_bias: float32 [1024], P(('dp', 'tensor')), may hold values from -3 to 3
- end_gain: float32 [1024], P(('dp', 'tensor')), may hold values from 0.5 to 1.5
- end_shift: float32 [1024], P(('dp', 'tensor')), may hold values from -3 to 3
- up_bias: float32 [4096], P(('dp', 'tensor')), may hold values from -6 to 6
- down_bias: float32 [1024], P(('dp', 'tensor')), may hold values from -3 to 3
- cotangent: bfloat16 [16384, 1024], P(('dp', 'tensor')), may hold values from -6 to 6
Outputs:
- encoded: bfloat16 [16384, 1024], P(('dp', 'tensor'))
- tokens_grad: float32 [16384, 1024], P(('dp', 'tensor'))
- qkv_grad: float32 [1024, 3, 1024], P('dp', None, 'tensor')
- out_grad: float32 [1024, 1024], P('tensor', 'dp')
- up_grad: float32 [1024, 4096], P('dp', 'tensor')
- down_grad: float32 [4096, 1024], P('tensor', 'dp')
- mid_gain_grad: float32 [1024], P(('dp', 'tensor'))
- mid_shift_grad: float32 [1024], P(('dp', 'tensor'))
- query_bias_grad: float32 [1024], P(('dp', 'tensor'))
- value_bias_grad: float32 [1024], P(('dp', 'tensor'))
- out_bias_grad: float32 [1024], P(('dp', 'tensor'))
- end_gain_grad: float32 [1024], P(('dp', 'tensor'))
- end_shift_grad: float32 [1024], P(('dp', 'tensor'))
- up_bias_grad: float32 [4096], P(('dp', 'tensor'))
- down_bias_grad: float32 [1024], P(('dp', 'tensor'))
All inputs are finite; a program needn't handle non-finite values.
Results may differ from a plain program's by a relative error of at most 0.02.
Values may be sent and summed in bfloat16 or wider, within the bound.
No kernel may reach another device: no remote copies, remote signals or barrier semaphores. Data moves between devices by JAX's collectives and lax.ppermute only.
A program may use at most 128 MiB of HBM per device.

v0:
```python
import jax
import jax.numpy as jnp
from jax import lax
from jax.sharding import PartitionSpec as P

HD = 64
LEN = 1024


norm_epsilon = 1e-05
block_limit = 512


def normalize(values_in, gain, shift):
    average = jnp.mean(values_in, axis=-1, keepdims=True)
    centred = values_in - average
    variance = jnp.mean(centred * centred, axis=-1, keepdims=True)
    return centred * lax.rsqrt(variance + norm_epsilon) * gain + shift


def gelu_exact(values_in):
    return jax.nn.gelu(values_in, approximate=False)


def spread_out(part_sum, full_size, member):
    return lax.dynamic_update_slice_in_dim(
        jnp.zeros((full_size,), jnp.float32), part_sum, member * part_sum.shape[0], 0
    )


def on_device(
    tokens,
    qkv_weight,
    out_weight,
    up_weight,
    down_weight,
    mid_gain,
    mid_shift,
    query_bias,
    value_bias,
    out_bias,
    end_gain,
    end_shift,
    up_bias,
    down_bias,
    cotangent,
):
    member = lax.axis_index("tensor")
    qkv_full, out_full, up_full, down_full = (
        lax.all_gather(qkv_weight, "dp", axis=0, tiled=True),
        lax.all_gather(out_weight, "dp", axis=1, tiled=True),
        lax.all_gather(up_weight, "dp", axis=0, tiled=True),
        lax.all_gather(down_weight, "dp", axis=1, tiled=True),
    )
    vector_full = (
        lax.all_gather(mid_gain, ("dp", "tensor"), axis=0, tiled=True),
        lax.all_gather(mid_shift, ("dp", "tensor"), axis=0, tiled=True),
        lax.all_gather(query_bias, ("dp", "tensor"), axis=0, tiled=True),
        lax.all_gather(value_bias, ("dp", "tensor"), axis=0, tiled=True),
        lax.all_gather(out_bias, ("dp", "tensor"), axis=0, tiled=True),
        lax.all_gather(end_gain, ("dp", "tensor"), axis=0, tiled=True),
        lax.all_gather(end_shift, ("dp", "tensor"), axis=0, tiled=True),
        lax.all_gather(up_bias, ("dp", "tensor"), axis=0, tiled=True),
        lax.all_gather(down_bias, ("dp", "tensor"), axis=0, tiled=True),
    )
    (
        gain_mid,
        shift_mid,
        bias_query,
        bias_value,
        bias_out,
        gain_end,
        shift_end,
        bias_up_whole,
        bias_down,
    ) = vector_full
    local_width = out_full.shape[0]
    model_width = out_full.shape[1]
    hidden_width = up_full.shape[1]
    head_count = local_width // HD
    bias_query = lax.dynamic_slice_in_dim(bias_query, member * local_width, local_width)
    bias_value = lax.dynamic_slice_in_dim(bias_value, member * local_width, local_width)
    bias_up = lax.dynamic_slice_in_dim(bias_up_whole, member * hidden_width, hidden_width)
    score_scale = HD ** (-0.5)
    seen_rows = lax.all_gather(tokens, "tensor", axis=0, tiled=True)
    group_rows = seen_rows.shape[0]
    qkv_rows = jnp.dot(
        seen_rows,
        qkv_full.reshape(model_width, 3 * local_width),
        preferred_element_type=jnp.float32,
    ).reshape(group_rows, 3, local_width)
    queries = (qkv_rows[:, 0] + bias_query).astype(jnp.bfloat16)
    key_rows = qkv_rows[:, 1].astype(jnp.bfloat16)
    value_rows = (qkv_rows[:, 2] + bias_value).astype(jnp.bfloat16)
    block_rows = min(block_limit, LEN)
    per_seq = LEN // block_rows
    seq_count = group_rows // LEN

    def forward_block(block_index):
        first_row = block_index // per_seq * LEN
        query_part = lax.dynamic_slice_in_dim(
            queries, block_index * block_rows, block_rows
        ).reshape(block_rows, head_count, HD)
        key_part = lax.dynamic_slice_in_dim(key_rows, first_row, LEN).reshape(LEN, head_count, HD)
        value_part = lax.dynamic_slice_in_dim(value_rows, first_row, LEN).reshape(
            LEN, head_count, HD
        )
        scores = (
            jnp.einsum("qhd,khd->hqk", query_part, key_part, preferred_element_type=jnp.float32)
            * score_scale
        )
        largest = jnp.max(scores, axis=-1, keepdims=True)
        weights = jnp.exp(scores - largest)
        totals = jnp.sum(weights, axis=-1, keepdims=True)
        softmax = (weights / totals).astype(jnp.bfloat16)
        context = jnp.einsum(
            "hqk,khd->qhd", softmax, value_part, preferred_element_type=jnp.float32
        )
        return (context.reshape(block_rows, local_width), largest + jnp.log(totals))

    context, log_sums = lax.map(forward_block, jnp.arange(group_rows // block_rows))
    context_low = context.reshape(group_rows, local_width).astype(jnp.bfloat16)
    branch = lax.psum_scatter(
        jnp.dot(context_low, out_full, preferred_element_type=jnp.float32).astype(jnp.bfloat16),
        "tensor",
        scatter_dimension=0,
        tiled=True,
    ).astype(jnp.float32)
    middle, mid_pull = jax.vjp(
        normalize, tokens.astype(jnp.float32) + branch + bias_out, gain_mid, shift_mid
    )
    middle_low = middle.astype(jnp.bfloat16)
    seen_middle = lax.all_gather(middle_low, "tensor", axis=0, tiled=True)
    pre_act = jnp.dot(seen_middle, up_full, preferred_element_type=jnp.float32) + bias_up
    activated, gelu_pull = jax.vjp(gelu_exact, pre_act)
    hidden_low = activated.astype(jnp.bfloat16)
    branch_two = lax.psum_scatter(
        jnp.dot(hidden_low, down_full, preferred_element_type=jnp.float32).astype(jnp.bfloat16),
        "tensor",
        scatter_dimension=0,
        tiled=True,
    ).astype(jnp.float32)
    result, end_pull = jax.vjp(normalize, middle + branch_two + bias_down, gain_end, shift_end)
    encoded = result.astype(jnp.bfloat16)
    qkv_back, out_back, up_back, down_back = (
        lax.all_gather(qkv_weight, "dp", axis=0, tiled=True),
        lax.all_gather(out_weight, "dp", axis=1, tiled=True),
        lax.all_gather(up_weight, "dp", axis=0, tiled=True),
        lax.all_gather(down_weight, "dp", axis=1, tiled=True),
    )
    second_grad, endgain_part, endshift_part = end_pull(cotangent.astype(jnp.float32))
    downbias_part = jnp.sum(second_grad, axis=0)
    portion = lax.all_gather(second_grad.astype(jnp.bfloat16), "tensor", axis=0, tiled=True)
    rows_here = hidden_low
    weight_sum = jnp.einsum("rf,rd->fd", rows_here, portion, preferred_element_type=jnp.float32)
    hidden_back = jnp.einsum("rd,fd->rf", portion, down_back, preferred_element_type=jnp.float32)
    down_sum, hidden_back = (weight_sum, hidden_back)
    pre_low = gelu_pull(hidden_back)[0].astype(jnp.bfloat16)
    upbias_vector = spread_out(
        jnp.sum(pre_low.astype(jnp.float32), axis=0), hidden_width * lax.axis_size("tensor"), member
    )
    up_sum = jnp.einsum("rd,rf->df", seen_middle, pre_low, preferred_element_type=jnp.float32)
    middle_grad = (
        lax.psum_scatter(
            jnp.einsum("rf,df->rd", pre_low, up_back, preferred_element_type=jnp.float32).astype(
                jnp.bfloat16
            ),
            "tensor",
            scatter_dimension=0,
            tiled=True,
        ).astype(jnp.float32)
        + second_grad
    )
    first_grad, midgain_part, midshift_part = mid_pull(middle_grad)
    outbias_part = jnp.sum(first_grad, axis=0)
    portion = lax.all_gather(first_grad.astype(jnp.bfloat16), "tensor", axis=0, tiled=True)
    rows_here = context_low
    weight_sum = jnp.einsum("rl,rd->ld", rows_here, portion, preferred_element_type=jnp.float32)
    context_back = jnp.einsum("rd,ld->rl", portion, out_back, preferred_element_type=jnp.float32)
    out_sum, context_back = (weight_sum, context_back)
    context_grad = context_back.astype(jnp.bfloat16)

    def sequence_back(seq_index):
        first_row = seq_index * LEN
        key_part = lax.dynamic_slice_in_dim(key_rows, first_row, LEN).reshape(LEN, head_count, HD)
        value_part = lax.dynamic_slice_in_dim(value_rows, first_row, LEN).reshape(
            LEN, head_count, HD
        )

        def block_back(running, inner_step):
            key_sum, value_sum = running
            block_index = seq_index * per_seq + inner_step
            offset = block_index * block_rows
            query_part = lax.dynamic_slice_in_dim(queries, offset, block_rows).reshape(
                block_rows, head_count, HD
            )
            grad_part = lax.dynamic_slice_in_dim(context_grad, offset, block_rows).reshape(
                block_rows, head_count, HD
            )
            scores = (
                jnp.einsum("qhd,khd->hqk", query_part, key_part, preferred_element_type=jnp.float32)
                * score_scale
            )
            softmax = jnp.exp(scores - log_sums[block_index])
            value_sum = value_sum + jnp.einsum(
                "hqk,qhd->khd",
                softmax.astype(jnp.bfloat16),
                grad_part,
                preferred_element_type=jnp.float32,
            )
            prob_grad = jnp.einsum(
                "qhd,khd->hqk", grad_part, value_part, preferred_element_type=jnp.float32
            )
            inner_sum = jnp.sum(prob_grad * softmax, axis=-1, keepdims=True)
            score_low = (softmax * (prob_grad - inner_sum)).astype(jnp.bfloat16)
            query_back = (
                jnp.einsum("hqk,khd->qhd", score_low, key_part, preferred_element_type=jnp.float32)
                * score_scale
            )
            key_sum = (
                key_sum
                + jnp.einsum(
                    "hqk,qhd->khd", score_low, query_part, preferred_element_type=jnp.float32
                )
                * score_scale
            )
            return ((key_sum, value_sum), query_back.reshape(block_rows, local_width))

        zero_part = jnp.zeros((LEN, head_count, HD), jnp.float32)
        (key_sum, value_sum), query_back = lax.scan(
            block_back, (zero_part, zero_part), jnp.arange(per_seq)
        )
        return (
            query_back.reshape(LEN, local_width),
            key_sum.reshape(LEN, local_width),
            value_sum.reshape(LEN, local_width),
        )

    query_grad, key_grad, value_grad = lax.map(sequence_back, jnp.arange(seq_count))
    qkv_low = jnp.stack(
        (
            query_grad.reshape(group_rows, local_width),
            key_grad.reshape(group_rows, local_width),
            value_grad.reshape(group_rows, local_width),
        ),
        axis=1,
    ).astype(jnp.bfloat16)
    querybias_part = jnp.sum(qkv_low[:, 0].astype(jnp.float32), axis=0)
    valuebias_part = jnp.sum(qkv_low[:, 2].astype(jnp.float32), axis=0)
    qkv_sum = jnp.einsum("rd,rcl->dcl", seen_rows, qkv_low, preferred_element_type=jnp.float32)
    input_grad = (
        lax.psum_scatter(
            jnp.einsum("rcl,dcl->rd", qkv_low, qkv_back, preferred_element_type=jnp.float32).astype(
                jnp.bfloat16
            ),
            "tensor",
            scatter_dimension=0,
            tiled=True,
        ).astype(jnp.float32)
        + first_grad
    )
    qkv_part, out_part, up_part, down_part = (
        lax.psum_scatter(qkv_sum, "dp", scatter_dimension=0, tiled=True),
        lax.psum_scatter(out_sum, "dp", scatter_dimension=1, tiled=True),
        lax.psum_scatter(up_sum, "dp", scatter_dimension=0, tiled=True),
        lax.psum_scatter(down_sum, "dp", scatter_dimension=1, tiled=True),
    )
    vector_parts = (
        lax.psum_scatter(midgain_part, ("dp", "tensor"), scatter_dimension=0, tiled=True),
        lax.psum_scatter(midshift_part, ("dp", "tensor"), scatter_dimension=0, tiled=True),
        lax.psum_scatter(
            spread_out(querybias_part, model_width, member),
            ("dp", "tensor"),
            scatter_dimension=0,
            tiled=True,
        ),
        lax.psum_scatter(
            spread_out(valuebias_part, model_width, member),
            ("dp", "tensor"),
            scatter_dimension=0,
            tiled=True,
        ),
        lax.psum_scatter(outbias_part, ("dp", "tensor"), scatter_dimension=0, tiled=True),
        lax.psum_scatter(endgain_part, ("dp", "tensor"), scatter_dimension=0, tiled=True),
        lax.psum_scatter(endshift_part, ("dp", "tensor"), scatter_dimension=0, tiled=True),
        lax.psum_scatter(upbias_vector, ("dp", "tensor"), scatter_dimension=0, tiled=True),
        lax.psum_scatter(downbias_part, ("dp", "tensor"), scatter_dimension=0, tiled=True),
    )
    return (
        encoded,
        input_grad,
        qkv_part,
        out_part,
        up_part,
        down_part,
        vector_parts[0],
        vector_parts[1],
        vector_parts[2],
        vector_parts[3],
        vector_parts[4],
        vector_parts[5],
        vector_parts[6],
        vector_parts[7],
        vector_parts[8],
    )


def solution(mesh):
    in_specs = (
        P(("dp", "tensor"), None),
        P("dp", None, "tensor"),
        P("tensor", "dp"),
        P("dp", "tensor"),
        P("tensor", "dp"),
        P(("dp", "tensor")),
        P(("dp", "tensor")),
        P(("dp", "tensor")),
        P(("dp", "tensor")),
        P(("dp", "tensor")),
        P(("dp", "tensor")),
        P(("dp", "tensor")),
        P(("dp", "tensor")),
        P(("dp", "tensor")),
        P(("dp", "tensor"), None),
    )
    out_specs = (
        P(("dp", "tensor"), None),
        P(("dp", "tensor"), None),
        P("dp", None, "tensor"),
        P("tensor", "dp"),
        P("dp", "tensor"),
        P("tensor", "dp"),
        P(("dp", "tensor")),
        P(("dp", "tensor")),
        P(("dp", "tensor")),
        P(("dp", "tensor")),
        P(("dp", "tensor")),
        P(("dp", "tensor")),
        P(("dp", "tensor")),
        P(("dp", "tensor")),
        P(("dp", "tensor")),
    )
    return jax.shard_map(
        on_device, mesh=mesh, in_specs=in_specs, out_specs=out_specs, check_vma=False
    )
```

profile of v0, /device:TPU:0, one launch (start us, length us, event | category | flops | bytes accessed | tf_op | source)
XLA Modules:
  0.0 1193.2 jit_solution(16281610830170294732)
XLA Ops:
  14.6 42.9 %all-reduce.18 = (f32[1024]{0:T(1024)S(1)}, f32[1024]{0:T(1024)S(1)}, f32[1024]{0:T(1024)S(1)}, f32[1024]{0:T(1024)S(1)}, f32[1024]{0:T(1024)S(1)}, /*index=5*/f32[1024]{0:T(1024)}, f32[1024]{0:T(1024)}) all-reduce(f32[1024]{0:T(1024)S(1)} %dynamic-update-slice.4, ...), channel_id=1, replica_groups=mesh['dp'=8,'tensor'=4] {'dp','tensor'}, use_global_device_ids=true, to_apply=%add.4 | all-reduce | flops 7168 | bytes 57344
  57.6 11.7 all_gather.59
  71.1 50.0 %all-gather.9.cloned.1.call-done = bf16[2048,1024]{1,0:T(8,128)(2,1)} async-done(((bf16[512,1024]{1,0:T(8,128)(2,1)}), bf16[2048,1024]{1,0:T(8,128)(2,1)}) %all-gather.9.cloned.1.call-update) | async-done | bytes 4194320 | tf_op jit(solution)/shard_map/all_gather | solution.py:85
  121.0 5.3 fusion.25
  131.1 49.8 %while.45 = (s32[]{:T(128)}, bf16[4,512,256]{2,1,0:T(8,128)(2,1)S(1)}, f32[4,4,512,1]{2,1,3,0:T(4,128)}, s32[4]{0:T(128)S(1)}, bf16[2048,256]{0,1:T(8,128)(2,1)}...) while((s32[]{:T(128)}, ...), condition=%wide.region_3.4_spmd, body=%wide.region_0.3_spmd.sunk | while | flops 555743232 | bytes 30475144 | solution.py:121
  185.0 74.6 %reduce-scatter.9.cloned.1.call-done = bf16[512,1024]{1,0:T(8,128)(2,1)} async-done(((bf16[2048,1024]{1,0:T(8,128)(2,1)}), bf16[512,1024]{1,0:T(8,128)(2,1)}) %reduce-scatter.9.cloned.1.call-update) | async-done | bytes 1048592 | tf_op jit(solution)/shard_map/reduce_scatter | solution.py:123
  265.4 67.7 %all-gather = f32[32,1,128]{2,1,0:T(1,128)S(1)} all-gather(f32[1,1,128]{2,1,0:T(1,128)S(1)} %bitcast.192), channel_id=1, replica_groups=mesh['dp'=8,'tensor'=4] {'dp','tensor'}, dimensions={0}, use_global_device_ids=true | all-gather | bytes 16896 | tf_op jit(solution)/shard_map/all_gather | solution.py:63
  333.1 39.8 %all-gather.13.cloned.1.call-done = bf16[2048,1024]{1,0:T(8,128)(2,1)} async-done(((bf16[512,1024]{1,0:T(8,128)(2,1)}), bf16[2048,1024]{1,0:T(8,128)(2,1)}) %all-gather.13.cloned.1.call-update) | async-done | bytes 4194320 | tf_op jit(solution)/shard_map/all_gather | solution.py:133
  372.9 26.3 %multiply_convert_fusion.1 = (bf16[2048,1024]{1,0:T(8,128)(2,1)}, f32[2048,1024]{1,0:T(8,128)}, f32[2048,1024]{1,0:T(8,128)}) fusion(f32[1024]{0:T(1024)S(1)} %dynamic_slice.66, bf16[2048,1024]{1,0:T(8,128)(2,1)} %all-gather.13.cloned.1.call-done, bf16[1024,1024]{1,0:T(8,128)(2,1)} %all-gather.15.cloned.1.call-done), kind=kOutput, calls=%fused_computation.39 | convolution fusion | flops 4433379328 | bytes 27267072 | tf_op jit(solution)/shard_map/dot_general | solution.py:134
  401.6 9.3 convolution_convert_fusion.2
  411.4 76.4 %reduce-scatter.11.cloned.1.call-done = bf16[512,1024]{1,0:T(8,128)(2,1)} async-done(((bf16[2048,1024]{1,0:T(8,128)(2,1)}), bf16[512,1024]{1,0:T(8,128)(2,1)}) %reduce-scatter.11.cloned.1.call-update) | async-done | bytes 1048592 | tf_op jit(solution)/shard_map/reduce_scatter | solution.py:137
  495.2 81.4 %all-gather.19.cloned.1.call-done = bf16[2048,1024]{1,0:T(8,128)(2,1)} async-done(((bf16[512,1024]{1,0:T(8,128)(2,1)}), bf16[2048,1024]{1,0:T(8,128)(2,1)}) %all-gather.19.cloned.1.call-update) | async-done | bytes 4194320 | tf_op jit(solution)/shard_map/all_gather | solution.py:153
  576.6 14.0 %convert_reduce_fusion = (f32[1024]{0:T(1024)}, bf16[2048,1024]{1,0:T(8,128)(2,1)S(1)}) fusion(f32[2048,1024]{1,0:T(8,128)} %get-tuple-element.515, f32[2048,1024]{1,0:T(8,128)} %get-tuple-element.530, f32[1024]{0:T(1024)S(1)} %dynamic_slice.66, bf16[2048,1024]{1,0:T(8,128)(2,1)} %all-gather.19.cloned.1.call-done, ...), kind=kOutput, calls=%fused_computation.37 | convolution fusion | flops 4330617856 | bytes 27271168 | tf_op jit(solution)/shard_map/rd,fd->rf/dot_general | solution.py:156
  592.6 6.3 convolution_convert_fusion.1
  599.0 75.4 %reduce-scatter.13.cloned.1.call-done = bf16[512,1024]{1,0:T(8,128)(2,1)} async-done(((bf16[2048,1024]{1,0:T(8,128)(2,1)}), bf16[512,1024]{1,0:T(8,128)(2,1)}) %reduce-scatter.13.cloned.1.call-update) | async-done | bytes 1048592 | tf_op jit(solution)/shard_map/reduce_scatter | solution.py:164
  682.3 81.2 %all-gather.21.cloned.1.call-done = bf16[2048,1024]{1,0:T(8,128)(2,1)} async-done(((bf16[512,1024]{1,0:T(8,128)(2,1)}), bf16[2048,1024]{1,0:T(8,128)(2,1)}) %all-gather.21.cloned.1.call-update) | async-done | bytes 4194320 | tf_op jit(solution)/shard_map/all_gather | solution.py:176
  768.4 130.6 %while.47 = (s32[]{:T(128)}, bf16[2,1024,256]{2,1,0:T(8,128)(2,1)}, bf16[2,1024,256]{1,2,0:T(8,128)(2,1)}, bf16[2,1024,256]{1,2,0:T(8,128)(2,1)}, s32[2]{0:T(128...) while((s32[]{:T(128)}, bf16[2,1024,256]{2,1,0:T(8,128)(2,1)}, ...), condition=%wide.region_19.20_spmd, body=%wide.region_15.19_spmd.sunk | while | flops 1368913920 | bytes 123529472 | solution.py:239
  773.3 58.4 %while.48 = (s32[]{:T(128)}, f32[1024,4,64]{0,2,1:T(8,128)S(1)}, f32[1024,4,64]{0,2,1:T(8,128)S(1)}, bf16[2,512,256]{2,1,0:T(8,128)(2,1)}, s32[2]{0:T(128)S(1)},...) while((s32[]{:T(128)}, f32[1024,4,64]{0,2,1:T(8,128)S(1)}, ...), condition=%wide.region_18.18_spmd.clone, body=%wide.region_16.17_spmd.clone.sunk | while | flops 1368913920 | bytes 114090840 | solution.py:230
  780.9 5.2 multiply_reduce_fusion.9
  810.0 5.2 multiply_reduce_fusion.9
  838.6 58.4 %while.48 = (s32[]{:T(128)}, f32[1024,4,64]{0,2,1:T(8,128)S(1)}, f32[1024,4,64]{0,2,1:T(8,128)S(1)}, bf16[2,512,256]{2,1,0:T(8,128)(2,1)}, s32[2]{0:T(128)S(1)},...) while((s32[]{:T(128)}, f32[1024,4,64]{0,2,1:T(8,128)S(1)}, ...), condition=%wide.region_18.18_spmd.clone, body=%wide.region_16.17_spmd.clone.sunk | while | flops 1368913920 | bytes 114090840 | solution.py:230
  846.1 5.2 multiply_reduce_fusion.9
  875.3 5.2 multiply_reduce_fusion.9
  902.8 8.1 fusion.35
  911.1 6.7 bitcast_convert_fusion
  917.8 10.6 fusion.55
  928.5 10.5 fusion.54
  947.8 8.0 reduce-scatter.17.cloned.1.call-done
  957.7 77.0 %reduce-scatter.15.cloned.1.call-done = bf16[512,1024]{1,0:T(8,128)(2,1)} async-done(((bf16[2048,1024]{1,0:T(8,128)(2,1)}), bf16[512,1024]{1,0:T(8,128)(2,1)}) %reduce-scatter.15.cloned.1.call-update) | async-done | bytes 1048592 | tf_op jit(solution)/shard_map/reduce_scatter | solution.py:252
  1038.4 41.9 %all-reduce.17 = (f32[1024]{0:T(1024)S(1)}, f32[1024]{0:T(1024)S(1)}, f32[1024]{0:T(1024)S(1)}, f32[1024]{0:T(1024)S(1)}, f32[1024]{0:T(1024)S(1)}, /*index=5*/f...) all-reduce(f32[1024]{0:T(1024)S(1)} %dynamic-update-slice.7, ...), channel_id=1, replica_groups=mesh['dp'=8,'tensor'=4] {'dp','tensor'}, use_global_device_ids=true, to_apply=%add.7 | all-reduce | flops 13312 | bytes 106496
  1091.1 55.1 %reduce-scatter.21.cloned.1.call-done = f32[128,1024]{1,0:T(8,128)} async-done(((f32[1024,1024]{1,0:T(8,128)}), f32[128,1024]{1,0:T(8,128)}) %reduce-scatter.21.cloned.1.call-update) | async-done | bytes 524304 | tf_op jit(solution)/shard_map/reduce_scatter | solution.py:265
  1146.2 40.0 %reduce-scatter.19.cloned.1.call-done = f32[256,128]{1,0:T(8,128)} async-done(((f32[256,1024]{1,0:T(8,128)}), f32[256,128]{1,0:T(8,128)}) %reduce-scatter.19.cloned.1.call-update) | async-done | bytes 131088 | tf_op jit(solution)/shard_map/reduce_scatter | solution.py:264
  (305 shorter events, 218.5 us)
Async XLA Ops:
  7.2 62.2 %all-gather.11.cloned.1.call-start = ((), (), s32[]{:S(2)}) async-start(), calls=%async_computation.9 | async-start | bytes 1769472 | tf_op jit(solution)/shard_map/all_gather | solution.py:50
  7.9 113.1 %all-gather.9.cloned.1.call-start = ((), (), s32[]{:S(2)}) async-start(), calls=%async_computation.8 | async-start | bytes 5242880 | tf_op jit(solution)/shard_map/all_gather | solution.py:85
  8.7 251.0 %reduce-scatter.9.cloned.1.call-start = ((), (), s32[]{:S(2)}) async-start(), calls=%async_computation.10 | async-start | bytes 5242880 | tf_op jit(solution)/shard_map/reduce_scatter | solution.py:123
  131.1 49.8 %copy-start.14 = (bf16[256,1024]{1,0:T(8,128)(2,1)S(1)}, bf16[256,1024]{1,0:T(8,128)(2,1)}, u32[]{:S(2)}) copy-start(bf16[256,1024]{1,0:T(8,128)(2,1)} %all_gather.59) | copy-start | bytes 1572868
  184.1 75.5 %copy-start.3 = (bf16[512,1024]{1,0:T(8,128)(2,1)S(1)}, bf16[512,1024]{1,0:T(8,128)(2,1)}, u32[]{:S(2)}) copy-start(bf16[512,1024]{1,0:T(8,128)(2,1)} %param.21) | copy-start | bytes 3145732
  184.2 148.9 %all-gather.15.cloned.1.call-start = ((), (), s32[]{:S(2)}) async-start(), calls=%async_computation.12 | async-start | bytes 2359296 | tf_op jit(solution)/shard_map/all_gather | solution.py:52
  184.7 188.2 %all-gather.13.cloned.1.call-start = ((), (), s32[]{:S(2)}) async-start(), calls=%async_computation.11 | async-start | bytes 5242880 | tf_op jit(solution)/shard_map/all_gather | solution.py:133
  264.8 136.8 %all-gather.17.cloned.1.call-start = ((), (), s32[]{:S(2)}) async-start(), calls=%async_computation.13 | async-start | bytes 2359296 | tf_op jit(solution)/shard_map/all_gather | solution.py:53
  265.4 222.5 %reduce-scatter.11.cloned.1.call-start = ((), (), s32[]{:S(2)}) async-start(), calls=%async_computation.14 | async-start | bytes 5242880 | tf_op jit(solution)/shard_map/reduce_scatter | solution.py:137
  410.9 76.9 %copy-start.31 = (f32[1024]{0:T(1024)S(1)}, f32[1024]{0:T(1024)}, u32[]{:S(2)}) copy-start(f32[1024]{0:T(1024)} %get-tuple-element.504) | copy-start | bytes 12292
  410.9 79.5 %copy-start.9 = (bf16[512,1024]{1,0:T(8,128)(2,1)S(1)}, bf16[512,1024]{1,0:T(8,128)(2,1)}, u32[]{:S(2)}) copy-start(bf16[512,1024]{1,0:T(8,128)(2,1)} %param.35) | copy-start | bytes 3145732
  411.0 79.5 %copy-start.19 = (f32[1024]{0:T(1024)S(1)}, f32[1024]{0:T(1024)}, u32[]{:S(2)}) copy-start(f32[1024]{0:T(1024)} %get-tuple-element.505) | copy-start | bytes 12292
  411.0 165.6 %all-gather.19.cloned.1.call-start = ((), (), s32[]{:S(2)}) async-start(), calls=%async_computation.15 | async-start | bytes 5242880 | tf_op jit(solution)/shard_map/all_gather | solution.py:153
  495.2 179.2 %reduce-scatter.13.cloned.1.call-start = ((), (), s32[]{:S(2)}) async-start(), calls=%async_computation.16 | async-start | bytes 5242880 | tf_op jit(solution)/shard_map/reduce_scatter | solution.py:164
  576.6 16.0 %copy-start.33 = (bf16[1024,1024]{1,0:T(8,128)(2,1)S(1)}, bf16[1024,1024]{1,0:T(8,128)(2,1)}, u32[]{:S(2)}) copy-start(bf16[1024,1024]{1,0:T(8,128)(2,1)} %all-gather.15.cloned.1.call-done) | copy-start | bytes 6291460
  598.9 164.5 %all-gather.21.cloned.1.call-start = ((), (), s32[]{:S(2)}) async-start(), calls=%async_computation.17 | async-start | bytes 5242880 | tf_op jit(solution)/shard_map/all_gather | solution.py:176
  678.3 85.1 %copy-start.15 = (bf16[256,1024]{1,0:T(8,128)(2,1)S(1)}, bf16[256,1024]{1,0:T(8,128)(2,1)}, u32[]{:S(2)}) copy-start(bf16[256,1024]{1,0:T(8,128)(2,1)} %all_gather.59) | copy-start | bytes 1572868
  682.1 273.7 %reduce-scatter.17.cloned.1.call-start = ((), (), s32[]{:S(2)}) async-start(), calls=%async_computation.19 | async-start | bytes 3538944 | tf_op jit(solution)/shard_map/reduce_scatter | solution.py:263
  910.8 123.9 %reduce-scatter.15.cloned.1.call-start = ((), (), s32[]{:S(2)}) async-start(), calls=%async_computation.18 | async-start | bytes 5242880 | tf_op jit(solution)/shard_map/reduce_scatter | solution.py:252
  917.8 173.3 %reduce-scatter.23.cloned.1.call-start = ((), (), s32[]{:S(2)}) async-start(), calls=%async_computation.22 | async-start | bytes 4718592 | tf_op jit(solution)/shard_map/reduce_scatter | solution.py:266
  928.4 217.8 %reduce-scatter.21.cloned.1.call-start = ((), (), s32[]{:S(2)}) async-start(), calls=%async_computation.21 | async-start | bytes 4718592 | tf_op jit(solution)/shard_map/reduce_scatter | solution.py:265
  939.0 95.7 %copy-start.24 = (f32[512]{0:T(512)S(1)}, f32[512]{0:T(512)}, u32[]{:S(2)}) copy-start(f32[512]{0:T(512)} %copy-done.23) | copy-start | bytes 6148
  939.0 247.2 %reduce-scatter.19.cloned.1.call-start = ((), (), s32[]{:S(2)}) async-start(), calls=%async_computation.20 | async-start | bytes 1179648 | tf_op jit(solution)/shard_map/reduce_scatter | solution.py:264
  944.8 93.5 %copy-start.25 = (f32[1024]{0:T(1024)S(1)}, f32[1024]{0:T(1024)}, u32[]{:S(2)}) copy-start(f32[1024]{0:T(1024)} %get-tuple-element.428) | copy-start | bytes 12292
  944.8 93.5 %copy-start.26 = (f32[1024]{0:T(1024)S(1)}, f32[1024]{0:T(1024)}, u32[]{:S(2)}) copy-start(f32[1024]{0:T(1024)} %get-tuple-element.432) | copy-start | bytes 12292
  944.8 93.5 %copy-start.27 = (f32[1024]{0:T(1024)S(1)}, f32[1024]{0:T(1024)}, u32[]{:S(2)}) copy-start(f32[1024]{0:T(1024)} %get-tuple-element.426) | copy-start | bytes 12292
  944.8 93.5 %copy-start.28 = (f32[1024]{0:T(1024)S(1)}, f32[1024]{0:T(1024)}, u32[]{:S(2)}) copy-start(f32[1024]{0:T(1024)} %get-tuple-element.430) | copy-start | bytes 12292
  944.8 93.5 %copy-start.29 = (f32[1024]{0:T(1024)S(1)}, f32[1024]{0:T(1024)}, u32[]{:S(2)}) copy-start(f32[1024]{0:T(1024)} %get-tuple-element.431) | copy-start | bytes 12292
  944.9 140.7 %copy-start.2 = (f32[512,1024]{1,0:T(8,128)S(1)}, f32[512,1024]{1,0:T(8,128)}, u32[]{:S(2)}) copy-start(f32[512,1024]{1,0:T(8,128)} %copy-done.1) | copy-start | bytes 6291460
  944.9 140.7 %copy-start.18 = (f32[512]{0:T(512)S(1)}, f32[512]{0:T(512)}, u32[]{:S(2)}) copy-start(f32[512]{0:T(512)} %copy-done.17) | copy-start | bytes 6148
  944.9 140.6 %copy-start.20 = (f32[1024]{0:T(1024)S(1)}, f32[1024]{0:T(1024)}, u32[]{:S(2)}) copy-start(f32[1024]{0:T(1024)} %get-tuple-element.505) | copy-start | bytes 12292
  944.9 140.6 %copy-start.22 = (f32[512]{0:T(512)S(1)}, f32[512]{0:T(512)}, u32[]{:S(2)}) copy-start(f32[512]{0:T(512)} %copy-done.21) | copy-start | bytes 6148
  (31 other events, 113.9 us)
Sparse Core Ops, SparseCore 0:
  9.9 28.7 all-gather.10
  40.3 80.6 all-gather.8
  184.3 75.2 reduce-scatter.8
  261.5 28.3 all-gather.14
  292.0 80.8 all-gather.12
  374.8 26.7 all-gather.16
  411.1 76.7 reduce-scatter.10
  495.3 81.2 all-gather.18
  599.1 75.2 reduce-scatter.12
  682.2 81.2 all-gather.20
  911.0 44.8 reduce-scatter.16
  958.0 76.7 reduce-scatter.14
  1039.0 51.9 reduce-scatter.22
  1094.9 51.3 reduce-scatter.20
  1150.1 36.0 reduce-scatter.18
where the time goes:
time: 1200 us; the launch traced here: 1190 us
  waiting for transfers between devices  668 us (56%)
  matrix products  201 us (17%)
  blocking collectives  164 us (14%)
  local copies, waits for them, and re-layouts  82.4 us (7%)
  other arithmetic  42.2 us (4%)
  loops' own time  18.9 us (2%)
  between operations  14.9 us (1%)
    unnamed x2, blocking collectives  84.8 us
    all_gather x1, waiting for transfers between devices, on_device(): lax.all_gather(second_grad.astype(jnp.bfloat16), 'tensor', axis=0, tiled=...  81.4 us
    all_gather x1, waiting for transfers between devices, on_device(): lax.all_gather(first_grad.astype(jnp.bfloat16), 'tensor', axis=0, tiled=T...  81.2 us
    reduce_scatter x1, waiting for transfers between devices, on_device(): lax.psum_scatter(jnp.einsum('rcl,dcl->rd', qkv_low, qkv_back, preferred_e...  77 us
    reduce_scatter x1, waiting for transfers between devices, on_device(): lax.psum_scatter(jnp.dot(hidden_low, down_full, preferred_element_type=jn...  76.4 us
    reduce_scatter x1, waiting for transfers between devices, on_device(): lax.psum_scatter(jnp.einsum('rf,df->rd', pre_low, up_back, preferred_elem...  75.4 us
    reduce_scatter x1, waiting for transfers between devices, on_device(): lax.psum_scatter(jnp.dot(context_low, out_full, preferred_element_type=jn...  74.6 us
    all_gather x1, blocking collectives, on_device(): lax.all_gather(up_bias, ('dp', 'tensor'), axis=0, tiled=True)  67.7 us
  transfers between devices with their start and end apart: 15, of which 13 were waited for; matrix products, arithmetic and copies ran while one was open for 7% of the time, Pallas kernels for 0%

commit v1 on v0

v1 whole, which is shorter than its diff:
```python
import functools

import jax
import jax.numpy as jnp
from jax import lax
from jax.experimental import pallas as pl
from jax.experimental.pallas import tpu as pltpu
from jax.sharding import Mesh
from jax.sharding import PartitionSpec as P

HD = 64
LEN = 1024
PAIR = 2 * HD
QB = 256
VMEM = 56 * 1024 * 1024
ALL = ("chip", "core", "tensor")
CHIPS = ("chip", "tensor")
F32 = jnp.float32
BF16 = jnp.bfloat16
SCALE = HD ** (-0.5)
EPS = 1e-05


def nt(left, right):
    return lax.dot_general(left, right, (((1,), (1,)), ((), ())), preferred_element_type=F32)


def nn(left, right):
    return lax.dot_general(left, right, (((1,), (0,)), ((), ())), preferred_element_type=F32)


def tn(left, right):
    return lax.dot_general(left, right, (((0,), (0,)), ((), ())), preferred_element_type=F32)


def head_lane(rows, head):
    lane = lax.broadcasted_iota(jnp.int32, (rows, PAIR), 1)
    return (lane >= head * HD) & (lane < (head + 1) * HD)


def attend_kernel(q_ref, k_ref, v_ref, o_ref, lse_ref):
    rows = q_ref.shape[0]
    keys = k_ref[...]
    values_t = v_ref[...].astype(F32).T
    sub = lax.broadcasted_iota(jnp.int32, values_t.shape, 0)
    values_h = [
        jnp.where((sub >= h * HD) & (sub < (h + 1) * HD), values_t, 1.0).astype(BF16)
        for h in range(2)
    ]

    def block(step, carry):
        at = pl.ds(pl.multiple_of(step * QB, QB), QB)
        q = q_ref[at, :].astype(F32) * SCALE
        parts = []
        for h in range(2):
            qm = jnp.where(head_lane(QB, h), q, 0.0).astype(BF16)
            scores = nt(keys, qm)
            largest = jnp.max(scores, axis=0, keepdims=True)
            weights = jnp.exp(scores - largest).astype(BF16)
            out = nn(values_h[h], weights)
            total = out[(1 - h) * HD : (1 - h) * HD + 1, :]
            parts.append(out[h * HD : (h + 1) * HD, :] / total)
            lse_ref[0, h : h + 1, at] = largest + jnp.log(total)
        o_ref[at, :] = jnp.concatenate(parts, axis=0).T.astype(BF16)
        return carry

    lax.fori_loop(0, rows // QB, block, 0)


def attend(joint, groups):
    rows = joint.shape[0]
    part = lambda c: pl.BlockSpec((rows, PAIR), lambda z: (0, 3 * z + c))
    return pl.pallas_call(
        attend_kernel,
        grid=(groups,),
        in_specs=[part(0), part(1), part(2)],
        out_specs=[
            pl.BlockSpec((rows, PAIR), lambda z: (0, z)),
            pl.BlockSpec((1, 2, rows), lambda z: (z, 0, 0)),
        ],
        out_shape=[
            jax.ShapeDtypeStruct((rows, groups * PAIR), BF16),
            jax.ShapeDtypeStruct((groups, 2, rows), F32),
        ],
        compiler_params=pltpu.CompilerParams(vmem_limit_bytes=VMEM),
        cost_estimate=pl.CostEstimate(
            flops=groups * 2 * 16 * rows * rows * HD,
            bytes_accessed=groups * rows * PAIR * 8,
            transcendentals=groups * 2 * rows * rows,
        ),
        name="attend",
    )(joint, joint, joint)


def attend_back_kernel(q_ref, k_ref, v_ref, g_ref, o_ref, lse_ref, d_ref, sum_ref, dk_ref, dv_ref):
    rows = q_ref.shape[0]
    keys = k_ref[...]
    values = v_ref[...]
    keys_t = keys.astype(F32).T
    sub = lax.broadcasted_iota(jnp.int32, keys_t.shape, 0)
    keys_h = [
        jnp.where((sub >= h * HD) & (sub < (h + 1) * HD), keys_t, 0.0).astype(BF16)
        for h in range(2)
    ]
    dk_ref[...] = jnp.zeros_like(dk_ref)
    dv_ref[...] = jnp.zeros_like(dv_ref)

    def block(step, query_sum):
        at = pl.ds(pl.multiple_of(step * QB, QB), QB)
        q = q_ref[at, :].astype(F32) * SCALE
        g = g_ref[at, :].astype(F32)
        inner = (g * o_ref[at, :].astype(F32)).T
        dq = None
        for h in range(2):
            here = head_lane(QB, h)
            qm = jnp.where(here, q, 0.0).astype(BF16)
            gm = jnp.where(here, g, 0.0).astype(BF16)
            delta = jnp.sum(inner[h * HD : (h + 1) * HD, :], axis=0, keepdims=True)
            probs = jnp.exp(nt(keys, qm) - lse_ref[0, h : h + 1, at])
            score_grad = (probs * (nt(values, gm) - delta)).astype(BF16)
            dv_ref[...] += nn(probs.astype(BF16), gm)
            dk_ref[...] += nn(score_grad, qm)
            part = nn(keys_h[h], score_grad)
            dq = part if dq is None else dq + part
        dq = (dq.T * SCALE).astype(BF16)
        d_ref[at, 0:PAIR] = dq
        return query_sum + jnp.sum(dq.astype(F32), axis=0, keepdims=True)

    query_sum = lax.fori_loop(0, rows // QB, block, jnp.zeros((1, PAIR), F32))
    dv = dv_ref[...].astype(BF16)
    d_ref[:, PAIR : 2 * PAIR] = dk_ref[...].astype(BF16)
    d_ref[:, 2 * PAIR :] = dv
    sum_ref[0, 0:1, :] = query_sum
    sum_ref[0, 1:2, :] = jnp.sum(dv.astype(F32), axis=0, keepdims=True)


def attend_back(joint, context_grad, context, lse, groups):
    rows = joint.shape[0]
    part = lambda c: pl.BlockSpec((rows, PAIR), lambda z: (0, 3 * z + c))
    one = pl.BlockSpec((rows, PAIR), lambda z: (0, z))
    return pl.pallas_call(
        attend_back_kernel,
        grid=(groups,),
        in_specs=[
            part(0),
            part(1),
            part(2),
            one,
            one,
            pl.BlockSpec((1, 2, rows), lambda z: (z, 0, 0)),
        ],
        out_specs=[
            pl.BlockSpec((rows, 3 * PAIR), lambda z: (0, z)),
            pl.BlockSpec((1, 2, PAIR), lambda z: (z, 0, 0)),
        ],
        out_shape=[
            jax.ShapeDtypeStruct((rows, 3 * groups * PAIR), BF16),
            jax.ShapeDtypeStruct((groups, 2, PAIR), F32),
        ],
        scratch_shapes=[pltpu.VMEM((rows, PAIR), F32), pltpu.VMEM((rows, PAIR), F32)],
        compiler_params=pltpu.CompilerParams(vmem_limit_bytes=VMEM),
        cost_estimate=pl.CostEstimate(
            flops=groups * 2 * 40 * rows * rows * HD,
            bytes_accessed=groups * rows * PAIR * 16,
            transcendentals=groups * 2 * rows * rows,
        ),
        name="attend_back",
    )(joint, joint, joint, context_grad, context, lse)


def normalized(values_in):
    average = jnp.mean(values_in, axis=-1, keepdims=True)
    centred = values_in - average
    inverse = lax.rsqrt(jnp.mean(centred * centred, axis=-1, keepdims=True) + EPS)
    return centred * inverse, inverse


def norm_back(grad, unit, inverse, gain):
    gain_part = jnp.sum(grad * unit, axis=0)
    shift_part = jnp.sum(grad, axis=0)
    u = grad * gain
    back = inverse * (
        u
        - jnp.mean(u, axis=-1, keepdims=True)
        - unit * jnp.mean(u * unit, axis=-1, keepdims=True)
    )
    return back, gain_part, shift_part, jnp.sum(back, axis=0)


def gelu_pair(x):
    phi = 0.5 * (1.0 + lax.erf(x * (0.5**0.5)))
    slope = phi + x * jnp.exp(-0.5 * x * x) * (0.5 / jnp.pi) ** 0.5
    return (x * phi).astype(BF16), slope.astype(BF16)


def to_other(value):
    return lax.ppermute(value, "core", [(0, 1), (1, 0)])


def both_rows(value):
    return jnp.concatenate((value, to_other(value)), axis=0)


def summed_rows(rows, weight, dot):
    half = rows.shape[0] // 2
    away = to_other(dot(rows[half:], weight).astype(BF16))
    return dot(rows[:half], weight) + away.astype(F32)


def on_device(
    tokens,
    qkv_weight,
    out_weight,
    up_weight,
    down_weight,
    mid_gain,
    mid_shift,
    query_bias,
    value_bias,
    out_bias,
    end_gain,
    end_shift,
    up_bias,
    down_bias,
    cotangent,
):
    core = lax.axis_index("core")
    n_chip = lax.axis_size("chip")
    n_ten = lax.axis_size("tensor")
    strip = tokens.shape[0]
    width = tokens.shape[1]
    slab = qkv_weight.shape[0]
    cols = qkv_weight.shape[2] // 2
    units = up_weight.shape[1] // 2
    assert 2 * strip == LEN and cols == PAIR

    pairs = []
    for z in range(n_ten):
        pairs.append((z, z) if z % 2 == 0 else (z, n_ten + z - 1))
        pairs.append((n_ten + z, z + 1) if z % 2 == 0 else (n_ten + z, n_ten + z))
    swap = lambda value: lax.ppermute(value, ("core", "tensor"), pairs)

    vectors = (
        mid_gain,
        mid_shift,
        query_bias,
        value_bias,
        out_bias,
        end_gain,
        end_shift,
        up_bias,
        down_bias,
    )
    packed = lax.all_gather(jnp.concatenate(vectors), ALL, axis=0, tiled=False)
    sizes = [v.shape[0] for v in vectors]
    starts = [sum(sizes[:i]) for i in range(len(sizes))]
    whole = [packed[:, s : s + n].reshape(-1) for s, n in zip(starts, sizes)]
    gain_mid, shift_mid, bias_q, bias_v, bias_out, gain_end, shift_end, bias_up, bias_down = whole

    def own_half(vector):
        return lax.dynamic_index_in_dim(vector.reshape(n_ten, 2, -1), core, 1, keepdims=False)

    bias_q, bias_v, bias_up = own_half(bias_q), own_half(bias_v), own_half(bias_up)
    bias_qkv = jnp.stack((bias_q, jnp.zeros_like(bias_q), bias_v), axis=1).reshape(-1)
    bias_up = bias_up.reshape(-1)

    stack = jnp.concatenate(
        (
            jnp.moveaxis(qkv_weight.reshape(slab, 3, 2, cols), 0, 3)
            .transpose(1, 0, 2, 3)
            .reshape(2, 3 * cols, slab),
            out_weight.reshape(2, cols, slab),
            up_weight.T.reshape(2, units, slab),
            down_weight.reshape(2, units, slab),
        ),
        axis=1,
    )
    keep = lax.dynamic_index_in_dim(stack, core, 0, keepdims=False)
    came = to_other(lax.dynamic_index_in_dim(stack, 1 - core, 0, keepdims=False))
    shard = jnp.concatenate(
        (jnp.where(core == 0, keep, came), jnp.where(core == 0, came, keep)), axis=1
    )
    bounds = (0, 3 * cols, 4 * cols, 4 * cols + units, 4 * cols + 2 * units)

    def gathered(index):
        part = shard[bounds[index] : bounds[index + 1]]
        rows = part.shape[0]
        full = lax.all_gather(part, CHIPS, axis=0, tiled=False)
        return (
            full.reshape(n_chip, n_ten, rows, 2 * slab)
            .transpose(1, 2, 0, 3)
            .reshape(n_ten * rows, width)
        )

    w_qkv, w_out, w_up, w_down = (gathered(i) for i in range(4))

    mine = swap(tokens)
    cot = swap(cotangent)
    seen = both_rows(mine)

    joint = (nt(seen, w_qkv) + bias_qkv).astype(BF16)
    context, lse = attend(joint, n_ten)
    branch = summed_rows(context, w_out, nn)
    unit_mid, inverse_mid = normalized(mine.astype(F32) + branch + bias_out)
    middle = unit_mid * gain_mid + shift_mid
    seen_middle = both_rows(middle.astype(BF16))
    hidden, slope = gelu_pair(nt(seen_middle, w_up) + bias_up)
    branch_two = summed_rows(hidden, w_down, nn)
    unit_end, inverse_end = normalized(middle + branch_two + bias_down)
    encoded = swap((unit_end * gain_end + shift_end).astype(BF16))

    second_grad, end_gain_part, end_shift_part, down_bias_part = norm_back(
        cot.astype(F32), unit_end, inverse_end, gain_end
    )
    seen_second = both_rows(second_grad.astype(BF16))
    pre_grad = (nt(seen_second, w_down) * slope.astype(F32)).astype(BF16)
    up_bias_part = jnp.sum(pre_grad.astype(F32), axis=0)
    middle_grad = summed_rows(pre_grad, w_up, nn) + second_grad
    down_sum = tn(hidden, seen_second)
    up_sum = tn(pre_grad, seen_middle)
    first_grad, mid_gain_part, mid_shift_part, out_bias_part = norm_back(
        middle_grad, unit_mid, inverse_mid, gain_mid
    )
    seen_first = both_rows(first_grad.astype(BF16))
    context_grad = nt(seen_first, w_out).astype(BF16)
    out_sum = tn(context, seen_first)
    qkv_low, bias_sums = attend_back(joint, context_grad, context, lse, n_ten)
    qkv_sum = tn(qkv_low, seen)
    input_grad = summed_rows(qkv_low, w_qkv, nn) + first_grad
    input_grad = swap(input_grad.astype(BF16)).astype(F32)

    def scattered(total, extra=None):
        rows = total.shape[0] // n_ten
        blocks = (
            total.astype(BF16)
            .reshape(n_ten, rows, n_chip, 2 * slab)
            .transpose(2, 0, 1, 3)
            .reshape(n_chip * n_ten, rows, 2 * slab)
        )
        if extra is not None:
            blocks = jnp.concatenate((blocks, extra), axis=1)
        return lax.psum_scatter(blocks, CHIPS, scatter_dimension=0, tiled=False)

    wide = (
        mid_gain_part,
        mid_shift_part,
        out_bias_part,
        end_gain_part,
        end_shift_part,
        down_bias_part,
    )
    narrow = (bias_sums[:, 0], bias_sums[:, 1], up_bias_part)
    aligned = n_chip == n_ten
    extra = None
    if aligned:
        tail = []
        for vector in wide:
            tail.append(vector.reshape(n_chip, 2, n_ten, -1).transpose(0, 2, 1, 3))
        for vector in narrow:
            tail.append(vector.reshape(n_chip, n_ten, 1, -1))
        tail = [t.reshape(n_chip * n_ten, -1) for t in tail]
        tail_sizes = [t.shape[1] for t in tail]
        used = sum(tail_sizes)
        lines = -(-used // (2 * slab))
        lines = -(-lines // 16) * 16
        extra = jnp.concatenate(
            tail + [jnp.zeros((n_chip * n_ten, lines * 2 * slab - used), F32)], axis=1
        )
        extra = extra.reshape(n_chip * n_ten, lines, 2 * slab).astype(BF16)
    down_part = scattered(down_sum)
    up_part = scattered(up_sum)
    out_part = scattered(out_sum)
    qkv_part = scattered(qkv_sum, extra)
    if aligned:
        vector_line = qkv_part[3 * cols :].reshape(-1).astype(F32)
        qkv_part = qkv_part[: 3 * cols]
    parts = jnp.concatenate((qkv_part, out_part, up_part, down_part), axis=0)
    parts = parts.reshape(-1, 2, slab)
    keep = lax.dynamic_index_in_dim(parts, core, 1, keepdims=False)
    came = to_other(lax.dynamic_index_in_dim(parts, 1 - core, 1, keepdims=False))
    halves = jnp.stack(
        (jnp.where(core == 0, keep, came), jnp.where(core == 0, came, keep)), axis=0
    ).astype(F32)
    cut = [halves[:, bounds[i] : bounds[i + 1]] for i in range(4)]
    qkv_out = (
        cut[0].reshape(2, 3, cols, slab).transpose(3, 1, 0, 2).reshape(slab, 3, 2 * cols)
    )
    out_out = cut[1].reshape(2 * cols, slab)
    up_out = cut[2].reshape(2 * units, slab).T
    down_out = cut[3].reshape(2 * units, slab)

    if aligned:
        n_wide = sum(tail_sizes[:6])
        doubled = vector_line[:n_wide].reshape(6, 2, -1)
        own = lax.dynamic_index_in_dim(doubled, core, 1, keepdims=False)
        away = to_other(lax.dynamic_index_in_dim(doubled, 1 - core, 1, keepdims=False))
        own = own + away
        rest = vector_line[n_wide:]
        n_q, n_v, n_up = tail_sizes[6:]
        grads = [own[i] for i in range(6)] + [
            rest[:n_q],
            rest[n_q : n_q + n_v],
            rest[n_q + n_v : n_q + n_v + n_up],
        ]
    else:

        def placed(vector):
            blank = jnp.zeros((n_ten, 2, vector.size // n_ten), F32)
            return lax.dynamic_update_slice_in_dim(
                blank, vector.reshape(n_ten, 1, -1), core, 1
            ).reshape(-1)

        flat = list(wide) + [placed(v) for v in narrow]
        devices = n_chip * 2 * n_ten
        flat = [v.reshape(devices, -1) for v in flat]
        sums = lax.psum_scatter(
            jnp.concatenate(flat, axis=1), ALL, scatter_dimension=0, tiled=False
        )
        grads = []
        at = 0
        for v in flat:
            grads.append(sums[at : at + v.shape[1]])
            at += v.shape[1]
    g_mid_gain, g_mid_shift, g_out_bias, g_end_gain, g_end_shift, g_down_bias, g_q, g_v, g_up = (
        grads
    )
    return (
        encoded,
        input_grad,
        qkv_out,
        out_out,
        up_out,
        down_out,
        g_mid_gain,
        g_mid_shift,
        g_q,
        g_v,
        g_out_bias,
        g_end_gain,
        g_end_shift,
        g_up,
        g_down_bias,
    )


def solution(mesh):
    n_dp, n_ten = mesh.devices.shape
    inner = Mesh(mesh.devices.reshape(n_dp // 2, 2, n_ten), ALL)
    rows = P(ALL, None)
    vector = P(ALL)
    dp = ("chip", "core")
    weights = (P(dp, None, "tensor"), P("tensor", dp), P(dp, "tensor"), P("tensor", dp))
    return jax.shard_map(
        on_device,
        mesh=inner,
        in_specs=(rows, *weights, *(vector,) * 9, rows),
        out_specs=(rows, rows, *weights, *(vector,) * 9),
        check_vma=False,
    )
```

time: 1200 us -> 779 us (0.65)
  waiting for transfers between devices: 668 us -> 414 us
  matrix products: 201 us -> 83.1 us
  blocking collectives: 164 us -> 70.2 us
  Pallas kernels: 0 us -> 55.9 us
  starting transfers between devices: 1.86 us -> 35.1 us
  other arithmetic: 42.2 us -> 14.2 us
  loops' own time: 18.9 us -> 0 us
    reduce_scatter x8 -> x4, waiting for transfers between devices: 411 us -> 270 us  [scattered(): return lax.psum_scatter(blocks, CHIPS, scatter_dimension=0, tiled=False)]
    all_gather x7 -> x4, waiting for transfers between devices: 255 us -> 130 us  [gathered(): full = lax.all_gather(part, CHIPS, axis=0, tiled=False)]
    dot_general x40 -> x16, matrix products: 201 us -> 83.1 us  [the longest x4 29.6 us: nt(): lax.dot_general(left, right, (((1,), (1,)), ((), ())), preferred_element_...]
    unnamed x2 -> x0, blocking collectives: 84.8 us -> none
    pallas_call x0 -> x2, Pallas kernels: none -> 55.9 us  [the longest x1 28 us: attend_back(): pl.pallas_call(attend_back_kernel, grid=(groups,), in_specs=[part(0), par...]
    reshape x0 -> x23, local copies, waits for them, and re-layouts: none -> 38 us  [the longest x8 33.9 us: scattered(): blocks = total.astype(BF16).reshape(n_ten, rows, n_chip, 2 * slab).transp...]
    ppermute x0 -> x15, starting transfers between devices: none -> 34.3 us  [the longest x11 28.2 us: to_other(): return lax.ppermute(value, 'core', [(0, 1), (1, 0)])]
    dynamic_slice x29 -> x6, local copies, waits for them, and re-layouts: 25.2 us -> 0.53 us  [the longest x2 0.28 us: on_device(): keep = lax.dynamic_index_in_dim(parts, core, 1, keepdims=False)]
  transfers between devices with their start and end apart: 15 -> 23, of which waited for: 13 -> 14; matrix products, arithmetic and copies ran while one was open for 7% -> 16% of each run, Pallas kernels for 0% -> 7%
where the time goes in v1:
time: 779 us; the launch traced here: 771 us
  waiting for transfers between devices  414 us (53%)
  local copies, waits for them, and re-layouts  83.2 us (11%)
  matrix products  83.1 us (11%)
  blocking collectives  70.2 us (9%)
  Pallas kernels  55.9 us (7%)
  starting transfers between devices  35.1 us (5%)
  between operations  15.3 us (2%)
  other arithmetic  14.2 us (2%)
    reduce_scatter x4, waiting for transfers between devices, scattered(): return lax.psum_scatter(blocks, CHIPS, scatter_dimension=0, tiled=False)  270 us
    all_gather x4, waiting for transfers between devices, gathered(): full = lax.all_gather(part, CHIPS, axis=0, tiled=False)  130 us
    all_gather x1, blocking collectives, on_device(): packed = lax.all_gather(jnp.concatenate(vectors), ALL, axis=0, tiled=False)  70.2 us
    reshape x8, local copies, waits for them, and re-layouts, scattered(): blocks = total.astype(BF16).reshape(n_ten, rows, n_chip, 2 * slab).transp...  33.9 us
    dot_general x4, matrix products, nt(): lax.dot_general(left, right, (((1,), (1,)), ((), ())), preferred_element_...  29.6 us
    dot_general x4, matrix products, tn(): lax.dot_general(left, right, (((0,), (0,)), ((), ())), preferred_element_...  28.3 us
    ppermute x11, starting transfers between devices, to_other(): return lax.ppermute(value, 'core', [(0, 1), (1, 0)])  28.2 us
    pallas_call x1, Pallas kernels, attend_back(): pl.pallas_call(attend_back_kernel, grid=(groups,), in_specs=[part(0), par...  28 us
  transfers between devices with their start and end apart: 23, of which 14 were waited for; matrix products, arithmetic and copies ran while one was open for 16% of the time, Pallas kernels for 7%

profile of v1, /device:TPU:0, one launch (start us, length us, event | category | flops | bytes accessed | tf_op | source)
XLA Modules:
  0.0 771.3 jit_solution(10092137339639855649)
XLA Ops:
  16.4 17.7 %collective-permute-start.1 = (bf16[512,1024]{1,0:T(8,128)(2,1)S(1)}, bf16[512,1024]{1,0:T(8,128)(2,1)S(1)}, u32[]{:S(2)}, u32[]{:S(2)}) collective-permute-start(bf16[512,1024]{1,0:T(8,128)(2,1)S(1)} %collective-permute-done), channel_id=1, source_target_pairs={{0,4},{4,0},{1,5},{5,1},{2,6},{6,2},{3,7},{7,3},{8,12},{12,8},{9,1... | collective-permute-start | bytes 3145736 | tf_op jit(solution)/shard_map/ppermute | solution.py:197
  34.3 70.2 %all-gather.5 = f32[32,1,384]{2,1,0:T(1,128)S(1)} all-gather(f32[1,1,384]{2,1,0:T(1,128)S(1)} %reshape.275), channel_id=3, replica_groups=mesh['chip'=4,'core'=2,'tensor'=4] {'chip','core','tensor'}, dimensions={0}, use_global_device_ids=true | all-gather | bytes 50688 | tf_op jit(solution)/shard_map/all_gather | solution.py:254
  109.3 32.8 %all-gather.11.cloned.1.call-done = bf16[6144,256]{1,0:T(8,128)(2,1)} async-done(((bf16[384,256]{1,0:T(8,128)(2,1)}), bf16[6144,256]{1,0:T(8,128)(2,1)}) %all-gather.11.cloned.1.call-update) | async-done | bytes 3145744 | tf_op jit(solution)/shard_map/all_gather | solution.py:288
  142.1 4.3 copy.99
  148.8 6.4 add_convert_fusion.q_ref.k_ref.v_ref
  155.3 28.0 %attend.1 = (bf16[1024,512]{1,0:T(8,128)(2,1)}, f32[4,2,1024]{2,1,0:T(2,128)}) custom-call(bf16[1024,1536]{1,0:T(8,128)(2,1)} %add_convert_fusion.q_ref.k_ref.v_ref, bf16[1024,1536]{1,0:T(8,128)(2,1)} %add_convert_fusion.q_ref.k_ref.v_ref, bf16[1024,1536]{1,0:T(8,128)(2,1)} %add_convert_fusion.q_ref.k_ref.v_ref), custom_call_target="tpu_custom_call" | custom-call | flops 8589934592 | bytes 4194304 | tf_op jit(solution)/shard_map/attend/pallas_call | solution.py:73
  191.6 28.3 %all-gather.15.cloned.1.call-done = bf16[8192,256]{1,0:T(8,128)(2,1)} async-done(((bf16[512,256]{1,0:T(8,128)(2,1)}), bf16[8192,256]{1,0:T(8,128)(2,1)}) %all-gather.15.cloned.1.call-update) | async-done | bytes 4194320 | tf_op jit(solution)/shard_map/all_gather | solution.py:288
  219.9 5.4 copy.101
  225.3 3.0 copy.128
  228.3 69.4 %all-gather.17.cloned.1.call-done = bf16[8192,256]{1,0:T(8,128)(2,1)} async-done(((bf16[512,256]{1,0:T(8,128)(2,1)}), bf16[8192,256]{1,0:T(8,128)(2,1)}) %all-gather.17.cloned.1.call-update) | async-done | bytes 4194320 | tf_op jit(solution)/shard_map/all_gather | solution.py:288
  297.6 5.4 copy.102
  305.7 8.4 %multiply_convert_fusion.1 = (bf16[1024,2048]{1,0:T(8,128)(2,1)S(1)}, f32[1024,2048]{1,0:T(8,128)}) fusion(f32[2048]{0:T(1024)S(1)} %bitcast.178, bf16[2048,1024]{1,0:T(8,128)(2,1)S(1)} %bitcast.133, bf16[512,1024]{1,0:T(8,128)(2,1)} %collective-permute-done.4, bf16[512,1024]{1,0:T(8,128)(2,1)S(1)} %fusion.20), kind=kOutput, calls=%fused_computation.7 | convolution fusion | flops 4311744512 | bytes 18882560 | tf_op jit(solution)/shard_map/dot_general | solution.py:25
  314.1 3.3 fusion.28
  320.5 5.8 fusion.56
  329.6 7.7 %collective-permute-start.8 = (bf16[512,1024]{1,0:T(8,128)(2,1)S(1)}, bf16[512,1024]{1,0:T(8,128)(2,1)S(1)}, u32[]{:S(2)}, u32[]{:S(2)}) collective-permute-start(bf16[512,1024]{1,0:T(8,128)(2,1)S(1)} %convert_element_type.108), channel_id=1, source_target_pairs={{0,4},{4,0},{1,5},{5,1},{2,6},{6,2},{3,7},{7,3},{8,12},{12,8},{9,1... | collective-permute-start | bytes 3145736 | tf_op jit(solution)/shard_map/ppermute | solution.py:197
  339.6 11.2 %fusion.61 = (bf16[2048]{0:T(1024)(128)(2,1)S(1)}, bf16[1024,2048]{1,0:T(8,128)(2,1)S(1)}) fusion(f32[1024,2048]{1,0:T(8,128)} %get-tuple-element.103, f32[2048]{0:T(1024)S(1)} %bitcast.179, bf16[2048,1024]{1,0:T(8,128)(2,1)S(1)} %bitcast.138, bf16[512,1024]{1,0:T(8,128)(2,1)S(1)} %collective-permute-done.8, bf16[512,1024]{1,0:T(8,128)(2,1)S(1)} %convert_element_type.108), kind=kOutput, calls=%fused_computation.128 | convolution fusion | flops 4328519680 | bytes 18886656 | tf_op jit(solution)/shard_map/dot_general | solution.py:25
  356.0 3.1 multiply_reduce_fusion
  370.7 9.3 %convolution_convert_fusion.1 = bf16[2048,1024]{1,0:T(8,128)(2,1)} fusion(bf16[1024,2048]{1,0:T(8,128)(2,1)} %copy-done.30, bf16[512,1024]{1,0:T(8,128)(2,1)} %copy-done.26, bf16[512,1024]{1,0:T(8,128)(2,1)} %copy-done.8), kind=kOutput, calls=%fused_computation.11 | convolution fusion | flops 4301258752 | bytes 10485760 | tf_op jit(solution)/shard_map/dot_general | solution.py:33
  380.0 8.0 %reshape.258 = bf16[4,512,4,256]{3,2,1,0:T(4,128)(2,1)} reshape(bf16[2048,1024]{1,0:T(8,128)(2,1)} %convolution_convert_fusion.1) | data formatting | bytes 8388608 | tf_op jit(solution)/shard_map/reshape | solution.py:336
  388.0 4.8 copy.115
  394.0 9.1 %convolution_convert_fusion.2 = bf16[2048,1024]{1,0:T(8,128)(2,1)} fusion(bf16[1024,2048]{1,0:T(8,128)(2,1)} %copy-done.28, bf16[512,1024]{1,0:T(8,128)(2,1)} %collective-permute-done.4, bf16[512,1024]{1,0:T(8,128)(2,1)S(1)} %copy-done.12), kind=kOutput, calls=%fused_computation.12 | convolution fusion | flops 4301258752 | bytes 10485760 | tf_op jit(solution)/shard_map/dot_general | solution.py:33
  403.1 7.9 %reshape.256 = bf16[4,512,4,256]{3,2,1,0:T(4,128)(2,1)} reshape(bf16[2048,1024]{1,0:T(8,128)(2,1)} %convolution_convert_fusion.2) | data formatting | bytes 8388608 | tf_op jit(solution)/shard_map/reshape | solution.py:336
  411.0 4.9 copy.113
  417.5 3.5 convolution_convert_fusion.4.g_ref
  421.0 28.0 %attend_back.1 = (bf16[1024,1536]{1,0:T(8,128)(2,1)}, f32[4,2,128]{2,1,0:T(2,128)}) custom-call(bf16[1024,1536]{1,0:T(8,128)(2,1)} %add_convert_fusion.q_ref.k_ref.v_ref, bf16[1024,1536]{1,0:T(8,128)(2,1)} %add_convert_fusion.q_ref.k_ref.v_ref, bf16[1024,1536]{1,0:T(8,128)(2,1)} %add_convert_fusion.q_ref.k_ref.v_ref, ...), custom_call_target="tpu_custom_call" | custom-call | flops 21474836480 | bytes 8388608 | tf_op jit(solution)/shard_map/attend_back/pallas_call | solution.py:141
  450.1 7.7 convolution_convert_fusion
  457.7 4.8 reshape.240
  466.9 3.4 fusion.25
  473.0 2.9 add_convert_fusion.1
  480.3 85.3 %reduce-scatter.11.cloned.1.call-done = bf16[1,512,256]{2,1,0:T(8,128)(2,1)} async-done(((bf16[16,512,256]{2,1,0:T(8,128)(2,1)}), bf16[1,512,256]{2,1,0:T(8,128)(2,1)}) %reduce-scatter.11.cloned.1.call-update) | async-done | bytes 262160 | tf_op jit(solution)/shard_map/reduce_scatter | solution.py:342
  566.7 96.0 %reduce-scatter.9.cloned.1.call-done = bf16[1,512,256]{2,1,0:T(8,128)(2,1)} async-done(((bf16[16,512,256]{2,1,0:T(8,128)(2,1)}), bf16[1,512,256]{2,1,0:T(8,128)(2,1)}) %reduce-scatter.9.cloned.1.call-update) | async-done | bytes 262160 | tf_op jit(solution)/shard_map/reduce_scatter | solution.py:342
  663.8 88.6 %reduce-scatter.5.cloned.1.call-done = bf16[1,400,256]{2,1,0:T(8,128)(2,1)} async-done(((bf16[16,400,256]{2,1,0:T(8,128)(2,1)}), bf16[1,400,256]{2,1,0:T(8,128)(2,1)}) %reduce-scatter.5.cloned.1.call-update) | async-done | bytes 204816 | tf_op jit(solution)/shard_map/reduce_scatter | solution.py:342
  (221 shorter events, 81.4 us)
Async XLA Ops:
  7.2 99.8 %all-gather.13.cloned.1.call-start = ((), (), s32[]{:S(2)}) async-start(), calls=%async_computation.9 | async-start | bytes 1114112 | tf_op jit(solution)/shard_map/all_gather | solution.py:288
  10.6 1.9 collective-permute-start.2
  12.5 21.6 %copy-start.15 = (f32[32]{0:T(128)S(1)}, f32[32]{0:T(128)}, u32[]{:S(2)}) copy-start(f32[32]{0:T(128)} %param.20) | copy-start | bytes 388
  12.5 21.6 %copy-start.16 = (f32[32]{0:T(128)S(1)}, f32[32]{0:T(128)}, u32[]{:S(2)}) copy-start(f32[32]{0:T(128)} %param.21) | copy-start | bytes 388
  12.5 21.6 %copy-start.17 = (f32[32]{0:T(128)S(1)}, f32[32]{0:T(128)}, u32[]{:S(2)}) copy-start(f32[32]{0:T(128)} %param.22) | copy-start | bytes 388
  12.6 21.6 %copy-start.18 = (f32[32]{0:T(128)S(1)}, f32[32]{0:T(128)}, u32[]{:S(2)}) copy-start(f32[32]{0:T(128)} %param.23) | copy-start | bytes 388
  12.6 21.6 %copy-start.19 = (f32[32]{0:T(128)S(1)}, f32[32]{0:T(128)}, u32[]{:S(2)}) copy-start(f32[32]{0:T(128)} %param.24) | copy-start | bytes 388
  12.6 21.6 %copy-start.20 = (f32[32]{0:T(128)S(1)}, f32[32]{0:T(128)}, u32[]{:S(2)}) copy-start(f32[32]{0:T(128)} %param.25) | copy-start | bytes 388
  13.3 128.8 %all-gather.11.cloned.1.call-start = ((), (), s32[]{:S(2)}) async-start(), calls=%async_computation.8 | async-start | bytes 3342336 | tf_op jit(solution)/shard_map/all_gather | solution.py:288
  14.1 205.8 %all-gather.15.cloned.1.call-start = ((), (), s32[]{:S(2)}) async-start(), calls=%async_computation.10 | async-start | bytes 4456448 | tf_op jit(solution)/shard_map/all_gather | solution.py:288
  15.0 282.7 %all-gather.17.cloned.1.call-start = ((), (), s32[]{:S(2)}) async-start(), calls=%async_computation.11 | async-start | bytes 4456448 | tf_op jit(solution)/shard_map/all_gather | solution.py:288
  15.6 462.2 %reduce-scatter.7.cloned.1.call-start = ((), (), s32[]{:S(2)}) async-start(), calls=%async_computation.5 | async-start | bytes 1114112 | tf_op jit(solution)/shard_map/reduce_scatter | solution.py:342
  15.6 0.7 collective-permute-start
  16.4 90.6 %copy-start.13 = (bf16[512,1024]{1,0:T(8,128)(2,1)}, bf16[512,1024]{1,0:T(8,128)(2,1)S(1)}, u32[]{:S(2)}) copy-start(bf16[512,1024]{1,0:T(8,128)(2,1)S(1)} %collective-permute-done) | copy-start | bytes 3145732
  16.4 89.6 %collective-permute-start.1 = (bf16[512,1024]{1,0:T(8,128)(2,1)S(1)}, bf16[512,1024]{1,0:T(8,128)(2,1)S(1)}, u32[]{:S(2)}, u32[]{:S(2)}) collective-permute-start(bf16[512,1024]{1,0:T(8,128)(2,1)S(1)} %collective-permute-done), channel_id=1, source_target_pairs={{0,4},{4,0},{1,5},{5,1},{2,6},{6,2},{3,7},{7,3},{8,12},{12,8},{9,1... | collective-permute-start | bytes 3145736 | tf_op jit(solution)/shard_map/ppermute | solution.py:197
  109.3 78.6 %copy-start.9 = (bf16[64,8,4,256]{3,1,2,0:T(8,128)(2,1)}, bf16[64,8,4,256]{3,1,2,0:T(8,128)(2,1)S(1)}, u32[]{:S(2)}) copy-start(bf16[64,8,4,256]{3,1,2,0:T(8,128)(2,1)S(1)} %copy.127) | copy-start | bytes 3145732
  185.0 2.9 collective-permute-start.3
  191.3 112.9 %copy-start.11 = (bf16[512,1024]{1,0:T(8,128)(2,1)}, bf16[512,1024]{1,0:T(8,128)(2,1)S(1)}, u32[]{:S(2)}) copy-start(bf16[512,1024]{1,0:T(8,128)(2,1)S(1)} %fusion.20) | copy-start | bytes 3145732
  191.3 112.9 %collective-permute-start.4 = (bf16[512,1024]{1,0:T(8,128)(2,1)S(1)}, bf16[512,1024]{1,0:T(8,128)(2,1)}, u32[]{:S(2)}, u32[]{:S(2)}) collective-permute-start(bf16[512,1024]{1,0:T(8,128)(2,1)S(1)} %fusion.20), channel_id=1, source_target_pairs={{0,4},{4,0},{1,5},{5,1},{2,6},{6,2},{3,7},{7,3},{8,12},{12,8},{9,1... | collective-permute-start | bytes 3145736 | tf_op jit(solution)/shard_map/ppermute | solution.py:197
  317.5 3.0 collective-permute-start.5
  317.5 9.1 %collective-permute-start.7 = (bf16[512,1024]{1,0:T(8,128)(2,1)}, bf16[512,1024]{1,0:T(8,128)(2,1)S(1)}, u32[]{:S(2)}, u32[]{:S(2)}) collective-permute-start(bf16[512,1024]{1,0:T(8,128)(2,1)} %param.29), channel_id=1, source_target_pairs={{0,0},{4,1},{1,4},{5,5},{2,2},{6,3},{3,6},{7,7},{8,8},{12,9},{9,12... | collective-permute-start | bytes 3145736 | tf_op jit(solution)/shard_map/ppermute | solution.py:241
  329.6 10.0 %collective-permute-start.8 = (bf16[512,1024]{1,0:T(8,128)(2,1)S(1)}, bf16[512,1024]{1,0:T(8,128)(2,1)S(1)}, u32[]{:S(2)}, u32[]{:S(2)}) collective-permute-start(bf16[512,1024]{1,0:T(8,128)(2,1)S(1)} %convert_element_type.108), channel_id=1, source_target_pairs={{0,4},{4,0},{1,5},{5,1},{2,6},{6,2},{3,7},{7,3},{8,12},{12,8},{9,1... | collective-permute-start | bytes 3145736 | tf_op jit(solution)/shard_map/ppermute | solution.py:197
  353.3 2.7 collective-permute-start.9
  361.4 2.7 collective-permute-start.10
  370.4 195.2 %reduce-scatter.11.cloned.1.call-start = ((), (), s32[]{:S(2)}) async-start(), calls=%async_computation.7 | async-start | bytes 4456448 | tf_op jit(solution)/shard_map/reduce_scatter | solution.py:342
  392.8 269.9 %reduce-scatter.9.cloned.1.call-start = ((), (), s32[]{:S(2)}) async-start(), calls=%async_computation.6 | async-start | bytes 4456448 | tf_op jit(solution)/shard_map/reduce_scatter | solution.py:342
  415.9 336.5 %reduce-scatter.5.cloned.1.call-start = ((), (), s32[]{:S(2)}) async-start(), calls=%async_computation.4 | async-start | bytes 3481600 | tf_op jit(solution)/shard_map/reduce_scatter | solution.py:342
  470.3 2.7 collective-permute-start.11
  470.7 7.0 collective-permute-start.6
  475.9 2.8 collective-permute-start.12
  754.5 2.3 collective-permute-start.14
  756.2 1.9 collective-permute-start.13
  (22 other events, 174.8 us)
Sparse Core Ops, SparseCore 0:
  13.4 58.1 all-gather.12
  75.0 66.9 all-gather.10
  145.4 74.4 all-gather.14
  223.0 74.5 all-gather.16
  370.5 77.5 reduce-scatter.6
  450.3 115.2 reduce-scatter.10
  568.0 94.6 reduce-scatter.8
  665.1 87.2 reduce-scatter.4

commit v2 on v1

--- a/solution.py
+++ b/solution.py
@@ -207,6 +207,102 @@
     return dot(rows[:half], weight) + away.astype(F32)
 
 
+def assemble_kernel(chip_ref, own_ref, x_ref, y_ref, low_ref, high_ref, *out_refs):
+    chip = chip_ref[0]
+    wide = own_ref.shape[2]
+    lower = pl.program_id(0) < pl.num_programs(0) // 2
+    start = 0
+    for out_ref in out_refs:
+        rows = slice(start, start + out_ref.shape[1])
+        start += out_ref.shape[1]
+
+        def columns(move):
+            at = pl.multiple_of(lax.bitwise_xor(chip, move) * wide, wide)
+            return pl.ds(at, wide)
+
+        out_ref[0, :, columns(0)] = own_ref[0, rows, :]
+        out_ref[0, :, columns(1)] = x_ref[0, rows, :]
+        out_ref[0, :, columns(2)] = y_ref[0, rows, :]
+        far = jnp.where(lower, low_ref[0, rows, :], high_ref[0, rows, :])
+        out_ref[0, :, columns(3)] = far
+
+
+def assemble(chip, blocks, heights):
+    own, low = blocks[0], blocks[3]
+    members, rows, wide = own.shape
+    half = low.shape[0]
+    one = pl.BlockSpec((1, rows, wide), lambda z, c: (z, 0, 0))
+    return pl.pallas_call(
+        assemble_kernel,
+        grid_spec=pltpu.PrefetchScalarGridSpec(
+            num_scalar_prefetch=1,
+            grid=(members,),
+            in_specs=[
+                one,
+                one,
+                one,
+                pl.BlockSpec((1, rows, wide), lambda z, c: (jnp.minimum(z, half - 1), 0, 0)),
+                pl.BlockSpec((1, rows, wide), lambda z, c: (jnp.maximum(z - half, 0), 0, 0)),
+            ],
+            out_specs=[pl.BlockSpec((1, h, 4 * wide), lambda z, c: (z, 0, 0)) for h in heights],
+        ),
+        out_shape=[jax.ShapeDtypeStruct((members, h, 4 * wide), BF16) for h in heights],
+        compiler_params=pltpu.CompilerParams(vmem_limit_bytes=VMEM),
+        cost_estimate=pl.CostEstimate(
+            flops=0, bytes_accessed=16 * members * rows * wide, transcendentals=0
+        ),
+        name="assemble",
+    )(chip.reshape(1), *blocks)
+
+
+def to_chip(value, move):
+    return lax.ppermute(value, "chip", [(i, i ^ move) for i in range(4)])
+
+
+def after(value, *earlier):
+    return lax.optimization_barrier((value, *earlier))[0]
+
+
+def layer_gather(part):
+    own = lax.all_gather(part, "tensor", axis=0, tiled=False)
+    half = own.shape[0] // 2
+    by_x = to_chip(own, 1)
+    by_y = to_chip(own, 2)
+    return own, by_x, by_y, to_chip(by_y[:half], 1), to_chip(by_x[half:], 2)
+
+
+def layer_scatter(block):
+    far = block(3)
+    half = far.shape[0] // 2
+    low = to_chip(far[:half], 1)
+    high = to_chip(far[half:], 2)
+    near_x = block(1)
+    near_y = block(2)
+    add = lambda a, b: (a.astype(F32) + b.astype(F32)).astype(BF16)
+    near_y = jnp.concatenate((add(near_y[:half], low), near_y[half:]), axis=0)
+    near_x = jnp.concatenate((near_x[:half], add(near_x[half:], high)), axis=0)
+    came_y = to_chip(near_y, 2)
+    came_x = to_chip(near_x, 1)
+    own = block(0)
+    return (own.astype(F32) + came_x.astype(F32) + came_y.astype(F32)).astype(BF16)
+
+
+def in_chip_order(chip, blocks):
+    b0, b1, b2, b3 = blocks
+    odd_x = (chip & 1) == 1
+    odd_y = (chip & 2) == 2
+    a0, a1 = jnp.where(odd_x, b1, b0), jnp.where(odd_x, b0, b1)
+    a2, a3 = jnp.where(odd_x, b3, b2), jnp.where(odd_x, b2, b3)
+    return jnp.stack(
+        (
+            jnp.where(odd_y, a2, a0),
+            jnp.where(odd_y, a3, a1),
+            jnp.where(odd_y, a0, a2),
+            jnp.where(odd_y, a1, a3),
+        )
+    )
+
+
 def on_device(
     tokens,
     qkv_weight,
@@ -225,6 +321,7 @@
     cotangent,
 ):
     core = lax.axis_index("core")
+    chip = lax.axis_index("chip")
     n_chip = lax.axis_size("chip")
     n_ten = lax.axis_size("tensor")
     strip = tokens.shape[0]
@@ -251,19 +348,6 @@
         up_bias,
         down_bias,
     )
-    packed = lax.all_gather(jnp.concatenate(vectors), ALL, axis=0, tiled=False)
-    sizes = [v.shape[0] for v in vectors]
-    starts = [sum(sizes[:i]) for i in range(len(sizes))]
-    whole = [packed[:, s : s + n].reshape(-1) for s, n in zip(starts, sizes)]
-    gain_mid, shift_mid, bias_q, bias_v, bias_out, gain_end, shift_end, bias_up, bias_down = whole
-
-    def own_half(vector):
-        return lax.dynamic_index_in_dim(vector.reshape(n_ten, 2, -1), core, 1, keepdims=False)
-
-    bias_q, bias_v, bias_up = own_half(bias_q), own_half(bias_v), own_half(bias_up)
-    bias_qkv = jnp.stack((bias_q, jnp.zeros_like(bias_q), bias_v), axis=1).reshape(-1)
-    bias_up = bias_up.reshape(-1)
-
     stack = jnp.concatenate(
         (
             jnp.moveaxis(qkv_weight.reshape(slab, 3, 2, cols), 0, 3)
@@ -282,23 +366,65 @@
     )
     bounds = (0, 3 * cols, 4 * cols, 4 * cols + units, 4 * cols + 2 * units)
 
-    def gathered(index):
-        part = shard[bounds[index] : bounds[index + 1]]
-        rows = part.shape[0]
-        full = lax.all_gather(part, CHIPS, axis=0, tiled=False)
-        return (
-            full.reshape(n_chip, n_ten, rows, 2 * slab)
-            .transpose(1, 2, 0, 3)
-            .reshape(n_ten * rows, width)
-        )
-
-    w_qkv, w_out, w_up, w_down = (gathered(i) for i in range(4))
-
     mine = swap(tokens)
-    cot = swap(cotangent)
     seen = both_rows(mine)
+    sizes = [v.shape[0] for v in vectors]
+    n_vec = sum(sizes)
+    flat = jnp.concatenate(vectors)
+    small = n_chip == 4 and n_ten == 4
+    if small:
+        coarse = lax.reduce_precision(flat, 8, 7)
+        middle_bits = lax.reduce_precision(flat - coarse, 8, 7)
+        thirds = jnp.concatenate((coarse, middle_bits, flat - coarse - middle_bits)).astype(BF16)
+        came = to_other(thirds)
+        both = jnp.concatenate(
+            (jnp.where(core == 0, thirds, came), jnp.where(core == 0, came, thirds))
+        )
+        lines = -(-both.size // (16 * 2 * slab)) * 16
+        both = jnp.concatenate((both, jnp.zeros((lines * 2 * slab - both.size,), BF16)))
+        first = jnp.concatenate((shard[: bounds[1]], both.reshape(lines, 2 * slab)), axis=0)
+        blocks = layer_gather(first)
+        (w_qkv,) = assemble(chip, blocks, (3 * cols,))
+        tails = [b[:, 3 * cols :] for b in blocks]
+        tails = tails[:3] + [jnp.concatenate(tails[3:], axis=0)]
+        packed = in_chip_order(chip, tails).reshape(n_chip, n_ten, -1)[:, :, : 6 * n_vec]
+        packed = packed.reshape(n_chip, n_ten, 2, 3, n_vec).astype(F32)
+        packed = packed[:, :, :, 0] + packed[:, :, :, 1] + packed[:, :, :, 2]
+        packed = packed.transpose(0, 2, 1, 3).reshape(-1, n_vec)
+        second = after(shard[bounds[1] : bounds[3]], blocks[0])
+        blocks = layer_gather(second)
+        w_out, w_up = assemble(chip, blocks, (cols, units))
+        third = after(shard[bounds[3] :], blocks[0])
+        blocks = layer_gather(third)
+        (w_down,) = assemble(chip, blocks, (units,))
+        w_qkv, w_out, w_up, w_down = (w.reshape(-1, width) for w in (w_qkv, w_out, w_up, w_down))
+    else:
+
+        def gathered(index):
+            part = shard[bounds[index] : bounds[index + 1]]
+            rows = part.shape[0]
+            full = lax.all_gather(part, CHIPS, axis=0, tiled=False)
+            return (
+                full.reshape(n_chip, n_ten, rows, 2 * slab)
+                .transpose(1, 2, 0, 3)
+                .reshape(n_ten * rows, width)
+            )
+
+        w_qkv, w_out, w_up, w_down = (gathered(i) for i in range(4))
+        packed = lax.all_gather(flat, ALL, axis=0, tiled=False)
+    starts = [sum(sizes[:i]) for i in range(len(sizes))]
+    whole = [packed[:, s : s + n].reshape(-1) for s, n in zip(starts, sizes)]
+    gain_mid, shift_mid, bias_q, bias_v, bias_out, gain_end, shift_end, bias_up, bias_down = whole
+
+    def own_half(vector):
+        return lax.dynamic_index_in_dim(vector.reshape(n_ten, 2, -1), core, 1, keepdims=False)
+
+    bias_q, bias_v, bias_up = own_half(bias_q), own_half(bias_v), own_half(bias_up)
+    bias_qkv = jnp.stack((bias_q, jnp.zeros_like(bias_q), bias_v), axis=1).reshape(-1)
+    bias_up = bias_up.reshape(-1)
 
     joint = (nt(seen, w_qkv) + bias_qkv).astype(BF16)
+    cot = swap(after(cotangent, joint))
     context, lse = attend(joint, n_ten)
     branch = summed_rows(context, w_out, nn)
     unit_mid, inverse_mid = normalized(mine.astype(F32) + branch + bias_out)
@@ -316,20 +442,49 @@
     pre_grad = (nt(seen_second, w_down) * slope.astype(F32)).astype(BF16)
     up_bias_part = jnp.sum(pre_grad.astype(F32), axis=0)
     middle_grad = summed_rows(pre_grad, w_up, nn) + second_grad
-    down_sum = tn(hidden, seen_second)
-    up_sum = tn(pre_grad, seen_middle)
+
+    def beside(rows, columns):
+        def block(move):
+            at = lax.bitwise_xor(chip, move) * (2 * slab)
+            return tn(rows, lax.dynamic_slice_in_dim(columns, at, 2 * slab, axis=1)).astype(BF16)
+
+        return block
+
+    if small:
+        down_layer = layer_scatter(beside(hidden, seen_second))
+        down_part = lax.psum_scatter(
+            down_layer.reshape(n_ten, -1, 2 * slab), "tensor", scatter_dimension=0, tiled=False
+        )
+    else:
+        down_sum = tn(hidden, seen_second)
+        up_sum = tn(pre_grad, seen_middle)
     first_grad, mid_gain_part, mid_shift_part, out_bias_part = norm_back(
         middle_grad, unit_mid, inverse_mid, gain_mid
     )
     seen_first = both_rows(first_grad.astype(BF16))
     context_grad = nt(seen_first, w_out).astype(BF16)
-    out_sum = tn(context, seen_first)
+    if small:
+        up_block = beside(pre_grad, seen_middle)
+        out_block = beside(context, seen_first)
+        n_up = n_ten * units
+        mid_layer = layer_scatter(
+            lambda move: jnp.concatenate((up_block(move), out_block(move)), axis=0)
+        )
+        mid_layer = jnp.concatenate(
+            (
+                mid_layer[n_up:].reshape(n_ten, cols, 2 * slab),
+                mid_layer[:n_up].reshape(n_ten, units, 2 * slab),
+            ),
+            axis=1,
+        )
+        mid_part = lax.psum_scatter(mid_layer, "tensor", scatter_dimension=0, tiled=False)
+    else:
+        out_sum = tn(context, seen_first)
     qkv_low, bias_sums = attend_back(joint, context_grad, context, lse, n_ten)
-    qkv_sum = tn(qkv_low, seen)
     input_grad = summed_rows(qkv_low, w_qkv, nn) + first_grad
     input_grad = swap(input_grad.astype(BF16)).astype(F32)
 
-    def scattered(total, extra=None):
+    def scattered(total):
         rows = total.shape[0] // n_ten
         blocks = (
             total.astype(BF16)
@@ -337,8 +492,6 @@
             .transpose(2, 0, 1, 3)
             .reshape(n_chip * n_ten, rows, 2 * slab)
         )
-        if extra is not None:
-            blocks = jnp.concatenate((blocks, extra), axis=1)
         return lax.psum_scatter(blocks, CHIPS, scatter_dimension=0, tiled=False)
 
     wide = (
@@ -350,9 +503,7 @@
         down_bias_part,
     )
     narrow = (bias_sums[:, 0], bias_sums[:, 1], up_bias_part)
-    aligned = n_chip == n_ten
-    extra = None
-    if aligned:
+    if small:
         tail = []
         for vector in wide:
             tail.append(vector.reshape(n_chip, 2, n_ten, -1).transpose(0, 2, 1, 3))
@@ -366,15 +517,30 @@
         extra = jnp.concatenate(
             tail + [jnp.zeros((n_chip * n_ten, lines * 2 * slab - used), F32)], axis=1
         )
-        extra = extra.reshape(n_chip * n_ten, lines, 2 * slab).astype(BF16)
-    down_part = scattered(down_sum)
-    up_part = scattered(up_sum)
-    out_part = scattered(out_sum)
-    qkv_part = scattered(qkv_sum, extra)
-    if aligned:
+        extra = extra.reshape(n_chip, n_ten * lines, 2 * slab).astype(BF16)
+        qkv_block = beside(qkv_low, seen)
+
+        def last_block(move):
+            owner = lax.bitwise_xor(chip, move)
+            mark = lax.dynamic_index_in_dim(extra, owner, 0, keepdims=False)
+            return jnp.concatenate((qkv_block(move), mark), axis=0)
+
+        last = layer_scatter(last_block)
+        n_qkv = 3 * n_ten * cols
+        last = jnp.concatenate(
+            (
+                last[:n_qkv].reshape(n_ten, 3 * cols, 2 * slab),
+                last[n_qkv:].reshape(n_ten, lines, 2 * slab),
+            ),
+            axis=1,
+        )
+        qkv_part = lax.psum_scatter(last, "tensor", scatter_dimension=0, tiled=False)
         vector_line = qkv_part[3 * cols :].reshape(-1).astype(F32)
         qkv_part = qkv_part[: 3 * cols]
-    parts = jnp.concatenate((qkv_part, out_part, up_part, down_part), axis=0)
+        parts = jnp.concatenate((qkv_part, mid_part, down_part), axis=0)
+    else:
+        qkv_sum = tn(qkv_low, seen)
+        parts = jnp.concatenate([scattered(t) for t in (qkv_sum, out_sum, up_sum, down_sum)], axis=0)
     parts = parts.reshape(-1, 2, slab)
     keep = lax.dynamic_index_in_dim(parts, core, 1, keepdims=False)
     came = to_other(lax.dynamic_index_in_dim(parts, 1 - core, 1, keepdims=False))
@@ -389,7 +555,7 @@
     up_out = cut[2].reshape(2 * units, slab).T
     down_out = cut[3].reshape(2 * units, slab)
 
-    if aligned:
+    if small:
         n_wide = sum(tail_sizes[:6])
         doubled = vector_line[:n_wide].reshape(6, 2, -1)
         own = lax.dynamic_index_in_dim(doubled, core, 1, keepdims=False)

time: 779 us -> 488 us (0.63)
  waiting for transfers between devices: 414 us -> 128 us
  starting transfers between devices: 35.1 us -> 91 us
  local copies, waits for them, and re-layouts: 83.2 us -> 31.7 us
  blocking collectives: 70.2 us -> 21.5 us
  matrix products: 83.1 us -> 99.6 us
  Pallas kernels: 55.9 us -> 70.9 us
  other arithmetic: 14.2 us -> 23.7 us
    reduce_scatter x4 -> x3, waiting for transfers between devices: 270 us -> 0.02 us  [the longest x1 0.02 us: on_device(): lax.psum_scatter(mid_layer, 'tensor', scatter_dimension=0, tiled=False)]
    all_gather x4 -> x2, waiting for transfers between devices: 130 us -> 11.5 us  [layer_gather(): own = lax.all_gather(part, 'tensor', axis=0, tiled=False)]
    ppermute x0 -> x24, waiting for transfers between devices: none -> 113 us  [to_chip(): return lax.ppermute(value, 'chip', [(i, i ^ move) for i in range(4)])]
    all_gather x1, blocking collectives: 70.2 us -> 21.5 us  [layer_gather(): own = lax.all_gather(part, 'tensor', axis=0, tiled=False)]
    reshape x8 -> x4, local copies, waits for them, and re-layouts: 33.9 us -> 1.3 us  [the longest x2 1.27 us: on_device(): cut[0].reshape(2, 3, cols, slab).transpose(3, 1, 0, 2)]
    ppermute x0 -> x24, starting transfers between devices: none -> 28.4 us  [to_chip(): return lax.ppermute(value, 'chip', [(i, i ^ move) for i in range(4)])]
    transpose x5 -> x0, local copies, waits for them, and re-layouts: 17.2 us -> none  [the longest x4 17.2 us: gathered(): return full.reshape(n_chip, n_ten, rows, 2 * slab).transpose(1, 2, 0, 3)....]
    ppermute x4, starting transfers between devices: 6.11 us -> 23.2 us  [on_device(): swap = lambda value: lax.ppermute(value, ('core', 'tensor'), pairs)]
  transfers between devices with their start and end apart: 23 -> 45, of which waited for: 14 -> 19; matrix products, arithmetic and copies ran while one was open for 16% -> 25% of each run, Pallas kernels for 7% -> 15%
where the time goes in v2:
time: 488 us; the launch traced here: 482 us
  waiting for transfers between devices  128 us (26%)
  matrix products  99.6 us (20%)
  starting transfers between devices  91 us (19%)
  Pallas kernels  70.9 us (15%)
  local copies, waits for them, and re-layouts  31.7 us (6%)
  other arithmetic  23.7 us (5%)
  blocking collectives  21.5 us (4%)
  between operations  15.4 us (3%)
    ppermute x24, waiting for transfers between devices, to_chip(): return lax.ppermute(value, 'chip', [(i, i ^ move) for i in range(4)])  113 us
    dot_general x16, matrix products, tn(): lax.dot_general(left, right, (((0,), (0,)), ((), ())), preferred_element_...  39.8 us
    ppermute x12, starting transfers between devices, to_other(): return lax.ppermute(value, 'core', [(0, 1), (1, 0)])  38.6 us
    dot_general x4, matrix products, nt(): lax.dot_general(left, right, (((1,), (1,)), ((), ())), preferred_element_...  30.9 us
    dot_general x8, matrix products, nn(): lax.dot_general(left, right, (((1,), (0,)), ((), ())), preferred_element_...  28.9 us
    ppermute x24, starting transfers between devices, to_chip(): return lax.ppermute(value, 'chip', [(i, i ^ move) for i in range(4)])  28.4 us
    pallas_call x1, Pallas kernels, attend_back(): pl.pallas_call(attend_back_kernel, grid=(groups,), in_specs=[part(0), par...  28.2 us
    pallas_call x1, Pallas kernels, attend(): pl.pallas_call(attend_kernel, grid=(groups,), in_specs=[part(0), part(1),...  27.8 us
  transfers between devices with their start and end apart: 45, of which 19 were waited for; matrix products, arithmetic and copies ran while one was open for 25% of the time, Pallas kernels for 15%

profile of v2, /device:TPU:0, one launch (start us, length us, event | category | flops | bytes accessed | tf_op | source)
XLA Modules:
  0.0 481.6 jit_solution(4802273157057202141)
XLA Ops:
  12.8 21.5 %all-gather = bf16[1600,256]{1,0:T(8,128)(2,1)S(1)} all-gather(bf16[400,256]{1,0:T(8,128)(2,1)S(1)} %fusion.88), channel_id=2, replica_groups=mesh['chip'=4,'core'=2,'tensor'=4] {'tensor'}, dimensions={0}, use_global_device_ids=true | all-gather | bytes 1024000 | tf_op jit(solution)/shard_map/all_gather | solution.py:267
  37.3 9.5 %collective-permute-start = (bf16[512,1024]{1,0:T(8,128)(2,1)}, bf16[512,1024]{1,0:T(8,128)(2,1)}, u32[]{:S(2)}, u32[]{:S(2)}) collective-permute-start(bf16[512,1024]{1,0:T(8,128)(2,1)} %param.15), channel_id=1, source_target_pairs={{0,0},{4,1},{1,4},{5,5},{2,2},{6,3},{3,6},{7,7},{8,8},{12,9},{9,12... | collective-permute-start | bytes 3145736 | tf_op jit(solution)/shard_map/ppermute | solution.py:338
  47.6 4.9 %collective-permute-done.5.y_ref = bf16[4,400,256]{2,1,0:T(8,128)(2,1)S(1)} collective-permute-done((bf16[4,400,256]{2,1,0:T(8,128)(2,1)S(1)}, bf16[4,400,256]{2,1,0:T(8,128)(2,1)S(1)}, u32[]{:S(2)}, u32[]{:S(2)}) %collective-permute-start.5) | collective-permute-done | bytes 819232 | tf_op jit(solution)/shard_map/ppermute | solution.py:259
  65.5 11.5 %all-gather.6.cloned.1.call-done = bf16[2560,256]{1,0:T(8,128)(2,1)} async-done(((bf16[640,256]{1,0:T(8,128)(2,1)}), bf16[2560,256]{1,0:T(8,128)(2,1)}) %all-gather.6.cloned.1.call-update) | async-done | bytes 1310736 | tf_op jit(solution)/shard_map/all_gather | solution.py:267
  80.0 4.7 assemble.3
  87.4 6.7 %add_convert_fusion.q_ref.k_ref.v_ref = bf16[1024,1536]{1,0:T(8,128)(2,1)} fusion(bf16[1024,1024]{1,0:T(8,128)(2,1)S(1)} %constant_dynamic-update-slice_fusion, bf16[1536,1024]{1,0:T(8,128)(2,1)} %bitcast.128, f32[1536]{0:T(1024)S(1)} %add.225), kind=kOutput, calls=%fused_computation.9 | convolution fusion | flops 3224371200 | bytes 8394752 | tf_op jit(solution)/shard_map/dot_general | solution.py:25
  94.5 12.6 %collective-permute-done.9.y_ref = bf16[4,640,256]{2,1,0:T(8,128)(2,1)S(1)} collective-permute-done((bf16[4,640,256]{2,1,0:T(8,128)(2,1)}, bf16[4,640,256]{2,1,0:T(8,128)(2,1)S(1)}, u32[]{:S(2)}, u32[]{:S(2)}) %collective-permute-start.9) | collective-permute-done | bytes 1310752 | tf_op jit(solution)/shard_map/ppermute | solution.py:259
  110.2 27.8 %attend.1 = (bf16[1024,512]{1,0:T(8,128)(2,1)}, f32[4,2,1024]{2,1,0:T(2,128)}) custom-call(bf16[1024,1536]{1,0:T(8,128)(2,1)} %add_convert_fusion.q_ref.k_ref.v_ref, bf16[1024,1536]{1,0:T(8,128)(2,1)} %add_convert_fusion.q_ref.k_ref.v_ref, bf16[1024,1536]{1,0:T(8,128)(2,1)} %add_convert_fusion.q_ref.k_ref.v_ref), custom_call_target="tpu_custom_call" | custom-call | flops 8589934592 | bytes 4194304 | tf_op jit(solution)/shard_map/attend/pallas_call | solution.py:73
  139.8 5.5 %assemble.4 = (bf16[4,128,1024]{2,1,0:T(8,128)(2,1)}, bf16[4,512,1024]{2,1,0:T(8,128)(2,1)}) custom-call(s32[1]{0:T(128)} %bitcast.chip_ref, bf16[4,640,256]{2,1,0:T(8,128)(2,1)} %bitcast.137, bf16[4,640,256]{2,1,0:T(8,128)(2,1)} %copy-done.8, bf16[4,640,256]{2,1,0:T(8,128)(2,1)} %copy-done.7, bf16[2,640,256]{2,1,0:T(8,128)(2,1)} %copy-done.21, ...), custom_call_target="tpu_custom_call" | custom-call | bytes 10485760 | tf_op jit(solution)/shard_map/assemble/pallas_call | solution.py:235
  150.0 2.9 fusion.129
  154.9 18.4 %collective-permute-done.15.y_ref = bf16[4,512,256]{2,1,0:T(8,128)(2,1)S(1)} collective-permute-done((bf16[4,512,256]{2,1,0:T(8,128)(2,1)}, bf16[4,512,256]{2,1,0:T(8,128)(2,1)S(1)}, u32[]{:S(2)}, u32[]{:S(2)}) %collective-permute-start.15) | collective-permute-done | bytes 1048608 | tf_op jit(solution)/shard_map/ppermute | solution.py:259
  177.7 10.2 %collective-permute-done.16.low_ref = bf16[2,512,256]{2,1,0:T(8,128)(2,1)} collective-permute-done((bf16[2,512,256]{2,1,0:T(8,128)(2,1)}, bf16[2,512,256]{2,1,0:T(8,128)(2,1)}, u32[]{:S(2)}, u32[]{:S(2)}) %collective-permute-start.16) | collective-permute-done | bytes 524320 | tf_op jit(solution)/shard_map/ppermute | solution.py:259
  190.1 4.8 %assemble.5 = bf16[4,512,1024]{2,1,0:T(8,128)(2,1)} custom-call(s32[1]{0:T(128)} %bitcast.chip_ref, bf16[4,512,256]{2,1,0:T(8,128)(2,1)} %bitcast.140, bf16[4,512,256]{2,1,0:T(8,128)(2,1)} %copy-done.12, bf16[4,512,256]{2,1,0:T(8,128)(2,1)} %copy-done.11, bf16[2,512,256]{2,1,0:T(8,128)(2,1)} %collective-permute-done.16.low_ref, ...), custom_call_target="tpu_custom_call" | custom-call | bytes 8388608 | tf_op jit(solution)/shard_map/assemble/pallas_call | solution.py:235
  194.9 9.0 %multiply_convert_fusion.1 = (bf16[1024,2048]{1,0:T(8,128)(2,1)S(1)}, f32[1024,2048]{1,0:T(8,128)}) fusion(f32[2048]{0:T(1024)S(1)} %bitcast.162, bf16[2048,1024]{1,0:T(8,128)(2,1)S(1)} %bitcast.166, bf16[512,1024]{1,0:T(8,128)(2,1)} %collective-permute-done.13, bf16[512,1024]{1,0:T(8,128)(2,1)} %fusion.27), kind=kOutput, calls=%fused_computation.7 | convolution fusion | flops 4311744512 | bytes 18882560 | tf_op jit(solution)/shard_map/dot_general | solution.py:25
  203.9 3.3 fusion.41
  210.2 5.8 %fusion.130 = (f32[512]{0:T(512)S(1)}, f32[512,1024]{1,0:T(8,128)S(1)}) fusion(f32[1024]{0:T(1024)S(1)} %add.244, bf16[512,1024]{1,0:T(8,128)(2,1)} %collective-permute-done.18, bf16[2048,1024]{1,0:T(8,128)(2,1)} %bitcast.119, bf16[1024,2048]{1,0:T(8,128)(2,1)} %copy-done.41, f32[1024]{0:T(1024)S(1)} %add.234, f32[1024]{0:T(1024)S(1)} %mul.157, ...), kind=kOutput, calls=%fused_computation.259 | convolution fusion | flops 2152201728 | bytes 11552768 | tf_op jit(solution)/shard_map/dot_general | solution.py:29
  221.6 7.9 %collective-permute-start.21 = (bf16[512,1024]{1,0:T(8,128)(2,1)}, bf16[512,1024]{1,0:T(8,128)(2,1)}, u32[]{:S(2)}, u32[]{:S(2)}) collective-permute-start(bf16[512,1024]{1,0:T(8,128)(2,1)} %convert_element_type.243), channel_id=1, source_target_pairs={{0,4},{4,0},{1,5},{5,1},{2,6},{6,2},{3,7},{7,3},{8,12},{12,8},{9,1... | collective-permute-start | bytes 3145736 | tf_op jit(solution)/shard_map/ppermute | solution.py:197
  230.2 9.5 %collective-permute-start.19 = (bf16[512,1024]{1,0:T(8,128)(2,1)}, bf16[512,1024]{1,0:T(8,128)(2,1)}, u32[]{:S(2)}, u32[]{:S(2)}) collective-permute-start(bf16[512,1024]{1,0:T(8,128)(2,1)} %get-tuple-element.49), channel_id=1, source_target_pairs={{0,0},{4,1},{1,4},{5,5},{2,2},{6,3},{3,6},{7,7},{8,8},{12,9},{9,12... | collective-permute-start | bytes 3145736 | tf_op jit(solution)/shard_map/ppermute | solution.py:338
  239.7 11.3 %fusion.131 = (bf16[2048]{0:T(1024)(128)(2,1)S(1)}, bf16[1024,2048]{1,0:T(8,128)(2,1)S(1)}) fusion(f32[1024,2048]{1,0:T(8,128)} %get-tuple-element.94, f32[2048]{0:T(1024)S(1)} %bitcast.163, bf16[2048,1024]{1,0:T(8,128)(2,1)} %bitcast.120, bf16[512,1024]{1,0:T(8,128)(2,1)} %collective-permute-done.21, bf16[512,1024]{1,0:T(8,128)(2,1)} %convert_element_type.243), kind=kOutput, calls=%fused_computation.260 | convolution fusion | flops 4328519680 | bytes 18886656 | tf_op jit(solution)/shard_map/dot_general | solution.py:25
  272.8 3.0 multiply_reduce_fusion
  279.9 3.4 convolution_convert_fusion.7
  283.8 11.6 %collective-permute-done.37 = bf16[2048,256]{1,0:T(8,128)(2,1)} collective-permute-done((bf16[2048,256]{1,0:T(8,128)(2,1)}, bf16[2048,256]{1,0:T(8,128)(2,1)}, u32[]{:S(2)}, u32[]{:S(2)}) %collective-permute-start.37) | collective-permute-done | bytes 1048608 | tf_op jit(solution)/shard_map/ppermute | solution.py:259
  297.8 5.4 %fusion.12 = bf16[2048,256]{1,0:T(8,128)(2,1)} fusion(bf16[1024,2048]{1,0:T(8,128)(2,1)} %copy-done.41, bf16[2048,256]{1,0:T(8,128)(2,1)} %collective-permute-done.37, bf16[2048,256]{1,0:T(8,128)(2,1)} %collective-permute-done.35, s32[]{:T(128)S(6)} %select_n.143, bf16[512,1024]{1,0:T(8,128)(2,1)} %convert_element_type.243, ...), kind=kOutput, calls=%fused_computation.52 | convolution fusion | flops 1078460416 | bytes 9437188 | tf_op jit(solution)/shard_map/dot_general | solution.py:33
  303.3 3.9 fusion.40.g_ref
  307.2 28.2 %attend_back.1 = (bf16[1024,1536]{1,0:T(8,128)(2,1)}, f32[4,2,128]{2,1,0:T(2,128)}) custom-call(bf16[1024,1536]{1,0:T(8,128)(2,1)} %add_convert_fusion.q_ref.k_ref.v_ref, bf16[1024,1536]{1,0:T(8,128)(2,1)} %add_convert_fusion.q_ref.k_ref.v_ref, bf16[1024,1536]{1,0:T(8,128)(2,1)} %add_convert_fusion.q_ref.k_ref.v_ref, bf16[1024,512]{1,0:T(8,128)(2,1)} %fusion.40.g_ref, ...), custom_call_target="tpu_custom_call" | custom-call | flops 21474836480 | bytes 8388608 | tf_op jit(solution)/shard_map/attend_back/pallas_call | solution.py:141
  335.4 4.0 convolution_convert_fusion.8
  354.8 15.3 %collective-permute-done.28 = bf16[800,256]{1,0:T(8,128)(2,1)S(1)} collective-permute-done((bf16[800,256]{1,0:T(8,128)(2,1)S(1)}, bf16[800,256]{1,0:T(8,128)(2,1)S(1)}, u32[]{:S(2)}, u32[]{:S(2)}) %collective-permute-start.28) | collective-permute-done | bytes 409632 | tf_op jit(solution)/shard_map/ppermute | solution.py:259
  378.0 13.5 %collective-permute-done.29 = bf16[1600,256]{1,0:T(8,128)(2,1)S(1)} collective-permute-done((bf16[1600,256]{1,0:T(8,128)(2,1)S(1)}, bf16[1600,256]{1,0:T(8,128)(2,1)S(1)}, u32[]{:S(2)}, u32[]{:S(2)}) %collective-permute-start.29) | collective-permute-done | bytes 819232 | tf_op jit(solution)/shard_map/ppermute | solution.py:259
  395.9 4.4 fusion.37
  401.9 15.0 %collective-permute-done.33 = bf16[2560,256]{1,0:T(8,128)(2,1)} collective-permute-done((bf16[2560,256]{1,0:T(8,128)(2,1)}, bf16[2560,256]{1,0:T(8,128)(2,1)}, u32[]{:S(2)}, u32[]{:S(2)}) %collective-permute-start.33) | collective-permute-done | bytes 1310752 | tf_op jit(solution)/shard_map/ppermute | solution.py:259
  422.9 5.1 %add_convert_fusion.2 = bf16[512,1024]{1,0:T(8,128)(2,1)} fusion(f32[512,1024]{1,0:T(8,128)S(1)} %copy-done.1, bf16[512,1024]{1,0:T(8,128)(2,1)S(1)} %collective-permute-done.24, bf16[1536,1024]{1,0:T(8,128)(2,1)} %bitcast.129, bf16[1024,1536]{1,0:T(8,128)(2,1)} %get-tuple-element.31), kind=kOutput, calls=%fused_computation.76 | convolution fusion | flops 1612709888 | bytes 8912896 | tf_op jit(solution)/shard_map/dot_general | solution.py:29
  435.0 29.7 %collective-permute-start.39 = (f32[6,32]{1,0:T(8,128)S(1)}, f32[6,32]{1,0:T(8,128)S(1)}, u32[]{:S(2)}, u32[]{:S(2)}) collective-permute-start(f32[6,32]{1,0:T(8,128)S(1)} %bitcast.165), channel_id=1, source_target_pairs={{0,4},{4,0},{1,5},{5,1},{2,6},{6,2},{3,7},{7,3},{8,12},{12,8},{9,1... | collective-permute-start | bytes 2312 | tf_op jit(solution)/shard_map/ppermute | solution.py:197
  (338 shorter events, 135.9 us)
Async XLA Ops:
  7.3 69.7 %all-gather.6.cloned.1.call-start = ((), (), s32[]{:S(2)}) async-start(), calls=%async_computation.6 | async-start | bytes 1638400 | tf_op jit(solution)/shard_map/all_gather | solution.py:267
  34.3 18.2 %collective-permute-start.5 = (bf16[4,400,256]{2,1,0:T(8,128)(2,1)S(1)}, bf16[4,400,256]{2,1,0:T(8,128)(2,1)S(1)}, u32[]{:S(2)}, u32[]{:S(2)}) collective-permute-start(bf16[4,400,256]{2,1,0:T(8,128)(2,1)S(1)} %bitcast.123), channel_id=1, source_target_pairs={{0,16},{8,24},{16,0},{24,8},{1,17},{9,25},{17,1},{25,9},{2,18},{10... | collective-permute-start | bytes 2457608 | tf_op jit(solution)/shard_map/ppermute | solution.py:259
  35.8 19.0 %collective-permute-start.4 = (bf16[4,400,256]{2,1,0:T(8,128)(2,1)S(1)}, bf16[4,400,256]{2,1,0:T(8,128)(2,1)S(1)}, u32[]{:S(2)}, u32[]{:S(2)}) collective-permute-start(bf16[4,400,256]{2,1,0:T(8,128)(2,1)S(1)} %bitcast.124), channel_id=1, source_target_pairs={{0,8},{8,0},{16,24},{24,16},{1,9},{9,1},{17,25},{25,17},{2,10},{10... | collective-permute-start | bytes 2457608 | tf_op jit(solution)/shard_map/ppermute | solution.py:259
  37.3 20.7 %collective-permute-start = (bf16[512,1024]{1,0:T(8,128)(2,1)}, bf16[512,1024]{1,0:T(8,128)(2,1)}, u32[]{:S(2)}, u32[]{:S(2)}) collective-permute-start(bf16[512,1024]{1,0:T(8,128)(2,1)} %param.15), channel_id=1, source_target_pairs={{0,0},{4,1},{1,4},{5,5},{2,2},{6,3},{3,6},{7,7},{8,8},{12,9},{9,12... | collective-permute-start | bytes 3145736 | tf_op jit(solution)/shard_map/ppermute | solution.py:338
  47.5 99.9 %all-gather.8.cloned.1.call-start = ((), (), s32[]{:S(2)}) async-start(), calls=%async_computation.7 | async-start | bytes 1310720 | tf_op jit(solution)/shard_map/all_gather | solution.py:267
  58.0 26.7 %collective-permute-start.1 = (bf16[512,1024]{1,0:T(8,128)(2,1)}, bf16[512,1024]{1,0:T(8,128)(2,1)}, u32[]{:S(2)}, u32[]{:S(2)}) collective-permute-start(bf16[512,1024]{1,0:T(8,128)(2,1)} %collective-permute-done), channel_id=1, source_target_pairs={{0,4},{4,0},{1,5},{5,1},{2,6},{6,2},{3,7},{7,3},{8,12},{12,8},{9,1... | collective-permute-start | bytes 3145736 | tf_op jit(solution)/shard_map/ppermute | solution.py:197
  77.0 30.1 %collective-permute-start.9 = (bf16[4,640,256]{2,1,0:T(8,128)(2,1)}, bf16[4,640,256]{2,1,0:T(8,128)(2,1)S(1)}, u32[]{:S(2)}, u32[]{:S(2)}) collective-permute-start(bf16[4,640,256]{2,1,0:T(8,128)(2,1)} %bitcast.135), channel_id=1, source_target_pairs={{0,16},{8,24},{16,0},{24,8},{1,17},{9,25},{17,1},{25,9},{2,18},{10... | collective-permute-start | bytes 3932168 | tf_op jit(solution)/shard_map/ppermute | solution.py:259
  78.5 30.2 %collective-permute-start.8 = (bf16[4,640,256]{2,1,0:T(8,128)(2,1)}, bf16[4,640,256]{2,1,0:T(8,128)(2,1)S(1)}, u32[]{:S(2)}, u32[]{:S(2)}) collective-permute-start(bf16[4,640,256]{2,1,0:T(8,128)(2,1)} %bitcast.136), channel_id=1, source_target_pairs={{0,8},{8,0},{16,24},{24,16},{1,9},{9,1},{17,25},{25,17},{2,10},{10... | collective-permute-start | bytes 3932168 | tf_op jit(solution)/shard_map/ppermute | solution.py:259
  94.2 335.8 %reduce-scatter.8.cloned.1.call-start = ((), (), s32[]{:S(2)}) async-start(), calls=%async_computation.5 | async-start | bytes 1310720 | tf_op jit(solution)/shard_map/reduce_scatter | solution.py:455
  107.1 31.0 %collective-permute-start.10 = (bf16[2,640,256]{2,1,0:T(8,128)(2,1)S(1)}, bf16[2,640,256]{2,1,0:T(8,128)(2,1)S(1)}, u32[]{:S(2)}, u32[]{:S(2)}) collective-permute-start(bf16[2,640,256]{2,1,0:T(8,128)(2,1)S(1)} %slice.325), channel_id=1, source_target_pairs={{0,8},{8,0},{16,24},{24,16},{1,9},{9,1},{17,25},{25,17},{2,10},{10... | collective-permute-start | bytes 1966088 | tf_op jit(solution)/shard_map/ppermute | solution.py:259
  108.7 29.4 %collective-permute-start.11 = (bf16[2,640,256]{2,1,0:T(8,128)(2,1)S(1)}, bf16[2,640,256]{2,1,0:T(8,128)(2,1)S(1)}, u32[]{:S(2)}, u32[]{:S(2)}) collective-permute-start(bf16[2,640,256]{2,1,0:T(8,128)(2,1)S(1)} %slice.326), channel_id=1, source_target_pairs={{0,16},{8,24},{16,0},{24,8},{1,17},{9,25},{17,1},{25,9},{2,18},{10... | collective-permute-start | bytes 1966088 | tf_op jit(solution)/shard_map/ppermute | solution.py:259
  147.5 25.8 %collective-permute-start.15 = (bf16[4,512,256]{2,1,0:T(8,128)(2,1)}, bf16[4,512,256]{2,1,0:T(8,128)(2,1)S(1)}, u32[]{:S(2)}, u32[]{:S(2)}) collective-permute-start(bf16[4,512,256]{2,1,0:T(8,128)(2,1)} %bitcast.138), channel_id=1, source_target_pairs={{0,16},{8,24},{16,0},{24,8},{1,17},{9,25},{17,1},{25,9},{2,18},{10... | collective-permute-start | bytes 3145736 | tf_op jit(solution)/shard_map/ppermute | solution.py:259
  148.0 26.7 %collective-permute-start.14 = (bf16[4,512,256]{2,1,0:T(8,128)(2,1)}, bf16[4,512,256]{2,1,0:T(8,128)(2,1)S(1)}, u32[]{:S(2)}, u32[]{:S(2)}) collective-permute-start(bf16[4,512,256]{2,1,0:T(8,128)(2,1)} %bitcast.139), channel_id=1, source_target_pairs={{0,8},{8,0},{16,24},{24,16},{1,9},{9,1},{17,25},{25,17},{2,10},{10... | collective-permute-start | bytes 3145736 | tf_op jit(solution)/shard_map/ppermute | solution.py:259
  154.7 40.2 %collective-permute-start.13 = (bf16[512,1024]{1,0:T(8,128)(2,1)}, bf16[512,1024]{1,0:T(8,128)(2,1)}, u32[]{:S(2)}, u32[]{:S(2)}) collective-permute-start(bf16[512,1024]{1,0:T(8,128)(2,1)} %fusion.27), channel_id=1, source_target_pairs={{0,4},{4,0},{1,5},{5,1},{2,6},{6,2},{3,7},{7,3},{8,12},{12,8},{9,1... | collective-permute-start | bytes 3145736 | tf_op jit(solution)/shard_map/ppermute | solution.py:197
  221.6 18.1 %collective-permute-start.21 = (bf16[512,1024]{1,0:T(8,128)(2,1)}, bf16[512,1024]{1,0:T(8,128)(2,1)}, u32[]{:S(2)}, u32[]{:S(2)}) collective-permute-start(bf16[512,1024]{1,0:T(8,128)(2,1)} %convert_element_type.243), channel_id=1, source_target_pairs={{0,4},{4,0},{1,5},{5,1},{2,6},{6,2},{3,7},{7,3},{8,12},{12,8},{9,1... | collective-permute-start | bytes 3145736 | tf_op jit(solution)/shard_map/ppermute | solution.py:197
  230.2 199.8 %collective-permute-start.19 = (bf16[512,1024]{1,0:T(8,128)(2,1)}, bf16[512,1024]{1,0:T(8,128)(2,1)}, u32[]{:S(2)}, u32[]{:S(2)}) collective-permute-start(bf16[512,1024]{1,0:T(8,128)(2,1)} %get-tuple-element.49), channel_id=1, source_target_pairs={{0,0},{4,1},{1,4},{5,5},{2,2},{6,3},{3,6},{7,7},{8,8},{12,9},{9,12... | collective-permute-start | bytes 3145736 | tf_op jit(solution)/shard_map/ppermute | solution.py:338
  256.0 15.0 %collective-permute-start.34 = (bf16[1024,256]{1,0:T(8,128)(2,1)S(1)}, bf16[1024,256]{1,0:T(8,128)(2,1)S(1)}, u32[]{:S(2)}, u32[]{:S(2)}) collective-permute-start(bf16[1024,256]{1,0:T(8,128)(2,1)S(1)} %get-tuple-element.56), channel_id=1, source_target_pairs={{0,16},{8,24},{16,0},{24,8},{1,17},{9,25},{17,1},{25,9},{2,18},{10... | collective-permute-start | bytes 1572872 | tf_op jit(solution)/shard_map/ppermute | solution.py:259
  269.5 25.9 %collective-permute-start.37 = (bf16[2048,256]{1,0:T(8,128)(2,1)}, bf16[2048,256]{1,0:T(8,128)(2,1)}, u32[]{:S(2)}, u32[]{:S(2)}) collective-permute-start(bf16[2048,256]{1,0:T(8,128)(2,1)} %pad_maximum_fusion.11), channel_id=1, source_target_pairs={{0,16},{8,24},{16,0},{24,8},{1,17},{9,25},{17,1},{25,9},{2,18},{10... | collective-permute-start | bytes 3145736 | tf_op jit(solution)/shard_map/ppermute | solution.py:259
  272.2 25.6 %collective-permute-start.35 = (bf16[2048,256]{1,0:T(8,128)(2,1)}, bf16[2048,256]{1,0:T(8,128)(2,1)}, u32[]{:S(2)}, u32[]{:S(2)}) collective-permute-start(bf16[2048,256]{1,0:T(8,128)(2,1)} %pad_maximum_fusion.10), channel_id=1, source_target_pairs={{0,8},{8,0},{16,24},{24,16},{1,9},{9,1},{17,25},{25,17},{2,10},{10... | collective-permute-start | bytes 3145736 | tf_op jit(solution)/shard_map/ppermute | solution.py:259
  276.9 26.4 %collective-permute-start.23 = (bf16[512,1024]{1,0:T(8,128)(2,1)S(1)}, bf16[512,1024]{1,0:T(8,128)(2,1)}, u32[]{:S(2)}, u32[]{:S(2)}) collective-permute-start(bf16[512,1024]{1,0:T(8,128)(2,1)S(1)} %convert_element_type.249), channel_id=1, source_target_pairs={{0,4},{4,0},{1,5},{5,1},{2,6},{6,2},{3,7},{7,3},{8,12},{12,8},{9,1... | collective-permute-start | bytes 3145736 | tf_op jit(solution)/shard_map/ppermute | solution.py:197
  303.2 129.3 %reduce-scatter.4.cloned.1.call-start = ((), (), s32[]{:S(2)}) async-start(), calls=%async_computation.3 | async-start | bytes 1024000 | tf_op jit(solution)/shard_map/reduce_scatter | solution.py:537
  345.0 30.2 %collective-permute-start.30 = (bf16[1280,256]{1,0:T(8,128)(2,1)S(1)}, bf16[1280,256]{1,0:T(8,128)(2,1)S(1)}, u32[]{:S(2)}, u32[]{:S(2)}) collective-permute-start(bf16[1280,256]{1,0:T(8,128)(2,1)S(1)} %get-tuple-element.58), channel_id=1, source_target_pairs={{0,16},{8,24},{16,0},{24,8},{1,17},{9,25},{17,1},{25,9},{2,18},{10... | collective-permute-start | bytes 1966088 | tf_op jit(solution)/shard_map/ppermute | solution.py:259
  345.5 27.1 %collective-permute-start.32 = (bf16[1280,256]{1,0:T(8,128)(2,1)S(1)}, bf16[1280,256]{1,0:T(8,128)(2,1)S(1)}, u32[]{:S(2)}, u32[]{:S(2)}) collective-permute-start(bf16[1280,256]{1,0:T(8,128)(2,1)S(1)} %get-tuple-element.59), channel_id=1, source_target_pairs={{0,8},{8,0},{16,24},{24,16},{1,9},{9,1},{17,25},{25,17},{2,10},{10... | collective-permute-start | bytes 1966088 | tf_op jit(solution)/shard_map/ppermute | solution.py:259
  346.8 25.1 %collective-permute-start.26 = (bf16[800,256]{1,0:T(8,128)(2,1)S(1)}, bf16[800,256]{1,0:T(8,128)(2,1)S(1)}, u32[]{:S(2)}, u32[]{:S(2)}) collective-permute-start(bf16[800,256]{1,0:T(8,128)(2,1)S(1)} %get-tuple-element.60), channel_id=1, source_target_pairs={{0,16},{8,24},{16,0},{24,8},{1,17},{9,25},{17,1},{25,9},{2,18},{10... | collective-permute-start | bytes 1228808 | tf_op jit(solution)/shard_map/ppermute | solution.py:259
  347.8 22.3 %collective-permute-start.28 = (bf16[800,256]{1,0:T(8,128)(2,1)S(1)}, bf16[800,256]{1,0:T(8,128)(2,1)S(1)}, u32[]{:S(2)}, u32[]{:S(2)}) collective-permute-start(bf16[800,256]{1,0:T(8,128)(2,1)S(1)} %get-tuple-element.61), channel_id=1, source_target_pairs={{0,8},{8,0},{16,24},{24,16},{1,9},{9,1},{17,25},{25,17},{2,10},{10... | collective-permute-start | bytes 1228808 | tf_op jit(solution)/shard_map/ppermute | solution.py:259
  370.2 21.2 %collective-permute-start.29 = (bf16[1600,256]{1,0:T(8,128)(2,1)S(1)}, bf16[1600,256]{1,0:T(8,128)(2,1)S(1)}, u32[]{:S(2)}, u32[]{:S(2)}) collective-permute-start(bf16[1600,256]{1,0:T(8,128)(2,1)S(1)} %fusion.52), channel_id=1, source_target_pairs={{0,16},{8,24},{16,0},{24,8},{1,17},{9,25},{17,1},{25,9},{2,18},{10... | collective-permute-start | bytes 2457608 | tf_op jit(solution)/shard_map/ppermute | solution.py:259
  372.1 21.2 %collective-permute-start.27 = (bf16[1600,256]{1,0:T(8,128)(2,1)S(1)}, bf16[1600,256]{1,0:T(8,128)(2,1)S(1)}, u32[]{:S(2)}, u32[]{:S(2)}) collective-permute-start(bf16[1600,256]{1,0:T(8,128)(2,1)S(1)} %pad_maximum_fusion.12), channel_id=1, source_target_pairs={{0,8},{8,0},{16,24},{24,16},{1,9},{9,1},{17,25},{25,17},{2,10},{10... | collective-permute-start | bytes 2457608 | tf_op jit(solution)/shard_map/ppermute | solution.py:259
  374.0 42.8 %collective-permute-start.33 = (bf16[2560,256]{1,0:T(8,128)(2,1)}, bf16[2560,256]{1,0:T(8,128)(2,1)}, u32[]{:S(2)}, u32[]{:S(2)}) collective-permute-start(bf16[2560,256]{1,0:T(8,128)(2,1)} %fusion.48), channel_id=1, source_target_pairs={{0,16},{8,24},{16,0},{24,8},{1,17},{9,25},{17,1},{25,9},{2,18},{10... | collective-permute-start | bytes 3932168 | tf_op jit(solution)/shard_map/ppermute | solution.py:259
  376.6 41.8 %collective-permute-start.31 = (bf16[2560,256]{1,0:T(8,128)(2,1)}, bf16[2560,256]{1,0:T(8,128)(2,1)}, u32[]{:S(2)}, u32[]{:S(2)}) collective-permute-start(bf16[2560,256]{1,0:T(8,128)(2,1)} %pad_maximum_fusion.8), channel_id=1, source_target_pairs={{0,8},{8,0},{16,24},{24,16},{1,9},{9,1},{17,25},{25,17},{2,10},{10... | collective-permute-start | bytes 3932168 | tf_op jit(solution)/shard_map/ppermute | solution.py:259
  394.7 70.5 %reduce-scatter.6.cloned.1.call-start = ((), (), s32[]{:S(2)}) async-start(), calls=%async_computation.4 | async-start | bytes 1638400 | tf_op jit(solution)/shard_map/reduce_scatter | solution.py:480
  400.3 21.8 %collective-permute-start.24 = (bf16[512,1024]{1,0:T(8,128)(2,1)}, bf16[512,1024]{1,0:T(8,128)(2,1)S(1)}, u32[]{:S(2)}, u32[]{:S(2)}) collective-permute-start(bf16[512,1024]{1,0:T(8,128)(2,1)} %fusion.37), channel_id=1, source_target_pairs={{0,4},{4,0},{1,5},{5,1},{2,6},{6,2},{3,7},{7,3},{8,12},{12,8},{9,1... | collective-permute-start | bytes 3145736 | tf_op jit(solution)/shard_map/ppermute | solution.py:197
  435.0 31.6 %collective-permute-start.39 = (f32[6,32]{1,0:T(8,128)S(1)}, f32[6,32]{1,0:T(8,128)S(1)}, u32[]{:S(2)}, u32[]{:S(2)}) collective-permute-start(f32[6,32]{1,0:T(8,128)S(1)} %bitcast.165), channel_id=1, source_target_pairs={{0,4},{4,0},{1,5},{5,1},{2,6},{6,2},{3,7},{7,3},{8,12},{12,8},{9,1... | collective-permute-start | bytes 2312 | tf_op jit(solution)/shard_map/ppermute | solution.py:197
  (59 other events, 472.2 us)
Sparse Core Ops, SparseCore 0:
  47.7 29.2 all-gather.5
  94.3 25.0 all-gather.7
  303.3 25.4 reduce-scatter.7
  394.9 21.8 reduce-scatter.3
  422.2 39.1 reduce-scatter.5

commit v3 on v2

--- a/solution.py
+++ b/solution.py
@@ -67,16 +67,25 @@
     lax.fori_loop(0, rows // QB, block, 0)
 
 
-def attend(joint, groups):
+def without(count, kernel):
+    def call(*refs):
+        return kernel(*refs[count:])
+
+    return call
+
+
+def attend(joint, groups, first, last, so_far=()):
     rows = joint.shape[0]
-    part = lambda c: pl.BlockSpec((rows, PAIR), lambda z: (0, 3 * z + c))
+    part = lambda c: pl.BlockSpec((rows, PAIR), lambda z: (0, 3 * (z + first) + c))
+    kept = len(so_far)
     return pl.pallas_call(
-        attend_kernel,
-        grid=(groups,),
-        in_specs=[part(0), part(1), part(2)],
+        without(kept, attend_kernel),
+        grid=(last - first,),
+        in_specs=[pl.BlockSpec(memory_space=pl.ANY)] * kept + [part(0), part(1), part(2)],
+        input_output_aliases={i: i for i in range(kept)},
         out_specs=[
-            pl.BlockSpec((rows, PAIR), lambda z: (0, z)),
-            pl.BlockSpec((1, 2, rows), lambda z: (z, 0, 0)),
+            pl.BlockSpec((rows, PAIR), lambda z: (0, z + first)),
+            pl.BlockSpec((1, 2, rows), lambda z: (z + first, 0, 0)),
         ],
         out_shape=[
             jax.ShapeDtypeStruct((rows, groups * PAIR), BF16),
@@ -84,12 +93,12 @@
         ],
         compiler_params=pltpu.CompilerParams(vmem_limit_bytes=VMEM),
         cost_estimate=pl.CostEstimate(
-            flops=groups * 2 * 16 * rows * rows * HD,
-            bytes_accessed=groups * rows * PAIR * 8,
-            transcendentals=groups * 2 * rows * rows,
+            flops=(last - first) * 2 * rows * HD,
+            bytes_accessed=(last - first) * rows,
+            transcendentals=(last - first) * 2 * rows,
         ),
         name="attend",
-    )(joint, joint, joint)
+    )(*so_far, joint, joint, joint)
 
 
 def attend_back_kernel(q_ref, k_ref, v_ref, g_ref, o_ref, lse_ref, d_ref, sum_ref, dk_ref, dv_ref):
@@ -134,24 +143,27 @@
     sum_ref[0, 1:2, :] = jnp.sum(dv.astype(F32), axis=0, keepdims=True)
 
 
-def attend_back(joint, context_grad, context, lse, groups):
+def attend_back(joint, context_grad, context, lse, groups, first, last, so_far=()):
     rows = joint.shape[0]
-    part = lambda c: pl.BlockSpec((rows, PAIR), lambda z: (0, 3 * z + c))
-    one = pl.BlockSpec((rows, PAIR), lambda z: (0, z))
+    part = lambda c: pl.BlockSpec((rows, PAIR), lambda z: (0, 3 * (z + first) + c))
+    one = pl.BlockSpec((rows, PAIR), lambda z: (0, z + first))
+    kept = len(so_far)
     return pl.pallas_call(
-        attend_back_kernel,
-        grid=(groups,),
-        in_specs=[
+        without(kept, attend_back_kernel),
+        grid=(last - first,),
+        input_output_aliases={i: i for i in range(kept)},
+        in_specs=[pl.BlockSpec(memory_space=pl.ANY)] * kept
+        + [
             part(0),
             part(1),
             part(2),
             one,
             one,
-            pl.BlockSpec((1, 2, rows), lambda z: (z, 0, 0)),
+            pl.BlockSpec((1, 2, rows), lambda z: (z + first, 0, 0)),
         ],
         out_specs=[
-            pl.BlockSpec((rows, 3 * PAIR), lambda z: (0, z)),
-            pl.BlockSpec((1, 2, PAIR), lambda z: (z, 0, 0)),
+            pl.BlockSpec((rows, 3 * PAIR), lambda z: (0, z + first)),
+            pl.BlockSpec((1, 2, PAIR), lambda z: (z + first, 0, 0)),
         ],
         out_shape=[
             jax.ShapeDtypeStruct((rows, 3 * groups * PAIR), BF16),
@@ -160,12 +172,12 @@
         scratch_shapes=[pltpu.VMEM((rows, PAIR), F32), pltpu.VMEM((rows, PAIR), F32)],
         compiler_params=pltpu.CompilerParams(vmem_limit_bytes=VMEM),
         cost_estimate=pl.CostEstimate(
-            flops=groups * 2 * 40 * rows * rows * HD,
-            bytes_accessed=groups * rows * PAIR * 16,
-            transcendentals=groups * 2 * rows * rows,
+            flops=(last - first) * 2 * rows * HD,
+            bytes_accessed=(last - first) * rows,
+            transcendentals=(last - first) * 2 * rows,
         ),
         name="attend_back",
-    )(joint, joint, joint, context_grad, context, lse)
+    )(*so_far, joint, joint, joint, context_grad, context, lse)
 
 
 def normalized(values_in):
@@ -207,7 +219,8 @@
     return dot(rows[:half], weight) + away.astype(F32)
 
 
-def assemble_kernel(chip_ref, own_ref, x_ref, y_ref, low_ref, high_ref, *out_refs):
+def assemble_kernel(n_far, chip_ref, own_ref, x_ref, y_ref, *refs):
+    far_refs, out_refs = refs[:n_far], refs[n_far:]
     chip = chip_ref[0]
     wide = own_ref.shape[2]
     lower = pl.program_id(0) < pl.num_programs(0) // 2
@@ -223,7 +236,9 @@
         out_ref[0, :, columns(0)] = own_ref[0, rows, :]
         out_ref[0, :, columns(1)] = x_ref[0, rows, :]
         out_ref[0, :, columns(2)] = y_ref[0, rows, :]
-        far = jnp.where(lower, low_ref[0, rows, :], high_ref[0, rows, :])
+        far = far_refs[0][0, rows, :]
+        if n_far == 2:
+            far = jnp.where(lower, far, far_refs[1][0, rows, :])
         out_ref[0, :, columns(3)] = far
 
 
@@ -232,24 +247,21 @@
     members, rows, wide = own.shape
     half = low.shape[0]
     one = pl.BlockSpec((1, rows, wide), lambda z, c: (z, 0, 0))
+    far = [pl.BlockSpec((1, rows, wide), lambda z, c: (jnp.minimum(z, half - 1), 0, 0))]
+    if len(blocks) == 5:
+        far.append(pl.BlockSpec((1, rows, wide), lambda z, c: (jnp.maximum(z - half, 0), 0, 0)))
     return pl.pallas_call(
-        assemble_kernel,
+        functools.partial(assemble_kernel, len(far)),
         grid_spec=pltpu.PrefetchScalarGridSpec(
             num_scalar_prefetch=1,
             grid=(members,),
-            in_specs=[
-                one,
-                one,
-                one,
-                pl.BlockSpec((1, rows, wide), lambda z, c: (jnp.minimum(z, half - 1), 0, 0)),
-                pl.BlockSpec((1, rows, wide), lambda z, c: (jnp.maximum(z - half, 0), 0, 0)),
-            ],
+            in_specs=[one, one, one, *far],
             out_specs=[pl.BlockSpec((1, h, 4 * wide), lambda z, c: (z, 0, 0)) for h in heights],
         ),
         out_shape=[jax.ShapeDtypeStruct((members, h, 4 * wide), BF16) for h in heights],
         compiler_params=pltpu.CompilerParams(vmem_limit_bytes=VMEM),
         cost_estimate=pl.CostEstimate(
-            flops=0, bytes_accessed=16 * members * rows * wide, transcendentals=0
+            flops=0, bytes_accessed=members * rows, transcendentals=0
         ),
         name="assemble",
     )(chip.reshape(1), *blocks)
@@ -263,28 +275,36 @@
     return lax.optimization_barrier((value, *earlier))[0]
 
 
-def layer_gather(part):
-    own = lax.all_gather(part, "tensor", axis=0, tiled=False)
-    half = own.shape[0] // 2
-    by_x = to_chip(own, 1)
-    by_y = to_chip(own, 2)
-    return own, by_x, by_y, to_chip(by_y[:half], 1), to_chip(by_x[half:], 2)
-
-
-def layer_scatter(block):
+def layer_near(part, ready=()):
+    own = after(lax.all_gather(part, "tensor", axis=0, tiled=False), *ready)
+    return own, to_chip(own, 1), to_chip(own, 2)
+
+
+def layer_far(by_x, by_y):
+    half = by_x.shape[0] // 2
+    return to_chip(by_y[:half], 1), to_chip(by_x[half:], 2)
+
+
+def scatter_far(block, ready=()):
     far = block(3)
     half = far.shape[0] // 2
-    low = to_chip(far[:half], 1)
-    high = to_chip(far[half:], 2)
+    return to_chip(after(far[:half], *ready), 1), to_chip(after(far[half:], *ready), 2)
+
+
+def scatter_near(block, low, high, ready=()):
+    half = low.shape[0]
     near_x = block(1)
     near_y = block(2)
     add = lambda a, b: (a.astype(F32) + b.astype(F32)).astype(BF16)
     near_y = jnp.concatenate((add(near_y[:half], low), near_y[half:]), axis=0)
     near_x = jnp.concatenate((near_x[:half], add(near_x[half:], high)), axis=0)
-    came_y = to_chip(near_y, 2)
-    came_x = to_chip(near_x, 1)
-    own = block(0)
-    return (own.astype(F32) + came_x.astype(F32) + came_y.astype(F32)).astype(BF16)
+    near_x = after(near_x, *ready)
+    near_y = after(near_y, *ready)
+    return block(0), to_chip(near_x, 1), to_chip(near_y, 2)
+
+
+def three_sum(parts):
+    return sum(p.astype(F32) for p in parts).astype(BF16)
 
 
 def in_chip_order(chip, blocks):
@@ -383,7 +403,10 @@
         lines = -(-both.size // (16 * 2 * slab)) * 16
         both = jnp.concatenate((both, jnp.zeros((lines * 2 * slab - both.size,), BF16)))
         first = jnp.concatenate((shard[: bounds[1]], both.reshape(lines, 2 * slab)), axis=0)
-        blocks = layer_gather(first)
+        third = shard[bounds[3] :][None]
+        third = (third, *(to_chip(third, move) for move in (1, 2, 3)))
+        blocks = layer_near(first, (mine, *third[1:]))
+        blocks += layer_far(*blocks[1:])
         (w_qkv,) = assemble(chip, blocks, (3 * cols,))
         tails = [b[:, 3 * cols :] for b in blocks]
         tails = tails[:3] + [jnp.concatenate(tails[3:], axis=0)]
@@ -392,12 +415,11 @@
         packed = packed[:, :, :, 0] + packed[:, :, :, 1] + packed[:, :, :, 2]
         packed = packed.transpose(0, 2, 1, 3).reshape(-1, n_vec)
         second = after(shard[bounds[1] : bounds[3]], blocks[0])
-        blocks = layer_gather(second)
-        w_out, w_up = assemble(chip, blocks, (cols, units))
-        third = after(shard[bounds[3] :], blocks[0])
-        blocks = layer_gather(third)
-        (w_down,) = assemble(chip, blocks, (units,))
-        w_qkv, w_out, w_up, w_down = (w.reshape(-1, width) for w in (w_qkv, w_out, w_up, w_down))
+        mid_blocks = layer_near(second)
+        (third,) = assemble(chip, third, (units,))
+        w_down = lax.all_gather(after(third[0], mid_blocks[0]), "tensor", axis=0, tiled=True)
+        cot = swap(after(cotangent, w_down))
+        w_qkv = w_qkv.reshape(-1, width)
     else:
 
         def gathered(index):
@@ -424,8 +446,17 @@
     bias_up = bias_up.reshape(-1)
 
     joint = (nt(seen, w_qkv) + bias_qkv).astype(BF16)
-    cot = swap(after(cotangent, joint))
-    context, lse = attend(joint, n_ten)
+    if not small:
+        cot = swap(cotangent)
+    half = n_ten // 2
+    context, lse = attend(joint, n_ten, 0, half)
+    if small:
+        far = layer_far(*(after(block, context) for block in mid_blocks[1:]))
+        context = after(context, *mid_blocks[1:])
+    context, lse = attend(joint, n_ten, half, n_ten, (context, lse))
+    if small:
+        w_out, w_up = assemble(chip, (after(mid_blocks[0], context), *mid_blocks[1:], *far), (cols, units))
+        w_out, w_up = w_out.reshape(-1, width), w_up.reshape(-1, width)
     branch = summed_rows(context, w_out, nn)
     unit_mid, inverse_mid = normalized(mine.astype(F32) + branch + bias_out)
     middle = unit_mid * gain_mid + shift_mid
@@ -433,7 +464,7 @@
     hidden, slope = gelu_pair(nt(seen_middle, w_up) + bias_up)
     branch_two = summed_rows(hidden, w_down, nn)
     unit_end, inverse_end = normalized(middle + branch_two + bias_down)
-    encoded = swap((unit_end * gain_end + shift_end).astype(BF16))
+    encoded = (unit_end * gain_end + shift_end).astype(BF16)
 
     second_grad, end_gain_part, end_shift_part, down_bias_part = norm_back(
         cot.astype(F32), unit_end, inverse_end, gain_end
@@ -443,6 +474,10 @@
     up_bias_part = jnp.sum(pre_grad.astype(F32), axis=0)
     middle_grad = summed_rows(pre_grad, w_up, nn) + second_grad
 
+    def member_sum(total):
+        total = total.reshape(n_ten, -1, 2 * slab)
+        return lax.psum_scatter(total, "tensor", scatter_dimension=0, tiled=False)
+
     def beside(rows, columns):
         def block(move):
             at = lax.bitwise_xor(chip, move) * (2 * slab)
@@ -451,10 +486,12 @@
         return block
 
     if small:
-        down_layer = layer_scatter(beside(hidden, seen_second))
-        down_part = lax.psum_scatter(
-            down_layer.reshape(n_ten, -1, 2 * slab), "tensor", scatter_dimension=0, tiled=False
-        )
+        down_sum = tn(hidden, seen_second).astype(BF16)
+        down_rows = lax.psum_scatter(
+            down_sum.reshape(n_ten, units, width), "tensor", scatter_dimension=0, tiled=False
+        )
+        up_block = beside(pre_grad, after(seen_middle, down_sum))
+        up_far = scatter_far(up_block)
     else:
         down_sum = tn(hidden, seen_second)
         up_sum = tn(pre_grad, seen_middle)
@@ -462,27 +499,31 @@
         middle_grad, unit_mid, inverse_mid, gain_mid
     )
     seen_first = both_rows(first_grad.astype(BF16))
+    if small:
+        up_far = [after(part, first_grad) for part in up_far]
+        up_layer = scatter_near(up_block, *up_far)
     context_grad = nt(seen_first, w_out).astype(BF16)
-    if small:
-        up_block = beside(pre_grad, seen_middle)
-        out_block = beside(context, seen_first)
-        n_up = n_ten * units
-        mid_layer = layer_scatter(
-            lambda move: jnp.concatenate((up_block(move), out_block(move)), axis=0)
-        )
-        mid_layer = jnp.concatenate(
-            (
-                mid_layer[n_up:].reshape(n_ten, cols, 2 * slab),
-                mid_layer[:n_up].reshape(n_ten, units, 2 * slab),
-            ),
-            axis=1,
-        )
-        mid_part = lax.psum_scatter(mid_layer, "tensor", scatter_dimension=0, tiled=False)
-    else:
+    if not small:
         out_sum = tn(context, seen_first)
-    qkv_low, bias_sums = attend_back(joint, context_grad, context, lse, n_ten)
+    given = (joint, context_grad, context, lse, n_ten)
+    half_back = attend_back(*given, 0, half)
+    if small:
+        up_total = three_sum((after(up_layer[0], half_back[0]), *up_layer[1:]))
+        half_back = (after(half_back[0], up_total), half_back[1])
+    qkv_low, bias_sums = attend_back(*given, half, n_ten, half_back)
+    if small:
+        up_part = member_sum(up_total)
+        encoded = after(encoded, up_part)
+    encoded = swap(encoded)
     input_grad = summed_rows(qkv_low, w_qkv, nn) + first_grad
     input_grad = swap(input_grad.astype(BF16)).astype(F32)
+
+    def core_halves(part):
+        keep = lax.dynamic_slice_in_dim(part, core * slab, slab, axis=1)
+        came = to_other(lax.dynamic_slice_in_dim(part, (1 - core) * slab, slab, axis=1))
+        return jnp.stack(
+            (jnp.where(core == 0, keep, came), jnp.where(core == 0, came, keep)), axis=0
+        ).astype(F32)
 
     def scattered(total):
         rows = total.shape[0] // n_ten
@@ -518,36 +559,45 @@
             tail + [jnp.zeros((n_chip * n_ten, lines * 2 * slab - used), F32)], axis=1
         )
         extra = extra.reshape(n_chip, n_ten * lines, 2 * slab).astype(BF16)
-        qkv_block = beside(qkv_low, seen)
+        out_block = beside(context, seen_first)
 
         def last_block(move):
             owner = lax.bitwise_xor(chip, move)
             mark = lax.dynamic_index_in_dim(extra, owner, 0, keepdims=False)
-            return jnp.concatenate((qkv_block(move), mark), axis=0)
-
-        last = layer_scatter(last_block)
+            return jnp.concatenate(
+                (beside(qkv_low, seen)(move), out_block(move), mark), axis=0
+            )
+
+        last = scatter_near(last_block, *scatter_far(last_block, (down_rows,)), (up_part,))
+        last = three_sum((after(last[0], input_grad, encoded), *last[1:]))
         n_qkv = 3 * n_ten * cols
+        n_out = n_ten * cols
         last = jnp.concatenate(
             (
                 last[:n_qkv].reshape(n_ten, 3 * cols, 2 * slab),
-                last[n_qkv:].reshape(n_ten, lines, 2 * slab),
+                last[n_qkv : n_qkv + n_out].reshape(n_ten, cols, 2 * slab),
+                last[n_qkv + n_out :].reshape(n_ten, lines, 2 * slab),
             ),
             axis=1,
         )
-        qkv_part = lax.psum_scatter(last, "tensor", scatter_dimension=0, tiled=False)
-        vector_line = qkv_part[3 * cols :].reshape(-1).astype(F32)
-        qkv_part = qkv_part[: 3 * cols]
-        parts = jnp.concatenate((qkv_part, mid_part, down_part), axis=0)
+        down_cut = lambda move: lax.dynamic_slice_in_dim(
+            down_rows, lax.bitwise_xor(chip, move) * (2 * slab), 2 * slab, axis=1
+        )
+        down_part = three_sum([down_cut(0)] + [to_chip(down_cut(move), move) for move in (1, 2, 3)])
+        last_part = member_sum(last)
+        vector_line = last_part[4 * cols :].reshape(-1).astype(F32)
+        last_halves = core_halves(last_part[: 4 * cols])
+        cut = [
+            last_halves[:, : 3 * cols],
+            last_halves[:, 3 * cols :],
+            core_halves(up_part),
+            core_halves(down_part),
+        ]
     else:
         qkv_sum = tn(qkv_low, seen)
         parts = jnp.concatenate([scattered(t) for t in (qkv_sum, out_sum, up_sum, down_sum)], axis=0)
-    parts = parts.reshape(-1, 2, slab)
-    keep = lax.dynamic_index_in_dim(parts, core, 1, keepdims=False)
-    came = to_other(lax.dynamic_index_in_dim(parts, 1 - core, 1, keepdims=False))
-    halves = jnp.stack(
-        (jnp.where(core == 0, keep, came), jnp.where(core == 0, came, keep)), axis=0
-    ).astype(F32)
-    cut = [halves[:, bounds[i] : bounds[i + 1]] for i in range(4)]
+        halves = core_halves(parts)
+        cut = [halves[:, bounds[i] : bounds[i + 1]] for i in range(4)]
     qkv_out = (
         cut[0].reshape(2, 3, cols, slab).transpose(3, 1, 0, 2).reshape(slab, 3, 2 * cols)
     )

time: 488 us -> 410 us (0.84)
  waiting for transfers between devices: 128 us -> 87.3 us
  starting transfers between devices: 91 us -> 51.1 us
  matrix products: 99.6 us -> 93.5 us
    ppermute x24 -> x22, waiting for transfers between devices: 113 us -> 53.6 us  [to_chip(): return lax.ppermute(value, 'chip', [(i, i ^ move) for i in range(4)])]
    ppermute x12 -> x14, starting transfers between devices: 38.6 us -> 14.9 us  [to_other(): return lax.ppermute(value, 'core', [(0, 1), (1, 0)])]
    ppermute x4, starting transfers between devices: 23.2 us -> 5.72 us  [on_device(): swap = lambda value: lax.ppermute(value, ('core', 'tensor'), pairs)]
    reduce_scatter x3, waiting for transfers between devices: 0.02 us -> 15.6 us  [the longest x2 15.6 us: member_sum(): return lax.psum_scatter(total, 'tensor', scatter_dimension=0, tiled=False)]
    dot_general x16 -> x13, matrix products: 39.8 us -> 31.3 us  [tn(): lax.dot_general(left, right, (((0,), (0,)), ((), ())), preferred_element_...]
    ppermute x24 -> x22, starting transfers between devices: 28.4 us -> 30.1 us  [to_chip(): return lax.ppermute(value, 'chip', [(i, i ^ move) for i in range(4)])]
    pallas_call x5 -> x7, Pallas kernels: 70.9 us -> 72.3 us  [the longest x2 30.2 us: attend_back(): pl.pallas_call(without(kept, attend_back_kernel), grid=(last - first,), i...]
    unnamed x96 -> x98, local copies, waits for them, and re-layouts: 12.2 us -> 11.6 us
  transfers between devices with their start and end apart: 45 -> 45, of which waited for: 19 -> 18; matrix products, arithmetic and copies ran while one was open for 25% -> 28% of each run, Pallas kernels for 15% -> 18%
where the time goes in v3:
time: 410 us; the launch traced here: 404 us
  matrix products  93.5 us (23%)
  waiting for transfers between devices  87.3 us (21%)
  Pallas kernels  72.3 us (18%)
  starting transfers between devices  51.1 us (12%)
  local copies, waits for them, and re-layouts  30.7 us (7%)
  other arithmetic  27 us (7%)
  blocking collectives  26.2 us (6%)
  between operations  15.5 us (4%)
    ppermute x22, waiting for transfers between devices, to_chip(): return lax.ppermute(value, 'chip', [(i, i ^ move) for i in range(4)])  53.6 us
    dot_general x4, matrix products, nt(): lax.dot_general(left, right, (((1,), (1,)), ((), ())), preferred_element_...  32.9 us
    dot_general x13, matrix products, tn(): lax.dot_general(left, right, (((0,), (0,)), ((), ())), preferred_element_...  31.3 us
    pallas_call x2, Pallas kernels, attend_back(): pl.pallas_call(without(kept, attend_back_kernel), grid=(last - first,), i...  30.2 us
    ppermute x22, starting transfers between devices, to_chip(): return lax.ppermute(value, 'chip', [(i, i ^ move) for i in range(4)])  30.1 us
    pallas_call x2, Pallas kernels, attend(): pl.pallas_call(without(kept, attend_kernel), grid=(last - first,), in_spe...  29.9 us
    dot_general x8, matrix products, nn(): lax.dot_general(left, right, (((1,), (0,)), ((), ())), preferred_element_...  29.3 us
    all_gather x1, blocking collectives, layer_near(): own = after(lax.all_gather(part, 'tensor', axis=0, tiled=False), *ready)  26.2 us
  transfers between devices with their start and end apart: 45, of which 18 were waited for; matrix products, arithmetic and copies ran while one was open for 28% of the time, Pallas kernels for 18%

profile of v3, /device:TPU:0, one launch (start us, length us, event | category | flops | bytes accessed | tf_op | source)
XLA Modules:
  0.0 403.6 jit_solution(12149477436867107064)
XLA Ops:
  13.5 4.0 collective-permute-start.6
  18.2 26.2 %all-gather = bf16[1600,256]{1,0:T(8,128)(2,1)S(1)} all-gather(bf16[400,256]{1,0:T(8,128)(2,1)S(1)} %fusion.68), channel_id=2, replica_groups=mesh['chip'=4,'core'=2,'tensor'=4] {'tensor'}, dimensions={0}, use_global_device_ids=true | all-gather | bytes 1024000 | tf_op jit(solution)/shard_map/all_gather | solution.py:279
  50.1 14.4 %collective-permute-done.8.y_ref = bf16[4,400,256]{2,1,0:T(8,128)(2,1)S(1)} collective-permute-done((bf16[4,400,256]{2,1,0:T(8,128)(2,1)S(1)}, bf16[4,400,256]{2,1,0:T(8,128)(2,1)S(1)}, u32[]{:S(2)}, u32[]{:S(2)}) %collective-permute-start.8) | collective-permute-done | bytes 819232 | tf_op jit(solution)/shard_map/ppermute | solution.py:271
  77.2 3.2 all-gather.7.cloned.1.call-done
  83.6 4.5 %assemble.3 = bf16[4,384,1024]{2,1,0:T(8,128)(2,1)} custom-call(s32[1]{0:T(128)} %bitcast.chip_ref, bf16[4,400,256]{2,1,0:T(8,128)(2,1)} %bitcast.156, bf16[4,400,256]{2,1,0:T(8,128)(2,1)} %copy-done.16, bf16[4,400,256]{2,1,0:T(8,128)(2,1)} %copy-done.15, bf16[2,400,256]{2,1,0:T(8,128)(2,1)} %collective-permute-done.9.refs_0_, bf16[2,400,256]{2,1,0:T(8,128)(2,1)} %copy-done.27), custom_call_target="tpu_custom_call" | custom-call | bytes 1600 | tf_op jit(solution)/shard_map/assemble/pallas_call | solution.py:253
  88.2 7.7 %add_convert_fusion.refs_0_.refs_1_.refs_2_.refs_3_.refs_4_ = bf16[1024,1536]{1,0:T(8,128)(2,1)} fusion(bf16[1024,1024]{1,0:T(8,128)(2,1)} %constant_dynamic-update-slice_fusion, bf16[1536,1024]{1,0:T(8,128)(2,1)} %bitcast.157, f32[1536]{0:T(1024)S(1)} %add.229), kind=kOutput, calls=%fused_computation.9 | convolution fusion | flops 3224371200 | bytes 8394752 | tf_op jit(solution)/shard_map/dot_general | solution.py:25
  95.9 15.1 %attend.2 = (bf16[1024,512]{1,0:T(8,128)(2,1)}, f32[4,2,1024]{2,1,0:T(2,128)}) custom-call(bf16[1024,1536]{1,0:T(8,128)(2,1)} %add_convert_fusion.refs_0_.refs_1_.refs_2_.refs_3_.refs_4_, bf16[1024,1536]{1,0:T(8,128)(2,1)} %add_convert_fusion.refs_0_.refs_1_.refs_2_.refs_3_.refs_4_, bf16[1024,1536]{1,0:T(8,128)(2,1)} %add_convert_fusion.refs_0_.refs_1_.refs_2_.refs_3_.refs_4_), custom_call_target="tpu_custom_call" | custom-call | flops 262144 | bytes 2048 | tf_op jit(solution)/shard_map/attend/pallas_call | solution.py:81
  115.4 14.8 %attend.3 = (bf16[1024,512]{1,0:T(8,128)(2,1)}, f32[4,2,1024]{2,1,0:T(2,128)}) custom-call(bf16[1024,512]{1,0:T(8,128)(2,1)} %get-tuple-element.47.refs_0_, f32[4,2,1024]{2,1,0:T(2,128)} %get-tuple-element.48.refs_1_, bf16[1024,1536]{1,0:T(8,128)(2,1)} %add_convert_fusion.refs_0_.refs_1_.refs_2_.refs_3_.refs_4_, ...), custom_call_target="tpu_custom_call", output_to_operand_aliasing={{0}: (0, {}), {1}: (1, {})} | custom-call | flops 262144 | bytes 2048 | tf_op jit(solution)/shard_map/attend/pallas_call | solution.py:81
  132.0 5.4 %assemble.4 = (bf16[4,128,1024]{2,1,0:T(8,128)(2,1)}, bf16[4,512,1024]{2,1,0:T(8,128)(2,1)}) custom-call(s32[1]{0:T(128)} %bitcast.chip_ref, bf16[4,640,256]{2,1,0:T(8,128)(2,1)} %bitcast.165, bf16[4,640,256]{2,1,0:T(8,128)(2,1)} %collective-permute-done.11.x_ref, bf16[4,640,256]{2,1,0:T(8,128)(2,1)} %copy-done.12, bf16[2,640,256]{2,1,0:T(8,128)(2,1)} %copy-done.26, ...), custom_call_target="tpu_custom_call" | custom-call | bytes 2560 | tf_op jit(solution)/shard_map/assemble/pallas_call | solution.py:253
  148.6 9.8 %multiply_convert_fusion.1 = (bf16[1024,2048]{1,0:T(8,128)(2,1)}, f32[1024,2048]{1,0:T(8,128)}) fusion(f32[2048]{0:T(1024)S(1)} %bitcast.185, bf16[2048,1024]{1,0:T(8,128)(2,1)} %bitcast.189, bf16[512,1024]{1,0:T(8,128)(2,1)} %collective-permute-done.16, bf16[512,1024]{1,0:T(8,128)(2,1)S(1)} %fusion.22), kind=kOutput, calls=%fused_computation.7 | convolution fusion | flops 4311744512 | bytes 18882560 | tf_op jit(solution)/shard_map/dot_general | solution.py:25
  158.4 8.8 %all-gather.5.cloned.1.call-done = bf16[2048,1024]{1,0:T(8,128)(2,1)} async-done(((bf16[512,1024]{1,0:T(8,128)(2,1)}), bf16[2048,1024]{1,0:T(8,128)(2,1)}) %all-gather.5.cloned.1.call-update) | async-done | bytes 4194320 | tf_op jit(solution)/shard_map/all_gather | solution.py:420
  167.2 6.1 %fusion.33 = bf16[512,1024]{1,0:T(8,128)(2,1)} fusion(bf16[2048,1024]{1,0:T(8,128)(2,1)} %all-gather.5.cloned.1.call-done, bf16[1024,2048]{1,0:T(8,128)(2,1)} %get-tuple-element.138), kind=kOutput, calls=%fused_computation.74 | convolution fusion | flops 2148007936 | bytes 7340032 | tf_op jit(solution)/shard_map/dot_general | solution.py:29
  176.3 5.8 %fusion.98 = (f32[512]{0:T(512)S(1)}, f32[512,1024]{1,0:T(8,128)S(1)}) fusion(f32[1024]{0:T(1024)S(1)} %add.248, bf16[512,1024]{1,0:T(8,128)(2,1)} %collective-permute-done.17, f32[1024]{0:T(1024)S(1)} %add.238, f32[1024]{0:T(1024)S(1)} %mul.167, f32[512]{0:T(512)S(1)} %add_rsqrt_fusion.1, f32[512,1024]{1,0:T(8,128)S(1)} %get-tuple-element.137, ...), kind=kOutput, calls=%fused_computation.225 | convolution fusion | flops 2152201728 | bytes 11552768 | tf_op jit(solution)/shard_map/dot_general | solution.py:29
  187.7 7.9 %collective-permute-start.19 = (bf16[512,1024]{1,0:T(8,128)(2,1)}, bf16[512,1024]{1,0:T(8,128)(2,1)}, u32[]{:S(2)}, u32[]{:S(2)}) collective-permute-start(bf16[512,1024]{1,0:T(8,128)(2,1)} %convert_element_type.234), channel_id=1, source_target_pairs={{0,4},{4,0},{1,5},{5,1},{2,6},{6,2},{3,7},{7,3},{8,12},{12,8},{9,1... | collective-permute-start | bytes 3145736 | tf_op jit(solution)/shard_map/ppermute | solution.py:209
  195.6 3.3 pad_maximum_fusion.2
  198.9 7.9 %convolution_convert_fusion = bf16[2048,1024]{1,0:T(8,128)(2,1)} fusion(bf16[1024,2048]{1,0:T(8,128)(2,1)S(1)} %copy-done.46, bf16[512,1024]{1,0:T(8,128)(2,1)} %collective-permute-done.19, bf16[512,1024]{1,0:T(8,128)(2,1)} %convert_element_type.234), kind=kOutput, calls=%fused_computation.10 | convolution fusion | flops 4301258752 | bytes 10485760 | tf_op jit(solution)/shard_map/dot_general | solution.py:33
  206.9 11.3 %fusion.103 = (bf16[2048]{0:T(1024)(128)(2,1)S(1)}, bf16[1024,2048]{1,0:T(8,128)(2,1)S(1)}) fusion(f32[1024,2048]{1,0:T(8,128)} %get-tuple-element.139, f32[2048]{0:T(1024)S(1)} %bitcast.186, bf16[2048,1024]{1,0:T(8,128)(2,1)} %all-gather.5.cloned.1.call-done, bf16[512,1024]{1,0:T(8,128)(2,1)} %collective-permute-done.19, ...), kind=kOutput, calls=%fused_computation.230 | convolution fusion | flops 4328519680 | bytes 18886656 | tf_op jit(solution)/shard_map/dot_general | solution.py:25
  230.4 3.0 multiply_reduce_fusion
  234.3 7.5 %collective-permute-done.24 = bf16[1024,256]{1,0:T(8,128)(2,1)S(1)} collective-permute-done((bf16[1024,256]{1,0:T(8,128)(2,1)S(1)}, bf16[1024,256]{1,0:T(8,128)(2,1)S(1)}, u32[]{:S(2)}, u32[]{:S(2)}) %collective-permute-start.24) | collective-permute-done | bytes 524320 | tf_op jit(solution)/shard_map/ppermute | solution.py:271
  248.1 3.6 convolution_convert_fusion.8
  252.3 4.1 %fusion.32.refs_3_.refs_5_ = bf16[1024,512]{1,0:T(8,128)(2,1)} fusion(bf16[512,1024]{1,0:T(8,128)(2,1)} %bitcast.194, bf16[512,1024]{1,0:T(8,128)(2,1)} %collective-permute-done.21, bf16[512,1024]{1,0:T(8,128)(2,1)S(1)} %convert_element_type.242), kind=kOutput, calls=%fused_computation.72 | convolution fusion | flops 1078460416 | bytes 4194304 | tf_op jit(solution)/shard_map/dot_general | solution.py:25
  256.4 15.1 %attend_back.2 = (bf16[1024,1536]{1,0:T(8,128)(2,1)}, f32[4,2,128]{2,1,0:T(2,128)}) custom-call(bf16[1024,1536]{1,0:T(8,128)(2,1)} %add_convert_fusion.refs_0_.refs_1_.refs_2_.refs_3_.refs_4_, bf16[1024,1536]{1,0:T(8,128)(2,1)} %add_convert_fusion.refs_0_.refs_1_.refs_2_.refs_3_.refs_4_, ...), custom_call_target="tpu_custom_call" | custom-call | flops 262144 | bytes 2048 | tf_op jit(solution)/shard_map/attend_back/pallas_call | solution.py:151
  271.5 2.9 add_convert_fusion.3
  274.4 15.1 %attend_back.3 = (bf16[1024,1536]{1,0:T(8,128)(2,1)}, f32[4,2,128]{2,1,0:T(2,128)}) custom-call(bf16[1024,1536]{1,0:T(8,128)(2,1)} %get-tuple-element.64.refs_0_, f32[4,2,128]{2,1,0:T(2,128)} %get-tuple-element.65.refs_1_, bf16[1024,1536]{1,0:T(8,128)(2,1)} %add_convert_fusion.refs_0_.refs_1_.refs_2_.refs_3_.refs_4_, ...), custom_call_target="tpu_custom_call", output_to_operand_aliasing={{0}: (0, {}), {1}: (1, {})} | custom-call | flops 262144 | bytes 2048 | tf_op jit(solution)/shard_map/attend_back/pallas_call | solution.py:151
  290.6 3.2 convolution_convert_fusion.3
  311.2 8.4 %collective-permute-done.31 = bf16[1056,256]{1,0:T(8,128)(2,1)S(1)} collective-permute-done((bf16[1056,256]{1,0:T(8,128)(2,1)}, bf16[1056,256]{1,0:T(8,128)(2,1)S(1)}, u32[]{:S(2)}, u32[]{:S(2)}) %collective-permute-start.31) | collective-permute-done | bytes 540704 | tf_op jit(solution)/shard_map/ppermute | solution.py:271
  320.8 4.4 %reduce-scatter.4.cloned.1.call-done = bf16[1,512,256]{2,1,0:T(8,128)(2,1)} async-done(((bf16[4,512,256]{2,1,0:T(8,128)(2,1)}), bf16[1,512,256]{2,1,0:T(8,128)(2,1)}) %reduce-scatter.4.cloned.1.call-update) | async-done | bytes 262160 | tf_op jit(solution)/shard_map/reduce_scatter | solution.py:479
  329.7 4.5 %add_convert_fusion.2 = bf16[512,1024]{1,0:T(8,128)(2,1)S(1)} fusion(f32[512,1024]{1,0:T(8,128)S(1)} %copy-done.3, bf16[512,1024]{1,0:T(8,128)(2,1)} %collective-permute-done.27, bf16[1536,1024]{1,0:T(8,128)(2,1)} %bitcast.158, bf16[1024,1536]{1,0:T(8,128)(2,1)} %get-tuple-element.66), kind=kOutput, calls=%fused_computation.52 | convolution fusion | flops 1612709888 | bytes 8912896 | tf_op jit(solution)/shard_map/dot_general | solution.py:29
  341.1 11.1 %collective-permute-done.30 = bf16[2112,256]{1,0:T(8,128)(2,1)S(1)} collective-permute-done((bf16[2112,256]{1,0:T(8,128)(2,1)S(1)}, bf16[2112,256]{1,0:T(8,128)(2,1)S(1)}, u32[]{:S(2)}, u32[]{:S(2)}) %collective-permute-start.30) | collective-permute-done | bytes 1081376 | tf_op jit(solution)/shard_map/ppermute | solution.py:271
  362.0 3.8 collective-permute-done.37
  369.4 5.4 %collective-permute-start.38 = (bf16[512,128]{1,0:T(8,128)(2,1)S(1)}, bf16[512,128]{1,0:T(8,128)(2,1)S(1)}, u32[]{:S(2)}, u32[]{:S(2)}) collective-permute-start(bf16[512,128]{1,0:T(8,128)(2,1)S(1)} %constant_dynamic-slice_fusion.2), channel_id=1, source_target_pairs={{0,4},{4,0},{1,5},{5,1},{2,6},{6,2},{3,7},{7,3},{8,12},{12,8},{9,1... | collective-permute-start | bytes 393224 | tf_op jit(solution)/shard_map/ppermute | solution.py:209
  376.7 11.1 %reduce-scatter.8.cloned.1.call-done = bf16[1,528,256]{2,1,0:T(8,128)(2,1)} async-done(((bf16[4,528,256]{2,1,0:T(8,128)(2,1)}), bf16[1,528,256]{2,1,0:T(8,128)(2,1)}) %reduce-scatter.8.cloned.1.call-update) | async-done | bytes 270352 | tf_op jit(solution)/shard_map/reduce_scatter | solution.py:479
  (336 shorter events, 128.9 us)
Async XLA Ops:
  7.3 73.1 %all-gather.7.cloned.1.call-start = ((), (), s32[]{:S(2)}) async-start(), calls=%async_computation.7 | async-start | bytes 1638400 | tf_op jit(solution)/shard_map/all_gather | solution.py:279
  11.5 33.0 %collective-permute-start = (bf16[512,1024]{1,0:T(8,128)(2,1)}, bf16[512,1024]{1,0:T(8,128)(2,1)S(1)}, u32[]{:S(2)}, u32[]{:S(2)}) collective-permute-start(bf16[512,1024]{1,0:T(8,128)(2,1)} %param.15), channel_id=1, source_target_pairs={{0,0},{4,1},{1,4},{5,5},{2,2},{6,3},{3,6},{7,7},{8,8},{12,9},{9,12... | collective-permute-start | bytes 3145736 | tf_op jit(solution)/shard_map/ppermute | solution.py:358
  13.5 30.8 %collective-permute-start.6 = (bf16[1,512,256]{2,1,0:T(8,128)(2,1)S(1)}, bf16[1,512,256]{2,1,0:T(8,128)(2,1)S(1)}, u32[]{:S(2)}, u32[]{:S(2)}) collective-permute-start(bf16[1,512,256]{2,1,0:T(8,128)(2,1)S(1)} %maximum_bitcast_fusion.own_ref), channel_id=1, source_target_pairs={{0,24},{8,16},{16,8},{24,0},{1,25},{9,17},{17,9},{25,1},{2,26},{10... | collective-permute-start | bytes 786440 | tf_op jit(solution)/shard_map/ppermute | solution.py:271
  17.5 26.9 %collective-permute-start.5 = (bf16[1,512,256]{2,1,0:T(8,128)(2,1)S(1)}, bf16[1,512,256]{2,1,0:T(8,128)(2,1)S(1)}, u32[]{:S(2)}, u32[]{:S(2)}) collective-permute-start(bf16[1,512,256]{2,1,0:T(8,128)(2,1)S(1)} %maximum_bitcast_fusion.own_ref), channel_id=1, source_target_pairs={{0,16},{8,24},{16,0},{24,8},{1,17},{9,25},{17,1},{25,9},{2,18},{10... | collective-permute-start | bytes 786440 | tf_op jit(solution)/shard_map/ppermute | solution.py:271
  18.0 26.4 %collective-permute-start.4 = (bf16[1,512,256]{2,1,0:T(8,128)(2,1)S(1)}, bf16[1,512,256]{2,1,0:T(8,128)(2,1)S(1)}, u32[]{:S(2)}, u32[]{:S(2)}) collective-permute-start(bf16[1,512,256]{2,1,0:T(8,128)(2,1)S(1)} %maximum_bitcast_fusion.own_ref), channel_id=1, source_target_pairs={{0,8},{8,0},{16,24},{24,16},{1,9},{9,1},{17,25},{25,17},{2,10},{10... | collective-permute-start | bytes 786440 | tf_op jit(solution)/shard_map/ppermute | solution.py:271
  46.3 18.3 %collective-permute-start.8 = (bf16[4,400,256]{2,1,0:T(8,128)(2,1)S(1)}, bf16[4,400,256]{2,1,0:T(8,128)(2,1)S(1)}, u32[]{:S(2)}, u32[]{:S(2)}) collective-permute-start(bf16[4,400,256]{2,1,0:T(8,128)(2,1)S(1)} %bitcast.152), channel_id=1, source_target_pairs={{0,16},{8,24},{16,0},{24,8},{1,17},{9,25},{17,1},{25,9},{2,18},{10... | collective-permute-start | bytes 2457608 | tf_op jit(solution)/shard_map/ppermute | solution.py:271
  47.8 19.0 %collective-permute-start.7 = (bf16[4,400,256]{2,1,0:T(8,128)(2,1)S(1)}, bf16[4,400,256]{2,1,0:T(8,128)(2,1)S(1)}, u32[]{:S(2)}, u32[]{:S(2)}) collective-permute-start(bf16[4,400,256]{2,1,0:T(8,128)(2,1)S(1)} %bitcast.153), channel_id=1, source_target_pairs={{0,8},{8,0},{16,24},{24,16},{1,9},{9,1},{17,25},{25,17},{2,10},{10... | collective-permute-start | bytes 2457608 | tf_op jit(solution)/shard_map/ppermute | solution.py:271
  49.3 24.6 %collective-permute-start.1 = (bf16[512,1024]{1,0:T(8,128)(2,1)}, bf16[512,1024]{1,0:T(8,128)(2,1)}, u32[]{:S(2)}, u32[]{:S(2)}) collective-permute-start(bf16[512,1024]{1,0:T(8,128)(2,1)} %copy-done.22), channel_id=1, source_target_pairs={{0,4},{4,0},{1,5},{5,1},{2,6},{6,2},{3,7},{7,3},{8,12},{12,8},{9,1... | collective-permute-start | bytes 3145736 | tf_op jit(solution)/shard_map/ppermute | solution.py:209
  50.1 117.2 %all-gather.5.cloned.1.call-start = ((), (), s32[]{:S(2)}) async-start(), calls=%async_computation.3 | async-start | bytes 5242880 | tf_op jit(solution)/shard_map/all_gather | solution.py:420
  65.3 10.8 %collective-permute-start.9 = (bf16[2,400,256]{2,1,0:T(8,128)(2,1)}, bf16[2,400,256]{2,1,0:T(8,128)(2,1)}, u32[]{:S(2)}, u32[]{:S(2)}) collective-permute-start(bf16[2,400,256]{2,1,0:T(8,128)(2,1)} %slice.269), channel_id=1, source_target_pairs={{0,8},{8,0},{16,24},{24,16},{1,9},{9,1},{17,25},{25,17},{2,10},{10... | collective-permute-start | bytes 1228808 | tf_op jit(solution)/shard_map/ppermute | solution.py:271
  67.7 9.2 %collective-permute-start.10 = (bf16[2,400,256]{2,1,0:T(8,128)(2,1)}, bf16[2,400,256]{2,1,0:T(8,128)(2,1)S(1)}, u32[]{:S(2)}, u32[]{:S(2)}) collective-permute-start(bf16[2,400,256]{2,1,0:T(8,128)(2,1)} %slice.270), channel_id=1, source_target_pairs={{0,16},{8,24},{16,0},{24,8},{1,17},{9,25},{17,1},{25,9},{2,18},{10... | collective-permute-start | bytes 1228808 | tf_op jit(solution)/shard_map/ppermute | solution.py:271
  80.3 31.4 %collective-permute-start.12 = (bf16[4,640,256]{2,1,0:T(8,128)(2,1)}, bf16[4,640,256]{2,1,0:T(8,128)(2,1)S(1)}, u32[]{:S(2)}, u32[]{:S(2)}) collective-permute-start(bf16[4,640,256]{2,1,0:T(8,128)(2,1)} %bitcast.163), channel_id=1, source_target_pairs={{0,16},{8,24},{16,0},{24,8},{1,17},{9,25},{17,1},{25,9},{2,18},{10... | collective-permute-start | bytes 3932168 | tf_op jit(solution)/shard_map/ppermute | solution.py:271
  81.8 29.9 %collective-permute-start.11 = (bf16[4,640,256]{2,1,0:T(8,128)(2,1)}, bf16[4,640,256]{2,1,0:T(8,128)(2,1)}, u32[]{:S(2)}, u32[]{:S(2)}) collective-permute-start(bf16[4,640,256]{2,1,0:T(8,128)(2,1)} %bitcast.164), channel_id=1, source_target_pairs={{0,8},{8,0},{16,24},{24,16},{1,9},{9,1},{17,25},{25,17},{2,10},{10... | collective-permute-start | bytes 3932168 | tf_op jit(solution)/shard_map/ppermute | solution.py:271
  88.2 216.5 %reduce-scatter.6.cloned.1.call-start = ((), (), s32[]{:S(2)}) async-start(), calls=%async_computation.5 | async-start | bytes 5242880 | tf_op jit(solution)/shard_map/reduce_scatter | solution.py:490
  113.3 16.9 %collective-permute-start.14 = (bf16[2,640,256]{2,1,0:T(8,128)(2,1)S(1)}, bf16[2,640,256]{2,1,0:T(8,128)(2,1)S(1)}, u32[]{:S(2)}, u32[]{:S(2)}) collective-permute-start(bf16[2,640,256]{2,1,0:T(8,128)(2,1)S(1)} %slice.222), channel_id=1, source_target_pairs={{0,16},{8,24},{16,0},{24,8},{1,17},{9,25},{17,1},{25,9},{2,18},{10... | collective-permute-start | bytes 1966088 | tf_op jit(solution)/shard_map/ppermute | solution.py:271
  114.0 16.3 %collective-permute-start.13 = (bf16[2,640,256]{2,1,0:T(8,128)(2,1)S(1)}, bf16[2,640,256]{2,1,0:T(8,128)(2,1)S(1)}, u32[]{:S(2)}, u32[]{:S(2)}) collective-permute-start(bf16[2,640,256]{2,1,0:T(8,128)(2,1)S(1)} %slice.221), channel_id=1, source_target_pairs={{0,8},{8,0},{16,24},{24,16},{1,9},{9,1},{17,25},{25,17},{2,10},{10... | collective-permute-start | bytes 1966088 | tf_op jit(solution)/shard_map/ppermute | solution.py:271
  187.7 11.2 %collective-permute-start.19 = (bf16[512,1024]{1,0:T(8,128)(2,1)}, bf16[512,1024]{1,0:T(8,128)(2,1)}, u32[]{:S(2)}, u32[]{:S(2)}) collective-permute-start(bf16[512,1024]{1,0:T(8,128)(2,1)} %convert_element_type.234), channel_id=1, source_target_pairs={{0,4},{4,0},{1,5},{5,1},{2,6},{6,2},{3,7},{7,3},{8,12},{12,8},{9,1... | collective-permute-start | bytes 3145736 | tf_op jit(solution)/shard_map/ppermute | solution.py:209
  206.8 118.4 %reduce-scatter.4.cloned.1.call-start = ((), (), s32[]{:S(2)}) async-start(), calls=%async_computation.4 | async-start | bytes 1310720 | tf_op jit(solution)/shard_map/reduce_scatter | solution.py:479
  227.4 14.4 %collective-permute-start.24 = (bf16[1024,256]{1,0:T(8,128)(2,1)S(1)}, bf16[1024,256]{1,0:T(8,128)(2,1)S(1)}, u32[]{:S(2)}, u32[]{:S(2)}) collective-permute-start(bf16[1024,256]{1,0:T(8,128)(2,1)S(1)} %get-tuple-element.98), channel_id=1, source_target_pairs={{0,8},{8,0},{16,24},{24,16},{1,9},{9,1},{17,25},{25,17},{2,10},{10... | collective-permute-start | bytes 1572872 | tf_op jit(solution)/shard_map/ppermute | solution.py:271
  228.9 14.0 %collective-permute-start.22 = (bf16[1024,256]{1,0:T(8,128)(2,1)S(1)}, bf16[1024,256]{1,0:T(8,128)(2,1)S(1)}, u32[]{:S(2)}, u32[]{:S(2)}) collective-permute-start(bf16[1024,256]{1,0:T(8,128)(2,1)S(1)} %get-tuple-element.97), channel_id=1, source_target_pairs={{0,16},{8,24},{16,0},{24,8},{1,17},{9,25},{17,1},{25,9},{2,18},{10... | collective-permute-start | bytes 1572872 | tf_op jit(solution)/shard_map/ppermute | solution.py:271
  243.0 9.3 %collective-permute-start.21 = (bf16[512,1024]{1,0:T(8,128)(2,1)S(1)}, bf16[512,1024]{1,0:T(8,128)(2,1)}, u32[]{:S(2)}, u32[]{:S(2)}) collective-permute-start(bf16[512,1024]{1,0:T(8,128)(2,1)S(1)} %convert_element_type.242), channel_id=1, source_target_pairs={{0,4},{4,0},{1,5},{5,1},{2,6},{6,2},{3,7},{7,3},{8,12},{12,8},{9,1... | collective-permute-start | bytes 3145736 | tf_op jit(solution)/shard_map/ppermute | solution.py:209
  245.3 26.1 %collective-permute-start.23 = (bf16[2048,256]{1,0:T(8,128)(2,1)}, bf16[2048,256]{1,0:T(8,128)(2,1)}, u32[]{:S(2)}, u32[]{:S(2)}) collective-permute-start(bf16[2048,256]{1,0:T(8,128)(2,1)} %pad_maximum_fusion.11), channel_id=1, source_target_pairs={{0,8},{8,0},{16,24},{24,16},{1,9},{9,1},{17,25},{25,17},{2,10},{10... | collective-permute-start | bytes 3145736 | tf_op jit(solution)/shard_map/ppermute | solution.py:271
  245.9 25.6 %collective-permute-start.25 = (bf16[2048,256]{1,0:T(8,128)(2,1)S(1)}, bf16[2048,256]{1,0:T(8,128)(2,1)}, u32[]{:S(2)}, u32[]{:S(2)}) collective-permute-start(bf16[2048,256]{1,0:T(8,128)(2,1)S(1)} %pad_maximum_fusion.12), channel_id=1, source_target_pairs={{0,16},{8,24},{16,0},{24,8},{1,17},{9,25},{17,1},{25,9},{2,18},{10... | collective-permute-start | bytes 3145736 | tf_op jit(solution)/shard_map/ppermute | solution.py:271
  297.4 32.3 %collective-permute-start.27 = (bf16[512,1024]{1,0:T(8,128)(2,1)}, bf16[512,1024]{1,0:T(8,128)(2,1)}, u32[]{:S(2)}, u32[]{:S(2)}) collective-permute-start(bf16[512,1024]{1,0:T(8,128)(2,1)} %fusion.29), channel_id=1, source_target_pairs={{0,4},{4,0},{1,5},{5,1},{2,6},{6,2},{3,7},{7,3},{8,12},{12,8},{9,1... | collective-permute-start | bytes 3145736 | tf_op jit(solution)/shard_map/ppermute | solution.py:209
  299.6 88.3 %reduce-scatter.8.cloned.1.call-start = ((), (), s32[]{:S(2)}) async-start(), calls=%async_computation.6 | async-start | bytes 1351680 | tf_op jit(solution)/shard_map/reduce_scatter | solution.py:479
  304.7 14.8 %collective-permute-start.31 = (bf16[1056,256]{1,0:T(8,128)(2,1)}, bf16[1056,256]{1,0:T(8,128)(2,1)S(1)}, u32[]{:S(2)}, u32[]{:S(2)}) collective-permute-start(bf16[1056,256]{1,0:T(8,128)(2,1)} %get-tuple-element.71), channel_id=1, source_target_pairs={{0,8},{8,0},{16,24},{24,16},{1,9},{9,1},{17,25},{25,17},{2,10},{10... | collective-permute-start | bytes 1622024 | tf_op jit(solution)/shard_map/ppermute | solution.py:271
  309.8 15.4 %collective-permute-start.29 = (bf16[1056,256]{1,0:T(8,128)(2,1)}, bf16[1056,256]{1,0:T(8,128)(2,1)}, u32[]{:S(2)}, u32[]{:S(2)}) collective-permute-start(bf16[1056,256]{1,0:T(8,128)(2,1)} %get-tuple-element.69), channel_id=1, source_target_pairs={{0,16},{8,24},{16,0},{24,8},{1,17},{9,25},{17,1},{25,9},{2,18},{10... | collective-permute-start | bytes 1622024 | tf_op jit(solution)/shard_map/ppermute | solution.py:271
  326.7 25.5 %collective-permute-start.30 = (bf16[2112,256]{1,0:T(8,128)(2,1)S(1)}, bf16[2112,256]{1,0:T(8,128)(2,1)S(1)}, u32[]{:S(2)}, u32[]{:S(2)}) collective-permute-start(bf16[2112,256]{1,0:T(8,128)(2,1)S(1)} %pad_maximum_fusion.9), channel_id=1, source_target_pairs={{0,8},{8,0},{16,24},{24,16},{1,9},{9,1},{17,25},{25,17},{2,10},{10... | collective-permute-start | bytes 3244040 | tf_op jit(solution)/shard_map/ppermute | solution.py:271
  328.2 25.2 %collective-permute-start.32 = (bf16[2112,256]{1,0:T(8,128)(2,1)S(1)}, bf16[2112,256]{1,0:T(8,128)(2,1)S(1)}, u32[]{:S(2)}, u32[]{:S(2)}) collective-permute-start(bf16[2112,256]{1,0:T(8,128)(2,1)S(1)} %copy-done.17), channel_id=1, source_target_pairs={{0,16},{8,24},{16,0},{24,8},{1,17},{9,25},{17,1},{25,9},{2,18},{10... | collective-permute-start | bytes 3244040 | tf_op jit(solution)/shard_map/ppermute | solution.py:271
  356.2 9.6 %collective-permute-start.37 = (bf16[512,256]{1,0:T(8,128)(2,1)S(1)}, bf16[512,256]{1,0:T(8,128)(2,1)S(1)}, u32[]{:S(2)}, u32[]{:S(2)}) collective-permute-start(bf16[512,256]{1,0:T(8,128)(2,1)S(1)} %get-tuple-element.95), channel_id=1, source_target_pairs={{0,24},{8,16},{16,8},{24,0},{1,25},{9,17},{17,9},{25,1},{2,26},{10... | collective-permute-start | bytes 786440 | tf_op jit(solution)/shard_map/ppermute | solution.py:271
  358.6 9.7 %collective-permute-start.36 = (bf16[512,256]{1,0:T(8,128)(2,1)S(1)}, bf16[512,256]{1,0:T(8,128)(2,1)}, u32[]{:S(2)}, u32[]{:S(2)}) collective-permute-start(bf16[512,256]{1,0:T(8,128)(2,1)S(1)} %get-tuple-element.96), channel_id=1, source_target_pairs={{0,16},{8,24},{16,0},{24,8},{1,17},{9,25},{17,1},{25,9},{2,18},{10... | collective-permute-start | bytes 786440 | tf_op jit(solution)/shard_map/ppermute | solution.py:271
  375.7 16.3 %collective-permute-start.34 = (bf16[512,128]{1,0:T(8,128)(2,1)S(1)}, bf16[512,128]{1,0:T(8,128)(2,1)S(1)}, u32[]{:S(2)}, u32[]{:S(2)}) collective-permute-start(bf16[512,128]{1,0:T(8,128)(2,1)S(1)} %dynamic-slice_bitcast_fusion.4), channel_id=1, source_target_pairs={{0,4},{4,0},{1,5},{5,1},{2,6},{6,2},{3,7},{7,3},{8,12},{12,8},{9,1... | collective-permute-start | bytes 393224 | tf_op jit(solution)/shard_map/ppermute | solution.py:209
  (61 other events, 453.5 us)
Sparse Core Ops, SparseCore 0:
  50.2 30.1 all-gather.6
  88.3 78.8 all-gather.4
  207.0 75.2 reduce-scatter.5
  299.7 25.4 reduce-scatter.3
  355.2 32.6 reduce-scatter.7

commit v4 on v3

--- a/solution.py
+++ b/solution.py
@@ -11,7 +11,7 @@
 HD = 64
 LEN = 1024
 PAIR = 2 * HD
-QB = 256
+QB = 1024
 VMEM = 56 * 1024 * 1024
 ALL = ("chip", "core", "tensor")
 CHIPS = ("chip", "tensor")
@@ -213,9 +213,9 @@
     return jnp.concatenate((value, to_other(value)), axis=0)
 
 
-def summed_rows(rows, weight, dot):
+def summed_rows(rows, weight, dot, ready=()):
     half = rows.shape[0] // 2
-    away = to_other(dot(rows[half:], weight).astype(BF16))
+    away = to_other(after(dot(rows[half:], weight).astype(BF16), *ready))
     return dot(rows[:half], weight) + away.astype(F32)
 
 
@@ -417,8 +417,7 @@
         second = after(shard[bounds[1] : bounds[3]], blocks[0])
         mid_blocks = layer_near(second)
         (third,) = assemble(chip, third, (units,))
-        w_down = lax.all_gather(after(third[0], mid_blocks[0]), "tensor", axis=0, tiled=True)
-        cot = swap(after(cotangent, w_down))
+        w_down = lax.all_gather(after(third[0], blocks[1]), "tensor", axis=0, tiled=True)
         w_qkv = w_qkv.reshape(-1, width)
     else:
 
@@ -446,8 +445,6 @@
     bias_up = bias_up.reshape(-1)
 
     joint = (nt(seen, w_qkv) + bias_qkv).astype(BF16)
-    if not small:
-        cot = swap(cotangent)
     half = n_ten // 2
     context, lse = attend(joint, n_ten, 0, half)
     if small:
@@ -462,6 +459,7 @@
     middle = unit_mid * gain_mid + shift_mid
     seen_middle = both_rows(middle.astype(BF16))
     hidden, slope = gelu_pair(nt(seen_middle, w_up) + bias_up)
+    cot = swap(after(cotangent, w_down, hidden))
     branch_two = summed_rows(hidden, w_down, nn)
     unit_end, inverse_end = normalized(middle + branch_two + bias_down)
     encoded = (unit_end * gain_end + shift_end).astype(BF16)
@@ -499,10 +497,9 @@
         middle_grad, unit_mid, inverse_mid, gain_mid
     )
     seen_first = both_rows(first_grad.astype(BF16))
-    if small:
-        up_far = [after(part, first_grad) for part in up_far]
-        up_layer = scatter_near(up_block, *up_far)
     context_grad = nt(seen_first, w_out).astype(BF16)
+    if small:
+        up_layer = scatter_near(up_block, *up_far, (context_grad,))
     if not small:
         out_sum = tn(context, seen_first)
     given = (joint, context_grad, context, lse, n_ten)

time: 410 us -> 389 us (0.949)
  Pallas kernels: 72.3 us -> 55.3 us
  waiting for transfers between devices: 87.3 us -> 99.8 us
  local copies, waits for them, and re-layouts: 30.7 us -> 22.9 us
    ppermute x22, waiting for transfers between devices: 53.6 us -> 72.9 us  [to_chip(): return lax.ppermute(value, 'chip', [(i, i ^ move) for i in range(4)])]
    pallas_call x2, Pallas kernels: 29.9 us -> 17.1 us  [attend(): pl.pallas_call(without(kept, attend_kernel), grid=(last - first,), in_spe...]
    unnamed x98 -> x112, local copies, waits for them, and re-layouts: 11.6 us -> 6.99 us
    pallas_call x2, Pallas kernels: 30.2 us -> 25.8 us  [attend_back(): pl.pallas_call(without(kept, attend_back_kernel), grid=(last - first,), i...]
  transfers between devices with their start and end apart: 45 -> 45, of which waited for: 18 -> 24; matrix products, arithmetic and copies ran while one was open for 28% -> 28% of each run, Pallas kernels for 18% -> 14%
where the time goes in v4:
time: 389 us; the launch traced here: 386 us
  waiting for transfers between devices  99.8 us (26%)
  matrix products  92.1 us (24%)
  Pallas kernels  55.3 us (14%)
  starting transfers between devices  47.4 us (12%)
  other arithmetic  27.2 us (7%)
  blocking collectives  25.4 us (7%)
  local copies, waits for them, and re-layouts  22.9 us (6%)
  between operations  15.5 us (4%)
    ppermute x22, waiting for transfers between devices, to_chip(): return lax.ppermute(value, 'chip', [(i, i ^ move) for i in range(4)])  72.9 us
    dot_general x13, matrix products, tn(): lax.dot_general(left, right, (((0,), (0,)), ((), ())), preferred_element_...  31.2 us
    dot_general x4, matrix products, nt(): lax.dot_general(left, right, (((1,), (1,)), ((), ())), preferred_element_...  31 us
    ppermute x22, starting transfers between devices, to_chip(): return lax.ppermute(value, 'chip', [(i, i ^ move) for i in range(4)])  30.2 us
    dot_general x8, matrix products, nn(): lax.dot_general(left, right, (((1,), (0,)), ((), ())), preferred_element_...  29.8 us
    pallas_call x2, Pallas kernels, attend_back(): pl.pallas_call(without(kept, attend_back_kernel), grid=(last - first,), i...  25.8 us
    all_gather x1, blocking collectives, layer_near(): own = after(lax.all_gather(part, 'tensor', axis=0, tiled=False), *ready)  25.4 us
    pallas_call x2, Pallas kernels, attend(): pl.pallas_call(without(kept, attend_kernel), grid=(last - first,), in_spe...  17.1 us
  transfers between devices with their start and end apart: 45, of which 24 were waited for; matrix products, arithmetic and copies ran while one was open for 28% of the time, Pallas kernels for 14%

profile of v4, /device:TPU:0, one launch (start us, length us, event | category | flops | bytes accessed | tf_op | source)
XLA Modules:
  0.0 385.7 jit_solution(5677144402290216845)
XLA Ops:
  13.5 4.0 %collective-permute-start.6 = (bf16[1,512,256]{2,1,0:T(8,128)(2,1)S(1)}, bf16[1,512,256]{2,1,0:T(8,128)(2,1)S(1)}, u32[]{:S(2)}, u32[]{:S(2)}) collective-permute-start(bf16[1,512,256]{2,1,0:T(8,128)(2,1)S(1)} %maximum_bitcast_fusion.own_ref), channel_id=1, source_target_pairs={{0,24},{8,16},{16,8},{24,0},{1,25},{9,17},{17,9},{25,1},{2,26},{10... | collective-permute-start | bytes 786440 | tf_op jit(solution)/shard_map/ppermute | solution.py:271
  18.9 25.4 %all-gather = bf16[1600,256]{1,0:T(8,128)(2,1)S(1)} all-gather(bf16[400,256]{1,0:T(8,128)(2,1)S(1)} %fusion.70), channel_id=2, replica_groups=mesh['chip'=4,'core'=2,'tensor'=4] {'tensor'}, dimensions={0}, use_global_device_ids=true | all-gather | bytes 1024000 | tf_op jit(solution)/shard_map/all_gather | solution.py:279
  48.6 15.2 %collective-permute-done.8.y_ref = bf16[4,400,256]{2,1,0:T(8,128)(2,1)S(1)} collective-permute-done((bf16[4,400,256]{2,1,0:T(8,128)(2,1)S(1)}, bf16[4,400,256]{2,1,0:T(8,128)(2,1)S(1)}, u32[]{:S(2)}, u32[]{:S(2)}) %collective-permute-start.8) | collective-permute-done | bytes 819232 | tf_op jit(solution)/shard_map/ppermute | solution.py:271
  79.8 4.6 %assemble.3 = bf16[4,384,1024]{2,1,0:T(8,128)(2,1)} custom-call(s32[1]{0:T(128)} %bitcast.chip_ref, bf16[4,400,256]{2,1,0:T(8,128)(2,1)} %bitcast.156, bf16[4,400,256]{2,1,0:T(8,128)(2,1)} %copy-done.17, bf16[4,400,256]{2,1,0:T(8,128)(2,1)} %copy-done.16, bf16[2,400,256]{2,1,0:T(8,128)(2,1)} %copy-done.30, bf16[2,400,256]{2,1,0:T(8,128)(2,1)} %copy-done.31), custom_call_target="tpu_custom_call" | custom-call | bytes 1600 | tf_op jit(solution)/shard_map/assemble/pallas_call | solution.py:253
  84.4 7.1 %add_convert_fusion.refs_0_.refs_1_.refs_2_.refs_3_.refs_4_ = bf16[1024,1536]{1,0:T(8,128)(2,1)} fusion(bf16[1024,1024]{1,0:T(8,128)(2,1)S(1)} %copy-done.29, bf16[1536,1024]{1,0:T(8,128)(2,1)} %bitcast.157, f32[1536]{0:T(1024)S(1)} %add.229), kind=kOutput, calls=%fused_computation.9 | convolution fusion | flops 3224371200 | bytes 8394752 | tf_op jit(solution)/shard_map/dot_general | solution.py:25
  91.5 8.5 %attend.2 = (bf16[1024,512]{1,0:T(8,128)(2,1)}, f32[4,2,1024]{2,1,0:T(2,128)}) custom-call(bf16[1024,1536]{1,0:T(8,128)(2,1)} %add_convert_fusion.refs_0_.refs_1_.refs_2_.refs_3_.refs_4_, bf16[1024,1536]{1,0:T(8,128)(2,1)} %add_convert_fusion.refs_0_.refs_1_.refs_2_.refs_3_.refs_4_, bf16[1024,1536]{1,0:T(8,128)(2,1)} %add_convert_fusion.refs_0_.refs_1_.refs_2_.refs_3_.refs_4_), custom_call_target="tpu_custom_call" | custom-call | flops 262144 | bytes 2048 | tf_op jit(solution)/shard_map/attend/pallas_call | solution.py:81
  100.0 7.8 %collective-permute-done.11.x_ref = bf16[4,640,256]{2,1,0:T(8,128)(2,1)S(1)} collective-permute-done((bf16[4,640,256]{2,1,0:T(8,128)(2,1)}, bf16[4,640,256]{2,1,0:T(8,128)(2,1)S(1)}, u32[]{:S(2)}, u32[]{:S(2)}) %collective-permute-start.11) | collective-permute-done | bytes 1310752 | tf_op jit(solution)/shard_map/ppermute | solution.py:271
  110.0 8.5 %attend.3 = (bf16[1024,512]{1,0:T(8,128)(2,1)}, f32[4,2,1024]{2,1,0:T(2,128)}) custom-call(bf16[1024,512]{1,0:T(8,128)(2,1)} %get-tuple-element.47.refs_0_, f32[4,2,1024]{2,1,0:T(2,128)} %get-tuple-element.48.refs_1_, bf16[1024,1536]{1,0:T(8,128)(2,1)} %add_convert_fusion.refs_0_.refs_1_.refs_2_.refs_3_.refs_4_, ...), custom_call_target="tpu_custom_call", output_to_operand_aliasing={{0}: (0, {}), {1}: (1, {})} | custom-call | flops 262144 | bytes 2048 | tf_op jit(solution)/shard_map/attend/pallas_call | solution.py:81
  118.5 4.1 %collective-permute-done.14.refs_1_ = bf16[2,640,256]{2,1,0:T(8,128)(2,1)S(1)} collective-permute-done((bf16[2,640,256]{2,1,0:T(8,128)(2,1)S(1)}, bf16[2,640,256]{2,1,0:T(8,128)(2,1)S(1)}, u32[]{:S(2)}, u32[]{:S(2)}) %collective-permute-start.14) | collective-permute-done | bytes 655392 | tf_op jit(solution)/shard_map/ppermute | solution.py:271
  124.3 5.4 %assemble.4 = (bf16[4,128,1024]{2,1,0:T(8,128)(2,1)}, bf16[4,512,1024]{2,1,0:T(8,128)(2,1)}) custom-call(s32[1]{0:T(128)} %bitcast.chip_ref, bf16[4,640,256]{2,1,0:T(8,128)(2,1)} %bitcast.165, bf16[4,640,256]{2,1,0:T(8,128)(2,1)} %copy-done.13, bf16[4,640,256]{2,1,0:T(8,128)(2,1)} %copy-done.12, bf16[2,640,256]{2,1,0:T(8,128)(2,1)} %copy-done.28, ...), custom_call_target="tpu_custom_call" | custom-call | bytes 2560 | tf_op jit(solution)/shard_map/assemble/pallas_call | solution.py:253
  141.0 10.4 %multiply_convert_fusion.1 = (bf16[1024,2048]{1,0:T(8,128)(2,1)}, f32[1024,2048]{1,0:T(8,128)}) fusion(f32[2048]{0:T(1024)S(1)} %bitcast.185, bf16[2048,1024]{1,0:T(8,128)(2,1)} %bitcast.189, bf16[512,1024]{1,0:T(8,128)(2,1)} %collective-permute-done.16, bf16[512,1024]{1,0:T(8,128)(2,1)S(1)} %fusion.22), kind=kOutput, calls=%fused_computation.7 | convolution fusion | flops 4311744512 | bytes 18882560 | tf_op jit(solution)/shard_map/dot_general | solution.py:25
  151.4 7.0 %all-gather.5.cloned.1.call-done = bf16[2048,1024]{1,0:T(8,128)(2,1)} async-done(((bf16[512,1024]{1,0:T(8,128)(2,1)}), bf16[2048,1024]{1,0:T(8,128)(2,1)}) %all-gather.5.cloned.1.call-update) | async-done | bytes 4194320 | tf_op jit(solution)/shard_map/all_gather | solution.py:420
  158.4 6.1 %fusion.35 = bf16[512,1024]{1,0:T(8,128)(2,1)} fusion(bf16[2048,1024]{1,0:T(8,128)(2,1)} %all-gather.5.cloned.1.call-done, bf16[1024,2048]{1,0:T(8,128)(2,1)} %get-tuple-element.136), kind=kOutput, calls=%fused_computation.74 | convolution fusion | flops 2148007936 | bytes 7340032 | tf_op jit(solution)/shard_map/dot_general | solution.py:29
  167.6 5.8 %fusion.104 = (f32[512]{0:T(512)S(1)}, f32[512,1024]{1,0:T(8,128)S(1)}) fusion(f32[1024]{0:T(1024)S(1)} %add.248, bf16[512,1024]{1,0:T(8,128)(2,1)} %collective-permute-done.17, bf16[2048,1024]{1,0:T(8,128)(2,1)} %all-gather.5.cloned.1.call-done, bf16[1024,2048]{1,0:T(8,128)(2,1)} %get-tuple-element.136, f32[1024]{0:T(1024)S(1)} %add.238, ...), kind=kOutput, calls=%fused_computation.229 | convolution fusion | flops 2152201728 | bytes 11552768 | tf_op jit(solution)/shard_map/dot_general | solution.py:29
  178.9 7.9 %collective-permute-start.19 = (bf16[512,1024]{1,0:T(8,128)(2,1)}, bf16[512,1024]{1,0:T(8,128)(2,1)}, u32[]{:S(2)}, u32[]{:S(2)}) collective-permute-start(bf16[512,1024]{1,0:T(8,128)(2,1)} %convert_element_type.234), channel_id=1, source_target_pairs={{0,4},{4,0},{1,5},{5,1},{2,6},{6,2},{3,7},{7,3},{8,12},{12,8},{9,1... | collective-permute-start | bytes 3145736 | tf_op jit(solution)/shard_map/ppermute | solution.py:209
  190.6 9.3 %convolution_convert_fusion = bf16[2048,1024]{1,0:T(8,128)(2,1)} fusion(bf16[1024,2048]{1,0:T(8,128)(2,1)} %get-tuple-element.136, bf16[512,1024]{1,0:T(8,128)(2,1)} %collective-permute-done.19, bf16[512,1024]{1,0:T(8,128)(2,1)} %convert_element_type.234), kind=kOutput, calls=%fused_computation.10 | convolution fusion | flops 4301258752 | bytes 10485760 | tf_op jit(solution)/shard_map/dot_general | solution.py:33
  200.0 11.3 %fusion.105 = (bf16[2048]{0:T(1024)(128)(2,1)S(1)}, bf16[1024,2048]{1,0:T(8,128)(2,1)S(1)}) fusion(f32[1024,2048]{1,0:T(8,128)} %get-tuple-element.137, f32[2048]{0:T(1024)S(1)} %bitcast.186, bf16[2048,1024]{1,0:T(8,128)(2,1)} %all-gather.5.cloned.1.call-done, bf16[512,1024]{1,0:T(8,128)(2,1)} %collective-permute-done.19, ...), kind=kOutput, calls=%fused_computation.230 | convolution fusion | flops 4328519680 | bytes 18886656 | tf_op jit(solution)/shard_map/dot_general | solution.py:25
  219.8 3.0 multiply_reduce_fusion
  225.3 4.4 %collective-permute-done.24 = bf16[1024,256]{1,0:T(8,128)(2,1)S(1)} collective-permute-done((bf16[1024,256]{1,0:T(8,128)(2,1)S(1)}, bf16[1024,256]{1,0:T(8,128)(2,1)S(1)}, u32[]{:S(2)}, u32[]{:S(2)}) %collective-permute-start.24) | collective-permute-done | bytes 524320 | tf_op jit(solution)/shard_map/ppermute | solution.py:271
  239.5 12.9 %attend_back.2 = (bf16[1024,1536]{1,0:T(8,128)(2,1)}, f32[4,2,128]{2,1,0:T(2,128)}) custom-call(bf16[1024,1536]{1,0:T(8,128)(2,1)} %add_convert_fusion.refs_0_.refs_1_.refs_2_.refs_3_.refs_4_, bf16[1024,1536]{1,0:T(8,128)(2,1)} %add_convert_fusion.refs_0_.refs_1_.refs_2_.refs_3_.refs_4_, ...), custom_call_target="tpu_custom_call" | custom-call | flops 262144 | bytes 2048 | tf_op jit(solution)/shard_map/attend_back/pallas_call | solution.py:151
  262.5 13.0 %attend_back.3 = (bf16[1024,1536]{1,0:T(8,128)(2,1)}, f32[4,2,128]{2,1,0:T(2,128)}) custom-call(bf16[1024,1536]{1,0:T(8,128)(2,1)} %get-tuple-element.64.refs_0_, f32[4,2,128]{2,1,0:T(2,128)} %get-tuple-element.65.refs_1_, bf16[1024,1536]{1,0:T(8,128)(2,1)} %add_convert_fusion.refs_0_.refs_1_.refs_2_.refs_3_.refs_4_, ...), custom_call_target="tpu_custom_call", output_to_operand_aliasing={{0}: (0, {}), {1}: (1, {})} | custom-call | flops 262144 | bytes 2048 | tf_op jit(solution)/shard_map/attend_back/pallas_call | solution.py:151
  276.6 4.0 %convolution_convert_fusion.2 = bf16[1536,256]{1,0:T(8,128)(2,1)} fusion(bf16[1024,1536]{1,0:T(8,128)(2,1)} %get-tuple-element.66, bf16[1024,1024]{1,0:T(8,128)(2,1)} %constant_dynamic-update-slice_fusion, s32[]{:T(128)S(6)} %select_n.172), kind=kOutput, calls=%fused_computation.26 | convolution fusion | flops 805699584 | bytes 4456452 | tf_op jit(solution)/shard_map/dot_general | solution.py:33
  283.8 4.3 %fusion.31 = bf16[512,1024]{1,0:T(8,128)(2,1)} fusion(bf16[1536,1024]{1,0:T(8,128)(2,1)S(1)} %bitcast.158, bf16[1024,1536]{1,0:T(8,128)(2,1)} %get-tuple-element.66), kind=kOutput, calls=%fused_computation.71 | convolution fusion | flops 1611137024 | bytes 5767168 | tf_op jit(solution)/shard_map/dot_general | solution.py:29
  288.6 3.3 convolution_convert_fusion.3
  295.9 5.1 %collective-permute-done.31 = bf16[1056,256]{1,0:T(8,128)(2,1)S(1)} collective-permute-done((bf16[1056,256]{1,0:T(8,128)(2,1)}, bf16[1056,256]{1,0:T(8,128)(2,1)S(1)}, u32[]{:S(2)}, u32[]{:S(2)}) %collective-permute-start.31) | collective-permute-done | bytes 540704 | tf_op jit(solution)/shard_map/ppermute | solution.py:271
  302.3 3.3 reduce-scatter.4.cloned.1.call-done
  305.6 3.6 collective-permute-done.29
  313.6 3.5 add_convert_fusion.2
  323.6 12.3 %collective-permute-done.30 = bf16[2112,256]{1,0:T(8,128)(2,1)S(1)} collective-permute-done((bf16[2112,256]{1,0:T(8,128)(2,1)S(1)}, bf16[2112,256]{1,0:T(8,128)(2,1)S(1)}, u32[]{:S(2)}, u32[]{:S(2)}) %collective-permute-start.30) | collective-permute-done | bytes 1081376 | tf_op jit(solution)/shard_map/ppermute | solution.py:271
  345.6 5.1 %collective-permute-done.37 = bf16[512,256]{1,0:T(8,128)(2,1)S(1)} collective-permute-done((bf16[512,256]{1,0:T(8,128)(2,1)S(1)}, bf16[512,256]{1,0:T(8,128)(2,1)S(1)}, u32[]{:S(2)}, u32[]{:S(2)}) %collective-permute-start.37) | collective-permute-done | bytes 262176 | tf_op jit(solution)/shard_map/ppermute | solution.py:271
  350.7 4.8 %collective-permute-done.36 = bf16[512,256]{1,0:T(8,128)(2,1)} collective-permute-done((bf16[512,256]{1,0:T(8,128)(2,1)S(1)}, bf16[512,256]{1,0:T(8,128)(2,1)}, u32[]{:S(2)}, u32[]{:S(2)}) %collective-permute-start.36) | collective-permute-done | bytes 262176 | tf_op jit(solution)/shard_map/ppermute | solution.py:271
  360.4 9.5 %reduce-scatter.8.cloned.1.call-done = bf16[1,528,256]{2,1,0:T(8,128)(2,1)} async-done(((bf16[4,528,256]{2,1,0:T(8,128)(2,1)}), bf16[1,528,256]{2,1,0:T(8,128)(2,1)}) %reduce-scatter.8.cloned.1.call-update) | async-done | bytes 270352 | tf_op jit(solution)/shard_map/reduce_scatter | solution.py:477
  (350 shorter events, 129.6 us)
Async XLA Ops:
  7.3 69.2 %all-gather.7.cloned.1.call-start = ((), (), s32[]{:S(2)}) async-start(), calls=%async_computation.7 | async-start | bytes 1638400 | tf_op jit(solution)/shard_map/all_gather | solution.py:279
  11.5 33.0 %collective-permute-start = (bf16[512,1024]{1,0:T(8,128)(2,1)}, bf16[512,1024]{1,0:T(8,128)(2,1)S(1)}, u32[]{:S(2)}, u32[]{:S(2)}) collective-permute-start(bf16[512,1024]{1,0:T(8,128)(2,1)} %param.15), channel_id=1, source_target_pairs={{0,0},{4,1},{1,4},{5,5},{2,2},{6,3},{3,6},{7,7},{8,8},{12,9},{9,12... | collective-permute-start | bytes 3145736 | tf_op jit(solution)/shard_map/ppermute | solution.py:358
  13.5 30.8 %collective-permute-start.6 = (bf16[1,512,256]{2,1,0:T(8,128)(2,1)S(1)}, bf16[1,512,256]{2,1,0:T(8,128)(2,1)S(1)}, u32[]{:S(2)}, u32[]{:S(2)}) collective-permute-start(bf16[1,512,256]{2,1,0:T(8,128)(2,1)S(1)} %maximum_bitcast_fusion.own_ref), channel_id=1, source_target_pairs={{0,24},{8,16},{16,8},{24,0},{1,25},{9,17},{17,9},{25,1},{2,26},{10... | collective-permute-start | bytes 786440 | tf_op jit(solution)/shard_map/ppermute | solution.py:271
  17.5 26.9 %collective-permute-start.5 = (bf16[1,512,256]{2,1,0:T(8,128)(2,1)S(1)}, bf16[1,512,256]{2,1,0:T(8,128)(2,1)S(1)}, u32[]{:S(2)}, u32[]{:S(2)}) collective-permute-start(bf16[1,512,256]{2,1,0:T(8,128)(2,1)S(1)} %maximum_bitcast_fusion.own_ref), channel_id=1, source_target_pairs={{0,16},{8,24},{16,0},{24,8},{1,17},{9,25},{17,1},{25,9},{2,18},{10... | collective-permute-start | bytes 786440 | tf_op jit(solution)/shard_map/ppermute | solution.py:271
  18.0 26.4 %collective-permute-start.4 = (bf16[1,512,256]{2,1,0:T(8,128)(2,1)S(1)}, bf16[1,512,256]{2,1,0:T(8,128)(2,1)S(1)}, u32[]{:S(2)}, u32[]{:S(2)}) collective-permute-start(bf16[1,512,256]{2,1,0:T(8,128)(2,1)S(1)} %maximum_bitcast_fusion.own_ref), channel_id=1, source_target_pairs={{0,8},{8,0},{16,24},{24,16},{1,9},{9,1},{17,25},{25,17},{2,10},{10... | collective-permute-start | bytes 786440 | tf_op jit(solution)/shard_map/ppermute | solution.py:271
  45.3 113.2 %all-gather.5.cloned.1.call-start = ((), (), s32[]{:S(2)}) async-start(), calls=%async_computation.3 | async-start | bytes 5242880 | tf_op jit(solution)/shard_map/all_gather | solution.py:420
  45.6 18.3 %collective-permute-start.8 = (bf16[4,400,256]{2,1,0:T(8,128)(2,1)S(1)}, bf16[4,400,256]{2,1,0:T(8,128)(2,1)S(1)}, u32[]{:S(2)}, u32[]{:S(2)}) collective-permute-start(bf16[4,400,256]{2,1,0:T(8,128)(2,1)S(1)} %bitcast.152), channel_id=1, source_target_pairs={{0,16},{8,24},{16,0},{24,8},{1,17},{9,25},{17,1},{25,9},{2,18},{10... | collective-permute-start | bytes 2457608 | tf_op jit(solution)/shard_map/ppermute | solution.py:271
  47.2 19.1 %collective-permute-start.7 = (bf16[4,400,256]{2,1,0:T(8,128)(2,1)S(1)}, bf16[4,400,256]{2,1,0:T(8,128)(2,1)S(1)}, u32[]{:S(2)}, u32[]{:S(2)}) collective-permute-start(bf16[4,400,256]{2,1,0:T(8,128)(2,1)S(1)} %bitcast.153), channel_id=1, source_target_pairs={{0,8},{8,0},{16,24},{24,16},{1,9},{9,1},{17,25},{25,17},{2,10},{10... | collective-permute-start | bytes 2457608 | tf_op jit(solution)/shard_map/ppermute | solution.py:271
  48.6 23.7 %collective-permute-start.1 = (bf16[512,1024]{1,0:T(8,128)(2,1)}, bf16[512,1024]{1,0:T(8,128)(2,1)}, u32[]{:S(2)}, u32[]{:S(2)}) collective-permute-start(bf16[512,1024]{1,0:T(8,128)(2,1)} %copy-done.22), channel_id=1, source_target_pairs={{0,4},{4,0},{1,5},{5,1},{2,6},{6,2},{3,7},{7,3},{8,12},{12,8},{9,1... | collective-permute-start | bytes 3145736 | tf_op jit(solution)/shard_map/ppermute | solution.py:209
  64.8 9.9 %collective-permute-start.9 = (bf16[2,400,256]{2,1,0:T(8,128)(2,1)}, bf16[2,400,256]{2,1,0:T(8,128)(2,1)S(1)}, u32[]{:S(2)}, u32[]{:S(2)}) collective-permute-start(bf16[2,400,256]{2,1,0:T(8,128)(2,1)} %slice.269), channel_id=1, source_target_pairs={{0,8},{8,0},{16,24},{24,16},{1,9},{9,1},{17,25},{25,17},{2,10},{10... | collective-permute-start | bytes 1228808 | tf_op jit(solution)/shard_map/ppermute | solution.py:271
  67.1 8.6 %collective-permute-start.10 = (bf16[2,400,256]{2,1,0:T(8,128)(2,1)}, bf16[2,400,256]{2,1,0:T(8,128)(2,1)S(1)}, u32[]{:S(2)}, u32[]{:S(2)}) collective-permute-start(bf16[2,400,256]{2,1,0:T(8,128)(2,1)} %slice.270), channel_id=1, source_target_pairs={{0,16},{8,24},{16,0},{24,8},{1,17},{9,25},{17,1},{25,9},{2,18},{10... | collective-permute-start | bytes 1228808 | tf_op jit(solution)/shard_map/ppermute | solution.py:271
  72.1 216.0 %reduce-scatter.6.cloned.1.call-start = ((), (), s32[]{:S(2)}) async-start(), calls=%async_computation.5 | async-start | bytes 5242880 | tf_op jit(solution)/shard_map/reduce_scatter | solution.py:488
  76.5 31.3 %collective-permute-start.12 = (bf16[4,640,256]{2,1,0:T(8,128)(2,1)}, bf16[4,640,256]{2,1,0:T(8,128)(2,1)S(1)}, u32[]{:S(2)}, u32[]{:S(2)}) collective-permute-start(bf16[4,640,256]{2,1,0:T(8,128)(2,1)} %bitcast.163), channel_id=1, source_target_pairs={{0,16},{8,24},{16,0},{24,8},{1,17},{9,25},{17,1},{25,9},{2,18},{10... | collective-permute-start | bytes 3932168 | tf_op jit(solution)/shard_map/ppermute | solution.py:271
  78.0 29.8 %collective-permute-start.11 = (bf16[4,640,256]{2,1,0:T(8,128)(2,1)}, bf16[4,640,256]{2,1,0:T(8,128)(2,1)S(1)}, u32[]{:S(2)}, u32[]{:S(2)}) collective-permute-start(bf16[4,640,256]{2,1,0:T(8,128)(2,1)} %bitcast.164), channel_id=1, source_target_pairs={{0,8},{8,0},{16,24},{24,16},{1,9},{9,1},{17,25},{25,17},{2,10},{10... | collective-permute-start | bytes 3932168 | tf_op jit(solution)/shard_map/ppermute | solution.py:271
  107.9 14.8 %collective-permute-start.14 = (bf16[2,640,256]{2,1,0:T(8,128)(2,1)S(1)}, bf16[2,640,256]{2,1,0:T(8,128)(2,1)S(1)}, u32[]{:S(2)}, u32[]{:S(2)}) collective-permute-start(bf16[2,640,256]{2,1,0:T(8,128)(2,1)S(1)} %slice.222), channel_id=1, source_target_pairs={{0,16},{8,24},{16,0},{24,8},{1,17},{9,25},{17,1},{25,9},{2,18},{10... | collective-permute-start | bytes 1966088 | tf_op jit(solution)/shard_map/ppermute | solution.py:271
  108.5 14.4 %collective-permute-start.13 = (bf16[2,640,256]{2,1,0:T(8,128)(2,1)S(1)}, bf16[2,640,256]{2,1,0:T(8,128)(2,1)S(1)}, u32[]{:S(2)}, u32[]{:S(2)}) collective-permute-start(bf16[2,640,256]{2,1,0:T(8,128)(2,1)S(1)} %slice.221), channel_id=1, source_target_pairs={{0,8},{8,0},{16,24},{24,16},{1,9},{9,1},{17,25},{25,17},{2,10},{10... | collective-permute-start | bytes 1966088 | tf_op jit(solution)/shard_map/ppermute | solution.py:271
  164.8 8.9 %collective-permute-start.18 = (bf16[512,1024]{1,0:T(8,128)(2,1)}, bf16[512,1024]{1,0:T(8,128)(2,1)S(1)}, u32[]{:S(2)}, u32[]{:S(2)}) collective-permute-start(bf16[512,1024]{1,0:T(8,128)(2,1)} %param.29), channel_id=1, source_target_pairs={{0,0},{4,1},{1,4},{5,5},{2,2},{6,3},{3,6},{7,7},{8,8},{12,9},{9,12... | collective-permute-start | bytes 3145736 | tf_op jit(solution)/shard_map/ppermute | solution.py:358
  178.9 11.6 %collective-permute-start.19 = (bf16[512,1024]{1,0:T(8,128)(2,1)}, bf16[512,1024]{1,0:T(8,128)(2,1)}, u32[]{:S(2)}, u32[]{:S(2)}) collective-permute-start(bf16[512,1024]{1,0:T(8,128)(2,1)} %convert_element_type.234), channel_id=1, source_target_pairs={{0,4},{4,0},{1,5},{5,1},{2,6},{6,2},{3,7},{7,3},{8,12},{12,8},{9,1... | collective-permute-start | bytes 3145736 | tf_op jit(solution)/shard_map/ppermute | solution.py:209
  199.9 105.6 %reduce-scatter.4.cloned.1.call-start = ((), (), s32[]{:S(2)}) async-start(), calls=%async_computation.4 | async-start | bytes 1310720 | tf_op jit(solution)/shard_map/reduce_scatter | solution.py:477
  215.3 14.4 %collective-permute-start.24 = (bf16[1024,256]{1,0:T(8,128)(2,1)S(1)}, bf16[1024,256]{1,0:T(8,128)(2,1)S(1)}, u32[]{:S(2)}, u32[]{:S(2)}) collective-permute-start(bf16[1024,256]{1,0:T(8,128)(2,1)S(1)} %get-tuple-element.96), channel_id=1, source_target_pairs={{0,8},{8,0},{16,24},{24,16},{1,9},{9,1},{17,25},{25,17},{2,10},{10... | collective-permute-start | bytes 1572872 | tf_op jit(solution)/shard_map/ppermute | solution.py:271
  216.9 14.0 %collective-permute-start.22 = (bf16[1024,256]{1,0:T(8,128)(2,1)S(1)}, bf16[1024,256]{1,0:T(8,128)(2,1)S(1)}, u32[]{:S(2)}, u32[]{:S(2)}) collective-permute-start(bf16[1024,256]{1,0:T(8,128)(2,1)S(1)} %get-tuple-element.95), channel_id=1, source_target_pairs={{0,16},{8,24},{16,0},{24,8},{1,17},{9,25},{17,1},{25,9},{2,18},{10... | collective-permute-start | bytes 1572872 | tf_op jit(solution)/shard_map/ppermute | solution.py:271
  233.4 25.0 %collective-permute-start.23 = (bf16[2048,256]{1,0:T(8,128)(2,1)S(1)}, bf16[2048,256]{1,0:T(8,128)(2,1)}, u32[]{:S(2)}, u32[]{:S(2)}) collective-permute-start(bf16[2048,256]{1,0:T(8,128)(2,1)S(1)} %pad_maximum_fusion.11), channel_id=1, source_target_pairs={{0,8},{8,0},{16,24},{24,16},{1,9},{9,1},{17,25},{25,17},{2,10},{10... | collective-permute-start | bytes 3145736 | tf_op jit(solution)/shard_map/ppermute | solution.py:271
  234.9 24.7 %collective-permute-start.25 = (bf16[2048,256]{1,0:T(8,128)(2,1)S(1)}, bf16[2048,256]{1,0:T(8,128)(2,1)}, u32[]{:S(2)}, u32[]{:S(2)}) collective-permute-start(bf16[2048,256]{1,0:T(8,128)(2,1)S(1)} %pad_maximum_fusion.12), channel_id=1, source_target_pairs={{0,16},{8,24},{16,0},{24,8},{1,17},{9,25},{17,1},{25,9},{2,18},{10... | collective-permute-start | bytes 3145736 | tf_op jit(solution)/shard_map/ppermute | solution.py:271
  280.6 89.4 %reduce-scatter.8.cloned.1.call-start = ((), (), s32[]{:S(2)}) async-start(), calls=%async_computation.6 | async-start | bytes 1351680 | tf_op jit(solution)/shard_map/reduce_scatter | solution.py:477
  288.1 12.9 %collective-permute-start.31 = (bf16[1056,256]{1,0:T(8,128)(2,1)}, bf16[1056,256]{1,0:T(8,128)(2,1)S(1)}, u32[]{:S(2)}, u32[]{:S(2)}) collective-permute-start(bf16[1056,256]{1,0:T(8,128)(2,1)} %get-tuple-element.71), channel_id=1, source_target_pairs={{0,8},{8,0},{16,24},{24,16},{1,9},{9,1},{17,25},{25,17},{2,10},{10... | collective-permute-start | bytes 1622024 | tf_op jit(solution)/shard_map/ppermute | solution.py:271
  291.9 21.7 %collective-permute-start.27 = (bf16[512,1024]{1,0:T(8,128)(2,1)}, bf16[512,1024]{1,0:T(8,128)(2,1)}, u32[]{:S(2)}, u32[]{:S(2)}) collective-permute-start(bf16[512,1024]{1,0:T(8,128)(2,1)} %fusion.31), channel_id=1, source_target_pairs={{0,4},{4,0},{1,5},{5,1},{2,6},{6,2},{3,7},{7,3},{8,12},{12,8},{9,1... | collective-permute-start | bytes 3145736 | tf_op jit(solution)/shard_map/ppermute | solution.py:209
  294.3 14.8 %collective-permute-start.29 = (bf16[1056,256]{1,0:T(8,128)(2,1)}, bf16[1056,256]{1,0:T(8,128)(2,1)}, u32[]{:S(2)}, u32[]{:S(2)}) collective-permute-start(bf16[1056,256]{1,0:T(8,128)(2,1)} %get-tuple-element.69), channel_id=1, source_target_pairs={{0,16},{8,24},{16,0},{24,8},{1,17},{9,25},{17,1},{25,9},{2,18},{10... | collective-permute-start | bytes 1622024 | tf_op jit(solution)/shard_map/ppermute | solution.py:271
  310.7 25.2 %collective-permute-start.30 = (bf16[2112,256]{1,0:T(8,128)(2,1)S(1)}, bf16[2112,256]{1,0:T(8,128)(2,1)S(1)}, u32[]{:S(2)}, u32[]{:S(2)}) collective-permute-start(bf16[2112,256]{1,0:T(8,128)(2,1)S(1)} %pad_maximum_fusion.9), channel_id=1, source_target_pairs={{0,8},{8,0},{16,24},{24,16},{1,9},{9,1},{17,25},{25,17},{2,10},{10... | collective-permute-start | bytes 3244040 | tf_op jit(solution)/shard_map/ppermute | solution.py:271
  312.0 24.9 %collective-permute-start.32 = (bf16[2112,256]{1,0:T(8,128)(2,1)S(1)}, bf16[2112,256]{1,0:T(8,128)(2,1)S(1)}, u32[]{:S(2)}, u32[]{:S(2)}) collective-permute-start(bf16[2112,256]{1,0:T(8,128)(2,1)S(1)} %copy-done.18), channel_id=1, source_target_pairs={{0,16},{8,24},{16,0},{24,8},{1,17},{9,25},{17,1},{25,9},{2,18},{10... | collective-permute-start | bytes 3244040 | tf_op jit(solution)/shard_map/ppermute | solution.py:271
  339.9 10.8 %collective-permute-start.37 = (bf16[512,256]{1,0:T(8,128)(2,1)S(1)}, bf16[512,256]{1,0:T(8,128)(2,1)S(1)}, u32[]{:S(2)}, u32[]{:S(2)}) collective-permute-start(bf16[512,256]{1,0:T(8,128)(2,1)S(1)} %get-tuple-element.93), channel_id=1, source_target_pairs={{0,24},{8,16},{16,8},{24,0},{1,25},{9,17},{17,9},{25,1},{2,26},{10... | collective-permute-start | bytes 786440 | tf_op jit(solution)/shard_map/ppermute | solution.py:271
  342.3 13.2 %collective-permute-start.36 = (bf16[512,256]{1,0:T(8,128)(2,1)S(1)}, bf16[512,256]{1,0:T(8,128)(2,1)}, u32[]{:S(2)}, u32[]{:S(2)}) collective-permute-start(bf16[512,256]{1,0:T(8,128)(2,1)S(1)} %get-tuple-element.94), channel_id=1, source_target_pairs={{0,16},{8,24},{16,0},{24,8},{1,17},{9,25},{17,1},{25,9},{2,18},{10... | collective-permute-start | bytes 786440 | tf_op jit(solution)/shard_map/ppermute | solution.py:271
  359.4 14.7 %collective-permute-start.34 = (bf16[512,128]{1,0:T(8,128)(2,1)S(1)}, bf16[512,128]{1,0:T(8,128)(2,1)S(1)}, u32[]{:S(2)}, u32[]{:S(2)}) collective-permute-start(bf16[512,128]{1,0:T(8,128)(2,1)S(1)} %dynamic-slice_bitcast_fusion.4), channel_id=1, source_target_pairs={{0,4},{4,0},{1,5},{5,1},{2,6},{6,2},{3,7},{7,3},{8,12},{12,8},{9,1... | collective-permute-start | bytes 393224 | tf_op jit(solution)/shard_map/ppermute | solution.py:209
  (68 other events, 477.9 us)
Sparse Core Ops, SparseCore 0:
  44.6 31.8 all-gather.6
  78.6 79.7 all-gather.4
  200.1 75.2 reduce-scatter.5
  280.7 24.8 reduce-scatter.3
  338.7 31.1 reduce-scatter.7

commit v5 on v4

--- a/solution.py
+++ b/solution.py
@@ -513,7 +513,7 @@
         encoded = after(encoded, up_part)
     encoded = swap(encoded)
     input_grad = summed_rows(qkv_low, w_qkv, nn) + first_grad
-    input_grad = swap(input_grad.astype(BF16)).astype(F32)
+    input_grad = swap(after(input_grad.astype(BF16), encoded)).astype(F32)
 
     def core_halves(part):
         keep = lax.dynamic_slice_in_dim(part, core * slab, slab, axis=1)
@@ -566,7 +566,7 @@
             )
 
         last = scatter_near(last_block, *scatter_far(last_block, (down_rows,)), (up_part,))
-        last = three_sum((after(last[0], input_grad, encoded), *last[1:]))
+        last = three_sum((after(last[0], input_grad), *last[1:]))
         n_qkv = 3 * n_ten * cols
         n_out = n_ten * cols
         last = jnp.concatenate(

time: 389 us -> 387 us (level)
    reduce_scatter x2, waiting for transfers between devices: 12.8 us -> 19.7 us  [member_sum(): return lax.psum_scatter(total, 'tensor', scatter_dimension=0, tiled=False)]
    ppermute x22, waiting for transfers between devices: 72.9 us -> 66.9 us  [to_chip(): return lax.ppermute(value, 'chip', [(i, i ^ move) for i in range(4)])]
    unnamed x112 -> x114, local copies, waits for them, and re-layouts: 6.99 us -> 8.16 us
  transfers between devices with their start and end apart: 45 -> 45, of which waited for: 24 -> 23; matrix products, arithmetic and copies ran while one was open for 28% -> 27% of each run, Pallas kernels for 14% -> 14%
where the time goes in v5:
time: 387 us; the launch traced here: 383 us
  waiting for transfers between devices  102 us (26%)
  matrix products  89.9 us (23%)
  Pallas kernels  55.4 us (14%)
  starting transfers between devices  47.9 us (12%)
  blocking collectives  25.4 us (7%)
  other arithmetic  24.9 us (6%)
  local copies, waits for them, and re-layouts  22.5 us (6%)
  between operations  15.5 us (4%)
    ppermute x22, waiting for transfers between devices, to_chip(): return lax.ppermute(value, 'chip', [(i, i ^ move) for i in range(4)])  66.9 us
    dot_general x13, matrix products, tn(): lax.dot_general(left, right, (((0,), (0,)), ((), ())), preferred_element_...  31.1 us
    dot_general x4, matrix products, nt(): lax.dot_general(left, right, (((1,), (1,)), ((), ())), preferred_element_...  30.9 us
    ppermute x22, starting transfers between devices, to_chip(): return lax.ppermute(value, 'chip', [(i, i ^ move) for i in range(4)])  30.3 us
    dot_general x8, matrix products, nn(): lax.dot_general(left, right, (((1,), (0,)), ((), ())), preferred_element_...  27.9 us
    pallas_call x2, Pallas kernels, attend_back(): pl.pallas_call(without(kept, attend_back_kernel), grid=(last - first,), i...  25.9 us
    all_gather x1, blocking collectives, layer_near(): own = after(lax.all_gather(part, 'tensor', axis=0, tiled=False), *ready)  25.4 us
    reduce_scatter x2, waiting for transfers between devices, member_sum(): return lax.psum_scatter(total, 'tensor', scatter_dimension=0, tiled=False)  19.7 us
  transfers between devices with their start and end apart: 45, of which 23 were waited for; matrix products, arithmetic and copies ran while one was open for 27% of the time, Pallas kernels for 14%

profile of v5, /device:TPU:0, one launch (start us, length us, event | category | flops | bytes accessed | tf_op | source)
XLA Modules:
  0.0 383.3 jit_solution(413681086953434027)
XLA Ops:
  13.5 4.0 %collective-permute-start.6 = (bf16[1,512,256]{2,1,0:T(8,128)(2,1)S(1)}, bf16[1,512,256]{2,1,0:T(8,128)(2,1)S(1)}, u32[]{:S(2)}, u32[]{:S(2)}) collective-permute-start(bf16[1,512,256]{2,1,0:T(8,128)(2,1)S(1)} %maximum_bitcast_fusion.own_ref), channel_id=1, source_target_pairs={{0,24},{8,16},{16,8},{24,0},{1,25},{9,17},{17,9},{25,1},{2,26},{10... | collective-permute-start | bytes 786440 | tf_op jit(solution)/shard_map/ppermute | solution.py:271
  18.9 25.4 %all-gather = bf16[1600,256]{1,0:T(8,128)(2,1)S(1)} all-gather(bf16[400,256]{1,0:T(8,128)(2,1)S(1)} %fusion.70), channel_id=2, replica_groups=mesh['chip'=4,'core'=2,'tensor'=4] {'tensor'}, dimensions={0}, use_global_device_ids=true | all-gather | bytes 1024000 | tf_op jit(solution)/shard_map/all_gather | solution.py:279
  48.7 15.2 %collective-permute-done.8.y_ref = bf16[4,400,256]{2,1,0:T(8,128)(2,1)S(1)} collective-permute-done((bf16[4,400,256]{2,1,0:T(8,128)(2,1)S(1)}, bf16[4,400,256]{2,1,0:T(8,128)(2,1)S(1)}, u32[]{:S(2)}, u32[]{:S(2)}) %collective-permute-start.8) | collective-permute-done | bytes 819232 | tf_op jit(solution)/shard_map/ppermute | solution.py:271
  79.8 4.6 %assemble.3 = bf16[4,384,1024]{2,1,0:T(8,128)(2,1)} custom-call(s32[1]{0:T(128)} %bitcast.chip_ref, bf16[4,400,256]{2,1,0:T(8,128)(2,1)} %bitcast.156, bf16[4,400,256]{2,1,0:T(8,128)(2,1)} %copy-done.20, bf16[4,400,256]{2,1,0:T(8,128)(2,1)} %copy-done.19, bf16[2,400,256]{2,1,0:T(8,128)(2,1)} %copy-done.33, bf16[2,400,256]{2,1,0:T(8,128)(2,1)} %copy-done.34), custom_call_target="tpu_custom_call" | custom-call | bytes 1600 | tf_op jit(solution)/shard_map/assemble/pallas_call | solution.py:253
  84.4 7.1 %add_convert_fusion.refs_0_.refs_1_.refs_2_.refs_3_.refs_4_ = bf16[1024,1536]{1,0:T(8,128)(2,1)} fusion(bf16[1024,1024]{1,0:T(8,128)(2,1)S(1)} %copy-done.32, bf16[1536,1024]{1,0:T(8,128)(2,1)} %bitcast.157, f32[1536]{0:T(1024)S(1)} %add.229), kind=kOutput, calls=%fused_computation.9 | convolution fusion | flops 3224371200 | bytes 8394752 | tf_op jit(solution)/shard_map/dot_general | solution.py:25
  91.5 8.5 %attend.2 = (bf16[1024,512]{1,0:T(8,128)(2,1)}, f32[4,2,1024]{2,1,0:T(2,128)}) custom-call(bf16[1024,1536]{1,0:T(8,128)(2,1)} %add_convert_fusion.refs_0_.refs_1_.refs_2_.refs_3_.refs_4_, bf16[1024,1536]{1,0:T(8,128)(2,1)} %add_convert_fusion.refs_0_.refs_1_.refs_2_.refs_3_.refs_4_, bf16[1024,1536]{1,0:T(8,128)(2,1)} %add_convert_fusion.refs_0_.refs_1_.refs_2_.refs_3_.refs_4_), custom_call_target="tpu_custom_call" | custom-call | flops 262144 | bytes 2048 | tf_op jit(solution)/shard_map/attend/pallas_call | solution.py:81
  100.0 7.8 %collective-permute-done.11.x_ref = bf16[4,640,256]{2,1,0:T(8,128)(2,1)S(1)} collective-permute-done((bf16[4,640,256]{2,1,0:T(8,128)(2,1)}, bf16[4,640,256]{2,1,0:T(8,128)(2,1)S(1)}, u32[]{:S(2)}, u32[]{:S(2)}) %collective-permute-start.11) | collective-permute-done | bytes 1310752 | tf_op jit(solution)/shard_map/ppermute | solution.py:271
  110.0 8.6 %attend.3 = (bf16[1024,512]{1,0:T(8,128)(2,1)}, f32[4,2,1024]{2,1,0:T(2,128)}) custom-call(bf16[1024,512]{1,0:T(8,128)(2,1)} %get-tuple-element.48.refs_0_, f32[4,2,1024]{2,1,0:T(2,128)} %get-tuple-element.49.refs_1_, bf16[1024,1536]{1,0:T(8,128)(2,1)} %add_convert_fusion.refs_0_.refs_1_.refs_2_.refs_3_.refs_4_, ...), custom_call_target="tpu_custom_call", output_to_operand_aliasing={{0}: (0, {}), {1}: (1, {})} | custom-call | flops 262144 | bytes 2048 | tf_op jit(solution)/shard_map/attend/pallas_call | solution.py:81
  118.5 4.1 %collective-permute-done.14.refs_1_ = bf16[2,640,256]{2,1,0:T(8,128)(2,1)S(1)} collective-permute-done((bf16[2,640,256]{2,1,0:T(8,128)(2,1)S(1)}, bf16[2,640,256]{2,1,0:T(8,128)(2,1)S(1)}, u32[]{:S(2)}, u32[]{:S(2)}) %collective-permute-start.14) | collective-permute-done | bytes 655392 | tf_op jit(solution)/shard_map/ppermute | solution.py:271
  124.3 5.4 %assemble.4 = (bf16[4,128,1024]{2,1,0:T(8,128)(2,1)}, bf16[4,512,1024]{2,1,0:T(8,128)(2,1)}) custom-call(s32[1]{0:T(128)} %bitcast.chip_ref, bf16[4,640,256]{2,1,0:T(8,128)(2,1)} %bitcast.165, bf16[4,640,256]{2,1,0:T(8,128)(2,1)} %copy-done.14, bf16[4,640,256]{2,1,0:T(8,128)(2,1)} %copy-done.13, bf16[2,640,256]{2,1,0:T(8,128)(2,1)} %copy-done.31, ...), custom_call_target="tpu_custom_call" | custom-call | bytes 2560 | tf_op jit(solution)/shard_map/assemble/pallas_call | solution.py:253
  141.0 10.3 %multiply_convert_fusion.1 = (bf16[1024,2048]{1,0:T(8,128)(2,1)}, f32[1024,2048]{1,0:T(8,128)}) fusion(f32[2048]{0:T(1024)S(1)} %bitcast.185, bf16[2048,1024]{1,0:T(8,128)(2,1)} %bitcast.189, bf16[512,1024]{1,0:T(8,128)(2,1)} %collective-permute-done.16, bf16[512,1024]{1,0:T(8,128)(2,1)S(1)} %fusion.22), kind=kOutput, calls=%fused_computation.7 | convolution fusion | flops 4311744512 | bytes 18882560 | tf_op jit(solution)/shard_map/dot_general | solution.py:25
  151.3 7.1 %all-gather.5.cloned.1.call-done = bf16[2048,1024]{1,0:T(8,128)(2,1)} async-done(((bf16[512,1024]{1,0:T(8,128)(2,1)}), bf16[2048,1024]{1,0:T(8,128)(2,1)}) %all-gather.5.cloned.1.call-update) | async-done | bytes 4194320 | tf_op jit(solution)/shard_map/all_gather | solution.py:420
  158.4 6.1 %fusion.35 = bf16[512,1024]{1,0:T(8,128)(2,1)} fusion(bf16[2048,1024]{1,0:T(8,128)(2,1)} %all-gather.5.cloned.1.call-done, bf16[1024,2048]{1,0:T(8,128)(2,1)} %get-tuple-element.138), kind=kOutput, calls=%fused_computation.74 | convolution fusion | flops 2148007936 | bytes 7340032 | tf_op jit(solution)/shard_map/dot_general | solution.py:29
  167.6 5.8 %fusion.104 = (f32[512]{0:T(512)S(1)}, f32[512,1024]{1,0:T(8,128)S(1)}) fusion(f32[1024]{0:T(1024)S(1)} %add.248, bf16[512,1024]{1,0:T(8,128)(2,1)} %collective-permute-done.17, bf16[2048,1024]{1,0:T(8,128)(2,1)} %all-gather.5.cloned.1.call-done, bf16[1024,2048]{1,0:T(8,128)(2,1)} %get-tuple-element.138, f32[1024]{0:T(1024)S(1)} %add.238, ...), kind=kOutput, calls=%fused_computation.229 | convolution fusion | flops 2152201728 | bytes 11552768 | tf_op jit(solution)/shard_map/dot_general | solution.py:29
  178.9 7.9 %collective-permute-start.19 = (bf16[512,1024]{1,0:T(8,128)(2,1)}, bf16[512,1024]{1,0:T(8,128)(2,1)}, u32[]{:S(2)}, u32[]{:S(2)}) collective-permute-start(bf16[512,1024]{1,0:T(8,128)(2,1)} %convert_element_type.234), channel_id=1, source_target_pairs={{0,4},{4,0},{1,5},{5,1},{2,6},{6,2},{3,7},{7,3},{8,12},{12,8},{9,1... | collective-permute-start | bytes 3145736 | tf_op jit(solution)/shard_map/ppermute | solution.py:209
  186.8 3.0 pad_maximum_fusion.2
  190.6 9.3 %convolution_convert_fusion = bf16[2048,1024]{1,0:T(8,128)(2,1)} fusion(bf16[1024,2048]{1,0:T(8,128)(2,1)} %get-tuple-element.138, bf16[512,1024]{1,0:T(8,128)(2,1)} %collective-permute-done.19, bf16[512,1024]{1,0:T(8,128)(2,1)} %convert_element_type.234), kind=kOutput, calls=%fused_computation.10 | convolution fusion | flops 4301258752 | bytes 10485760 | tf_op jit(solution)/shard_map/dot_general | solution.py:33
  200.0 11.3 %fusion.105 = (bf16[2048]{0:T(1024)(128)(2,1)S(1)}, bf16[1024,2048]{1,0:T(8,128)(2,1)S(1)}) fusion(f32[1024,2048]{1,0:T(8,128)} %get-tuple-element.139, f32[2048]{0:T(1024)S(1)} %bitcast.186, bf16[2048,1024]{1,0:T(8,128)(2,1)} %all-gather.5.cloned.1.call-done, bf16[512,1024]{1,0:T(8,128)(2,1)} %collective-permute-done.19, ...), kind=kOutput, calls=%fused_computation.230 | convolution fusion | flops 4328519680 | bytes 18886656 | tf_op jit(solution)/shard_map/dot_general | solution.py:25
  219.8 3.0 multiply_reduce_fusion
  225.3 4.4 %collective-permute-done.24 = bf16[1024,256]{1,0:T(8,128)(2,1)S(1)} collective-permute-done((bf16[1024,256]{1,0:T(8,128)(2,1)S(1)}, bf16[1024,256]{1,0:T(8,128)(2,1)S(1)}, u32[]{:S(2)}, u32[]{:S(2)}) %collective-permute-start.24) | collective-permute-done | bytes 524320 | tf_op jit(solution)/shard_map/ppermute | solution.py:271
  239.5 12.9 %attend_back.2 = (bf16[1024,1536]{1,0:T(8,128)(2,1)}, f32[4,2,128]{2,1,0:T(2,128)}) custom-call(bf16[1024,1536]{1,0:T(8,128)(2,1)} %add_convert_fusion.refs_0_.refs_1_.refs_2_.refs_3_.refs_4_, bf16[1024,1536]{1,0:T(8,128)(2,1)} %add_convert_fusion.refs_0_.refs_1_.refs_2_.refs_3_.refs_4_, ...), custom_call_target="tpu_custom_call" | custom-call | flops 262144 | bytes 2048 | tf_op jit(solution)/shard_map/attend_back/pallas_call | solution.py:151
  255.3 3.0 collective-permute-done.23
  259.5 2.9 add_convert_fusion.3
  262.4 13.0 %attend_back.3 = (bf16[1024,1536]{1,0:T(8,128)(2,1)}, f32[4,2,128]{2,1,0:T(2,128)}) custom-call(bf16[1024,1536]{1,0:T(8,128)(2,1)} %get-tuple-element.65.refs_0_, f32[4,2,128]{2,1,0:T(2,128)} %get-tuple-element.66.refs_1_, bf16[1024,1536]{1,0:T(8,128)(2,1)} %add_convert_fusion.refs_0_.refs_1_.refs_2_.refs_3_.refs_4_, ...), custom_call_target="tpu_custom_call", output_to_operand_aliasing={{0}: (0, {}), {1}: (1, {})} | custom-call | flops 262144 | bytes 2048 | tf_op jit(solution)/shard_map/attend_back/pallas_call | solution.py:151
  276.7 3.2 convolution_convert_fusion.2
  285.0 4.2 %convolution_convert_fusion.1 = bf16[1536,256]{1,0:T(8,128)(2,1)} fusion(bf16[1024,1536]{1,0:T(8,128)(2,1)} %get-tuple-element.67, bf16[1024,1024]{1,0:T(8,128)(2,1)} %constant_dynamic-update-slice_fusion, s32[]{:T(128)S(6)} %select_n.173), kind=kOutput, calls=%fused_computation.25 | convolution fusion | flops 805699584 | bytes 4456452 | tf_op jit(solution)/shard_map/dot_general | solution.py:33
  293.7 11.6 %reduce-scatter.4.cloned.1.call-done = bf16[1,512,256]{2,1,0:T(8,128)(2,1)} async-done(((bf16[4,512,256]{2,1,0:T(8,128)(2,1)}), bf16[1,512,256]{2,1,0:T(8,128)(2,1)}) %reduce-scatter.4.cloned.1.call-update) | async-done | bytes 262160 | tf_op jit(solution)/shard_map/reduce_scatter | solution.py:477
  313.3 3.1 add_convert_fusion.2
  321.5 14.4 %collective-permute-done.30 = bf16[2112,256]{1,0:T(8,128)(2,1)S(1)} collective-permute-done((bf16[2112,256]{1,0:T(8,128)(2,1)S(1)}, bf16[2112,256]{1,0:T(8,128)(2,1)S(1)}, u32[]{:S(2)}, u32[]{:S(2)}) %collective-permute-start.30) | collective-permute-done | bytes 1081376 | tf_op jit(solution)/shard_map/ppermute | solution.py:271
  342.8 4.2 %collective-permute-done.35 = bf16[512,256]{1,0:T(8,128)(2,1)S(1)} collective-permute-done((bf16[512,256]{1,0:T(8,128)(2,1)S(1)}, bf16[512,256]{1,0:T(8,128)(2,1)S(1)}, u32[]{:S(2)}, u32[]{:S(2)}) %collective-permute-start.35) | collective-permute-done | bytes 262176 | tf_op jit(solution)/shard_map/ppermute | solution.py:271
  347.0 6.7 %collective-permute-done.37 = bf16[512,256]{1,0:T(8,128)(2,1)S(1)} collective-permute-done((bf16[512,256]{1,0:T(8,128)(2,1)S(1)}, bf16[512,256]{1,0:T(8,128)(2,1)S(1)}, u32[]{:S(2)}, u32[]{:S(2)}) %collective-permute-start.37) | collective-permute-done | bytes 262176 | tf_op jit(solution)/shard_map/ppermute | solution.py:271
  359.4 8.1 %reduce-scatter.8.cloned.1.call-done = bf16[1,528,256]{2,1,0:T(8,128)(2,1)} async-done(((bf16[4,528,256]{2,1,0:T(8,128)(2,1)}), bf16[1,528,256]{2,1,0:T(8,128)(2,1)}) %reduce-scatter.8.cloned.1.call-update) | async-done | bytes 270352 | tf_op jit(solution)/shard_map/reduce_scatter | solution.py:477
  (352 shorter events, 121.6 us)
Async XLA Ops:
  7.3 69.2 %all-gather.7.cloned.1.call-start = ((), (), s32[]{:S(2)}) async-start(), calls=%async_computation.7 | async-start | bytes 1638400 | tf_op jit(solution)/shard_map/all_gather | solution.py:279
  11.5 33.0 %collective-permute-start = (bf16[512,1024]{1,0:T(8,128)(2,1)}, bf16[512,1024]{1,0:T(8,128)(2,1)S(1)}, u32[]{:S(2)}, u32[]{:S(2)}) collective-permute-start(bf16[512,1024]{1,0:T(8,128)(2,1)} %param.15), channel_id=1, source_target_pairs={{0,0},{4,1},{1,4},{5,5},{2,2},{6,3},{3,6},{7,7},{8,8},{12,9},{9,12... | collective-permute-start | bytes 3145736 | tf_op jit(solution)/shard_map/ppermute | solution.py:358
  13.5 30.8 %collective-permute-start.6 = (bf16[1,512,256]{2,1,0:T(8,128)(2,1)S(1)}, bf16[1,512,256]{2,1,0:T(8,128)(2,1)S(1)}, u32[]{:S(2)}, u32[]{:S(2)}) collective-permute-start(bf16[1,512,256]{2,1,0:T(8,128)(2,1)S(1)} %maximum_bitcast_fusion.own_ref), channel_id=1, source_target_pairs={{0,24},{8,16},{16,8},{24,0},{1,25},{9,17},{17,9},{25,1},{2,26},{10... | collective-permute-start | bytes 786440 | tf_op jit(solution)/shard_map/ppermute | solution.py:271
  17.5 26.9 %collective-permute-start.5 = (bf16[1,512,256]{2,1,0:T(8,128)(2,1)S(1)}, bf16[1,512,256]{2,1,0:T(8,128)(2,1)S(1)}, u32[]{:S(2)}, u32[]{:S(2)}) collective-permute-start(bf16[1,512,256]{2,1,0:T(8,128)(2,1)S(1)} %maximum_bitcast_fusion.own_ref), channel_id=1, source_target_pairs={{0,16},{8,24},{16,0},{24,8},{1,17},{9,25},{17,1},{25,9},{2,18},{10... | collective-permute-start | bytes 786440 | tf_op jit(solution)/shard_map/ppermute | solution.py:271
  18.0 26.4 %collective-permute-start.4 = (bf16[1,512,256]{2,1,0:T(8,128)(2,1)S(1)}, bf16[1,512,256]{2,1,0:T(8,128)(2,1)S(1)}, u32[]{:S(2)}, u32[]{:S(2)}) collective-permute-start(bf16[1,512,256]{2,1,0:T(8,128)(2,1)S(1)} %maximum_bitcast_fusion.own_ref), channel_id=1, source_target_pairs={{0,8},{8,0},{16,24},{24,16},{1,9},{9,1},{17,25},{25,17},{2,10},{10... | collective-permute-start | bytes 786440 | tf_op jit(solution)/shard_map/ppermute | solution.py:271
  45.2 113.2 %all-gather.5.cloned.1.call-start = ((), (), s32[]{:S(2)}) async-start(), calls=%async_computation.3 | async-start | bytes 5242880 | tf_op jit(solution)/shard_map/all_gather | solution.py:420
  45.6 18.3 %collective-permute-start.8 = (bf16[4,400,256]{2,1,0:T(8,128)(2,1)S(1)}, bf16[4,400,256]{2,1,0:T(8,128)(2,1)S(1)}, u32[]{:S(2)}, u32[]{:S(2)}) collective-permute-start(bf16[4,400,256]{2,1,0:T(8,128)(2,1)S(1)} %bitcast.152), channel_id=1, source_target_pairs={{0,16},{8,24},{16,0},{24,8},{1,17},{9,25},{17,1},{25,9},{2,18},{10... | collective-permute-start | bytes 2457608 | tf_op jit(solution)/shard_map/ppermute | solution.py:271
  47.2 19.1 %collective-permute-start.7 = (bf16[4,400,256]{2,1,0:T(8,128)(2,1)S(1)}, bf16[4,400,256]{2,1,0:T(8,128)(2,1)S(1)}, u32[]{:S(2)}, u32[]{:S(2)}) collective-permute-start(bf16[4,400,256]{2,1,0:T(8,128)(2,1)S(1)} %bitcast.153), channel_id=1, source_target_pairs={{0,8},{8,0},{16,24},{24,16},{1,9},{9,1},{17,25},{25,17},{2,10},{10... | collective-permute-start | bytes 2457608 | tf_op jit(solution)/shard_map/ppermute | solution.py:271
  48.6 23.7 %collective-permute-start.1 = (bf16[512,1024]{1,0:T(8,128)(2,1)}, bf16[512,1024]{1,0:T(8,128)(2,1)}, u32[]{:S(2)}, u32[]{:S(2)}) collective-permute-start(bf16[512,1024]{1,0:T(8,128)(2,1)} %copy-done.24), channel_id=1, source_target_pairs={{0,4},{4,0},{1,5},{5,1},{2,6},{6,2},{3,7},{7,3},{8,12},{12,8},{9,1... | collective-permute-start | bytes 3145736 | tf_op jit(solution)/shard_map/ppermute | solution.py:209
  64.8 9.9 %collective-permute-start.9 = (bf16[2,400,256]{2,1,0:T(8,128)(2,1)}, bf16[2,400,256]{2,1,0:T(8,128)(2,1)S(1)}, u32[]{:S(2)}, u32[]{:S(2)}) collective-permute-start(bf16[2,400,256]{2,1,0:T(8,128)(2,1)} %slice.269), channel_id=1, source_target_pairs={{0,8},{8,0},{16,24},{24,16},{1,9},{9,1},{17,25},{25,17},{2,10},{10... | collective-permute-start | bytes 1228808 | tf_op jit(solution)/shard_map/ppermute | solution.py:271
  72.1 212.3 %reduce-scatter.6.cloned.1.call-start = ((), (), s32[]{:S(2)}) async-start(), calls=%async_computation.5 | async-start | bytes 5242880 | tf_op jit(solution)/shard_map/reduce_scatter | solution.py:488
  76.5 31.3 %collective-permute-start.12 = (bf16[4,640,256]{2,1,0:T(8,128)(2,1)}, bf16[4,640,256]{2,1,0:T(8,128)(2,1)S(1)}, u32[]{:S(2)}, u32[]{:S(2)}) collective-permute-start(bf16[4,640,256]{2,1,0:T(8,128)(2,1)} %bitcast.163), channel_id=1, source_target_pairs={{0,16},{8,24},{16,0},{24,8},{1,17},{9,25},{17,1},{25,9},{2,18},{10... | collective-permute-start | bytes 3932168 | tf_op jit(solution)/shard_map/ppermute | solution.py:271
  78.0 29.8 %collective-permute-start.11 = (bf16[4,640,256]{2,1,0:T(8,128)(2,1)}, bf16[4,640,256]{2,1,0:T(8,128)(2,1)S(1)}, u32[]{:S(2)}, u32[]{:S(2)}) collective-permute-start(bf16[4,640,256]{2,1,0:T(8,128)(2,1)} %bitcast.164), channel_id=1, source_target_pairs={{0,8},{8,0},{16,24},{24,16},{1,9},{9,1},{17,25},{25,17},{2,10},{10... | collective-permute-start | bytes 3932168 | tf_op jit(solution)/shard_map/ppermute | solution.py:271
  107.9 14.8 %collective-permute-start.14 = (bf16[2,640,256]{2,1,0:T(8,128)(2,1)S(1)}, bf16[2,640,256]{2,1,0:T(8,128)(2,1)S(1)}, u32[]{:S(2)}, u32[]{:S(2)}) collective-permute-start(bf16[2,640,256]{2,1,0:T(8,128)(2,1)S(1)} %slice.222), channel_id=1, source_target_pairs={{0,16},{8,24},{16,0},{24,8},{1,17},{9,25},{17,1},{25,9},{2,18},{10... | collective-permute-start | bytes 1966088 | tf_op jit(solution)/shard_map/ppermute | solution.py:271
  108.5 14.4 %collective-permute-start.13 = (bf16[2,640,256]{2,1,0:T(8,128)(2,1)S(1)}, bf16[2,640,256]{2,1,0:T(8,128)(2,1)S(1)}, u32[]{:S(2)}, u32[]{:S(2)}) collective-permute-start(bf16[2,640,256]{2,1,0:T(8,128)(2,1)S(1)} %slice.221), channel_id=1, source_target_pairs={{0,8},{8,0},{16,24},{24,16},{1,9},{9,1},{17,25},{25,17},{2,10},{10... | collective-permute-start | bytes 1966088 | tf_op jit(solution)/shard_map/ppermute | solution.py:271
  164.8 8.9 %collective-permute-start.18 = (bf16[512,1024]{1,0:T(8,128)(2,1)}, bf16[512,1024]{1,0:T(8,128)(2,1)S(1)}, u32[]{:S(2)}, u32[]{:S(2)}) collective-permute-start(bf16[512,1024]{1,0:T(8,128)(2,1)} %param.29), channel_id=1, source_target_pairs={{0,0},{4,1},{1,4},{5,5},{2,2},{6,3},{3,6},{7,7},{8,8},{12,9},{9,12... | collective-permute-start | bytes 3145736 | tf_op jit(solution)/shard_map/ppermute | solution.py:358
  178.9 11.6 %collective-permute-start.19 = (bf16[512,1024]{1,0:T(8,128)(2,1)}, bf16[512,1024]{1,0:T(8,128)(2,1)}, u32[]{:S(2)}, u32[]{:S(2)}) collective-permute-start(bf16[512,1024]{1,0:T(8,128)(2,1)} %convert_element_type.234), channel_id=1, source_target_pairs={{0,4},{4,0},{1,5},{5,1},{2,6},{6,2},{3,7},{7,3},{8,12},{12,8},{9,1... | collective-permute-start | bytes 3145736 | tf_op jit(solution)/shard_map/ppermute | solution.py:209
  199.9 105.4 %reduce-scatter.4.cloned.1.call-start = ((), (), s32[]{:S(2)}) async-start(), calls=%async_computation.4 | async-start | bytes 1310720 | tf_op jit(solution)/shard_map/reduce_scatter | solution.py:477
  215.3 14.4 %collective-permute-start.24 = (bf16[1024,256]{1,0:T(8,128)(2,1)S(1)}, bf16[1024,256]{1,0:T(8,128)(2,1)S(1)}, u32[]{:S(2)}, u32[]{:S(2)}) collective-permute-start(bf16[1024,256]{1,0:T(8,128)(2,1)S(1)} %get-tuple-element.98), channel_id=1, source_target_pairs={{0,8},{8,0},{16,24},{24,16},{1,9},{9,1},{17,25},{25,17},{2,10},{10... | collective-permute-start | bytes 1572872 | tf_op jit(solution)/shard_map/ppermute | solution.py:271
  216.8 14.0 %collective-permute-start.22 = (bf16[1024,256]{1,0:T(8,128)(2,1)S(1)}, bf16[1024,256]{1,0:T(8,128)(2,1)S(1)}, u32[]{:S(2)}, u32[]{:S(2)}) collective-permute-start(bf16[1024,256]{1,0:T(8,128)(2,1)S(1)} %get-tuple-element.97), channel_id=1, source_target_pairs={{0,16},{8,24},{16,0},{24,8},{1,17},{9,25},{17,1},{25,9},{2,18},{10... | collective-permute-start | bytes 1572872 | tf_op jit(solution)/shard_map/ppermute | solution.py:271
  233.4 24.9 %collective-permute-start.23 = (bf16[2048,256]{1,0:T(8,128)(2,1)S(1)}, bf16[2048,256]{1,0:T(8,128)(2,1)}, u32[]{:S(2)}, u32[]{:S(2)}) collective-permute-start(bf16[2048,256]{1,0:T(8,128)(2,1)S(1)} %pad_maximum_fusion.11), channel_id=1, source_target_pairs={{0,8},{8,0},{16,24},{24,16},{1,9},{9,1},{17,25},{25,17},{2,10},{10... | collective-permute-start | bytes 3145736 | tf_op jit(solution)/shard_map/ppermute | solution.py:271
  234.8 24.7 %collective-permute-start.25 = (bf16[2048,256]{1,0:T(8,128)(2,1)S(1)}, bf16[2048,256]{1,0:T(8,128)(2,1)}, u32[]{:S(2)}, u32[]{:S(2)}) collective-permute-start(bf16[2048,256]{1,0:T(8,128)(2,1)S(1)} %pad_maximum_fusion.12), channel_id=1, source_target_pairs={{0,16},{8,24},{16,0},{24,8},{1,17},{9,25},{17,1},{25,9},{2,18},{10... | collective-permute-start | bytes 3145736 | tf_op jit(solution)/shard_map/ppermute | solution.py:271
  276.6 91.0 %reduce-scatter.8.cloned.1.call-start = ((), (), s32[]{:S(2)}) async-start(), calls=%async_computation.6 | async-start | bytes 1351680 | tf_op jit(solution)/shard_map/reduce_scatter | solution.py:477
  284.5 22.9 %collective-permute-start.31 = (bf16[1056,256]{1,0:T(8,128)(2,1)}, bf16[1056,256]{1,0:T(8,128)(2,1)}, u32[]{:S(2)}, u32[]{:S(2)}) collective-permute-start(bf16[1056,256]{1,0:T(8,128)(2,1)} %get-tuple-element.73), channel_id=1, source_target_pairs={{0,8},{8,0},{16,24},{24,16},{1,9},{9,1},{17,25},{25,17},{2,10},{10... | collective-permute-start | bytes 1622024 | tf_op jit(solution)/shard_map/ppermute | solution.py:271
  289.2 19.5 %collective-permute-start.29 = (bf16[1056,256]{1,0:T(8,128)(2,1)}, bf16[1056,256]{1,0:T(8,128)(2,1)}, u32[]{:S(2)}, u32[]{:S(2)}) collective-permute-start(bf16[1056,256]{1,0:T(8,128)(2,1)} %get-tuple-element.71), channel_id=1, source_target_pairs={{0,16},{8,24},{16,0},{24,8},{1,17},{9,25},{17,1},{25,9},{2,18},{10... | collective-permute-start | bytes 1622024 | tf_op jit(solution)/shard_map/ppermute | solution.py:271
  293.7 19.6 %collective-permute-start.27 = (bf16[512,1024]{1,0:T(8,128)(2,1)}, bf16[512,1024]{1,0:T(8,128)(2,1)}, u32[]{:S(2)}, u32[]{:S(2)}) collective-permute-start(bf16[512,1024]{1,0:T(8,128)(2,1)} %fusion.31), channel_id=1, source_target_pairs={{0,4},{4,0},{1,5},{5,1},{2,6},{6,2},{3,7},{7,3},{8,12},{12,8},{9,1... | collective-permute-start | bytes 3145736 | tf_op jit(solution)/shard_map/ppermute | solution.py:209
  305.3 11.1 %collective-permute-start.26 = (bf16[512,1024]{1,0:T(8,128)(2,1)}, bf16[512,1024]{1,0:T(8,128)(2,1)S(1)}, u32[]{:S(2)}, u32[]{:S(2)}) collective-permute-start(bf16[512,1024]{1,0:T(8,128)(2,1)} %get-tuple-element.64), channel_id=1, source_target_pairs={{0,0},{4,1},{1,4},{5,5},{2,2},{6,3},{3,6},{7,7},{8,8},{12,9},{9,12... | collective-permute-start | bytes 3145736 | tf_op jit(solution)/shard_map/ppermute | solution.py:358
  310.3 25.5 %collective-permute-start.30 = (bf16[2112,256]{1,0:T(8,128)(2,1)S(1)}, bf16[2112,256]{1,0:T(8,128)(2,1)S(1)}, u32[]{:S(2)}, u32[]{:S(2)}) collective-permute-start(bf16[2112,256]{1,0:T(8,128)(2,1)S(1)} %pad_maximum_fusion.9), channel_id=1, source_target_pairs={{0,8},{8,0},{16,24},{24,16},{1,9},{9,1},{17,25},{25,17},{2,10},{10... | collective-permute-start | bytes 3244040 | tf_op jit(solution)/shard_map/ppermute | solution.py:271
  311.8 25.2 %collective-permute-start.32 = (bf16[2112,256]{1,0:T(8,128)(2,1)S(1)}, bf16[2112,256]{1,0:T(8,128)(2,1)S(1)}, u32[]{:S(2)}, u32[]{:S(2)}) collective-permute-start(bf16[2112,256]{1,0:T(8,128)(2,1)S(1)} %fusion.45), channel_id=1, source_target_pairs={{0,16},{8,24},{16,0},{24,8},{1,17},{9,25},{17,1},{25,9},{2,18},{10... | collective-permute-start | bytes 3244040 | tf_op jit(solution)/shard_map/ppermute | solution.py:271
  339.9 13.8 %collective-permute-start.37 = (bf16[512,256]{1,0:T(8,128)(2,1)S(1)}, bf16[512,256]{1,0:T(8,128)(2,1)S(1)}, u32[]{:S(2)}, u32[]{:S(2)}) collective-permute-start(bf16[512,256]{1,0:T(8,128)(2,1)S(1)} %get-tuple-element.95), channel_id=1, source_target_pairs={{0,24},{8,16},{16,8},{24,0},{1,25},{9,17},{17,9},{25,1},{2,26},{10... | collective-permute-start | bytes 786440 | tf_op jit(solution)/shard_map/ppermute | solution.py:271
  342.2 14.0 %collective-permute-start.36 = (bf16[512,256]{1,0:T(8,128)(2,1)S(1)}, bf16[512,256]{1,0:T(8,128)(2,1)S(1)}, u32[]{:S(2)}, u32[]{:S(2)}) collective-permute-start(bf16[512,256]{1,0:T(8,128)(2,1)S(1)} %get-tuple-element.96), channel_id=1, source_target_pairs={{0,16},{8,24},{16,0},{24,8},{1,17},{9,25},{17,1},{25,9},{2,18},{10... | collective-permute-start | bytes 786440 | tf_op jit(solution)/shard_map/ppermute | solution.py:271
  357.5 14.2 %collective-permute-start.34 = (bf16[512,128]{1,0:T(8,128)(2,1)S(1)}, bf16[512,128]{1,0:T(8,128)(2,1)S(1)}, u32[]{:S(2)}, u32[]{:S(2)}) collective-permute-start(bf16[512,128]{1,0:T(8,128)(2,1)S(1)} %dynamic-slice_bitcast_fusion.4), channel_id=1, source_target_pairs={{0,4},{4,0},{1,5},{5,1},{2,6},{6,2},{3,7},{7,3},{8,12},{12,8},{9,1... | collective-permute-start | bytes 393224 | tf_op jit(solution)/shard_map/ppermute | solution.py:209
  (69 other events, 442.3 us)
Sparse Core Ops, SparseCore 0:
  44.6 31.8 all-gather.6
  78.6 79.7 all-gather.4
  200.0 75.2 reduce-scatter.5
  277.6 27.6 reduce-scatter.3
  338.8 28.7 reduce-scatter.7
